TPU v7x, 768 devices: a whole 4x8x12 slice. The times are simulated.
768 devices in a mesh: grp: 16 (over y, core), shard: 48 (over z, x).
Axes of the slice: x: 4, y: 8, z: 12, core: 2. Of those that a mesh axis runs over, the one named last changes fastest.
Arguments:
- target: bfloat16 [6144, 128], P(('grp', 'shard')), may hold values from -6 to 6
- history: bfloat16 [6144, 128, 128], P(('grp', 'shard')), may hold values from -6 to 6
- lengths: int32 [6144], P(('grp', 'shard')), may hold values from 1 to 128, as said below
- hist_ids: int32 [6144, 128], P(('grp', 'shard')), may hold values from 0 to 98303, as said below
- block_rows: int32 [768, 48, 48], P(('grp', 'shard')), may hold values from 0 to 1023, as said below
- block_counts: int32 [768, 48], P(('grp', 'shard')), may hold values from 0 to 48, as said below
- attn_w1: bfloat16 [512, 256], replicated, may hold values from -0.25 to 0.25
- attn_b1: float32 [256], replicated, may hold values from -4 to 4
- attn_w2: bfloat16 [256, 128], replicated, may hold values from -0.375 to 0.375
- attn_b2: float32 [128], replicated, may hold values from -4 to 4
- attn_w3: float32 [128], replicated, may hold values from -3 to 3
- pooled_gradient: float32 [6144, 128], P(('grp', 'shard')), may hold values from -6 to 6
Outputs:
- table_grad: float32 [16, 98304, 128], P('grp', 'shard')
- grad_w1: float32 [512, 256], P('grp')
- grad_b1: float32 [256], P('grp')
- grad_w2: float32 [256, 128], P('grp')
- grad_b2: float32 [128], P('grp')
- grad_w3: float32 [128], P('grp')
Inputs may be any that keep to these rules, and one draw needn't show every extreme that they name: Each device's 8 lengths sum to 768; one of them is 128. `hist_ids`: A history slot listed in owner o's block holds an id in o * 2048 to (o + 1) * 2048 - 1. `block_rows`: for each device and owner o, entries c < block_counts[o] are distinct live slots b * 128 + j (j < lengths[b]) of that device's own samples; every live slot stands in exactly one owner's block; other entries are 0. `block_counts`: A device's counts sum to 768; in each grp index one owner receives 48 slots from every device; every other count of a device is at most 24, and each device has one count of exactly 24.
All inputs are finite; a program needn't handle non-finite values.
Results may differ from a plain program's by a relative error of at most 0.0067.
Values sent between devices are 32-bit elements; how exact they have to be, the bound alone decides.
No kernel may reach another device: no remote copies, remote signals or barrier semaphores. Data moves between devices by JAX's collectives and lax.ppermute only.
A program may use at most 32 MiB of HBM per device.

v0:
```python
import jax
import jax.numpy as jnp
from jax import lax
from jax.sharding import PartitionSpec as P

ROWS_DEV = 2048


def local_terms(
    target, history, lengths, pooled_gradient, attn_w1, attn_b1, attn_w2, attn_b2, attn_w3
):
    sample_count, slot_count, feature_width = history.shape
    query = target.astype(jnp.float32)[:, None, :]
    hist = history.astype(jnp.float32)
    item_minus_target = (query - hist).astype(jnp.bfloat16)
    item_times_target = (query * hist).astype(jnp.bfloat16)
    query_tile = jnp.broadcast_to(target[:, None, :], history.shape)
    feature_rows = jnp.concatenate(
        [query_tile, history, item_minus_target, item_times_target], axis=-1
    ).reshape(sample_count * slot_count, 4 * feature_width)
    act1 = jax.nn.sigmoid(
        jnp.dot(feature_rows, attn_w1, preferred_element_type=jnp.float32) + attn_b1
    )
    act1_low = act1.astype(jnp.bfloat16)
    act2 = jax.nn.sigmoid(jnp.dot(act1_low, attn_w2, preferred_element_type=jnp.float32) + attn_b2)
    live_mask = (jnp.arange(slot_count, dtype=jnp.int32)[None, :] < lengths[:, None]).reshape(-1)
    attention_score = jnp.where(live_mask, jnp.sum(act2 * attn_w3, axis=-1), 0.0)
    dscore = jnp.sum(pooled_gradient[:, None, :] * hist, axis=-1).reshape(-1)
    dscore = jnp.where(live_mask, dscore, 0.0)
    dz2_full = dscore[:, None] * attn_w3[None, :] * act2 * (1.0 - act2)
    dz2 = dz2_full.astype(jnp.bfloat16)
    grad_w3 = jnp.sum(dscore[:, None] * act2, axis=0)
    grad_b2 = jnp.sum(dz2_full, axis=0)
    grad_w2 = jnp.dot(act1_low.T, dz2, preferred_element_type=jnp.float32)
    dz1_full = jnp.dot(dz2, attn_w2.T, preferred_element_type=jnp.float32) * act1 * (1.0 - act1)
    dz1 = dz1_full.astype(jnp.bfloat16)
    grad_b1 = jnp.sum(dz1_full, axis=0)
    grad_w1 = jnp.dot(feature_rows.T, dz1, preferred_element_type=jnp.float32)
    dfeat = jnp.dot(dz1, attn_w1.T, preferred_element_type=jnp.float32)
    part_h = dfeat[:, feature_width : 2 * feature_width]
    part_d = dfeat[:, 2 * feature_width : 3 * feature_width]
    part_p = dfeat[:, 3 * feature_width :]
    qflat = jnp.broadcast_to(query, hist.shape).reshape(-1, feature_width)
    pooled_contribution = (
        attention_score.reshape(sample_count, slot_count)[:, :, None] * pooled_gradient[:, None, :]
    ).reshape(-1, feature_width)
    drow = part_h - part_d + part_p * qflat + pooled_contribution
    return (drow, (grad_w1, grad_b1, grad_w2, grad_b2, grad_w3))


def shards(
    target,
    history,
    lengths,
    hist_ids,
    block_rows,
    block_counts,
    attn_w1,
    attn_b1,
    attn_w2,
    attn_b2,
    attn_w3,
    pooled_gradient,
):
    feature_width = history.shape[2]
    drow, grads = local_terms(
        target, history, lengths, pooled_gradient, attn_w1, attn_b1, attn_w2, attn_b2, attn_w3
    )
    blocks = block_rows[0]
    counts = block_counts[0]
    capacity = blocks.shape[1]
    used = jnp.arange(capacity, dtype=jnp.int32)[None, :] < counts[:, None]
    rows = jnp.where(used[:, :, None], drow[blocks], 0.0)
    dest = jnp.where(used, hist_ids.reshape(-1)[blocks] % ROWS_DEV, 0)
    table = jnp.zeros((ROWS_DEV, feature_width), jnp.float32)
    got_rows, got_dest = (
        lax.all_to_all(rows, "shard", split_axis=0, concat_axis=0, tiled=True),
        lax.all_to_all(dest, "shard", split_axis=0, concat_axis=0, tiled=True),
    )
    table = table.at[got_dest.reshape(-1)].add(got_rows.reshape(-1, feature_width))
    totals = lax.psum((grads[0], grads[1], grads[2], grads[3], grads[4]), ("grp", "shard"))
    groups = lax.axis_size("grp")
    gindex = lax.axis_index("grp")
    shares = tuple(
        (
            lax.dynamic_slice_in_dim(
                arr, gindex * (arr.shape[0] // groups), arr.shape[0] // groups, 0
            )
            for arr in totals
        )
    )
    return (table[None], shares[0], shares[1], shares[2], shares[3], shares[4])


def solution(mesh):
    placed = (
        P(("grp", "shard"), None),
        P(("grp", "shard"), None, None),
        P(("grp", "shard")),
        P(("grp", "shard"), None),
        P(("grp", "shard"), None, None),
        P(("grp", "shard"), None),
        P(),
        P(),
        P(),
        P(),
        P(),
        P(("grp", "shard"), None),
    )
    return jax.shard_map(
        shards,
        mesh=mesh,
        in_specs=placed,
        out_specs=(
            P("grp", "shard", None),
            P("grp", None),
            P("grp"),
            P("grp", None),
            P("grp"),
            P("grp"),
        ),
        check_vma=False,
    )
```

profile of v0, /device:TPU:6, one launch (start us, length us, event | category | flops | bytes accessed | tf_op | source)
XLA Modules:
  0.0 570.9 jit_solution(7439168284579336668)
XLA Ops:
  7.2 0.8 compare_select_fusion.3
  8.1 8.5 %gather_fusion = s32[2304]{0:T(1024)S(1)} fusion(s32[1024]{0:T(1024)S(1)} %bitcast.32, s32[3072]{0:T(1024)S(1)} %pad_clamp_fusion), kind=kCustom, calls=%fused_computation | custom fusion | bytes 27648 | tf_op jit(solution)/shard_map/gather | solution.py:74
  16.7 0.1 gather.9
  16.8 0.7 compare_select_fusion.2
  17.5 18.5 %all-to-all-start = ((s32[48,1,48]{2,1,0:T(1,128)}), s32[48,1,48]{2,1,0:T(1,128)}, u32[]{:S(2)}, u32[]{:S(2)}) async-start(s32[48,1,48]{2,1,0:T(1,128)} %compare_select_fusion.2), calls=%async_computation | async-start | bytes 49152 | tf_op jit(solution)/shard_map/all_to_all | solution.py:78
  36.0 0.7 iota_compare_fusion
  36.7 0.2 fusion.10
  37.1 0.1 pad_maximum_fusion
  37.2 0.5 copy-done.17
  37.7 0.4 fusion.4
  38.2 0.4 copy-done.7
  38.6 1.0 multiply_reduce_fusion
  39.6 1.0 fusion.31
  40.6 0.8 copy-done.2
  41.4 0.5 fusion.20
  41.9 0.2 fusion.13
  42.1 3.9 gather_fusion.1
  46.0 2.0 broadcast_select_fusion
  48.0 12.6 %all-to-all-start.1 = ((f32[48,48,128]{2,1,0:T(8,128)}), f32[48,48,128]{2,1,0:T(8,128)S(1)}, u32[]{:S(2)}, u32[]{:S(2)}) async-start(f32[48,48,128]{2,1,0:T(8,128)} %broadcast_select_fusion), calls=%async_computation.1 | async-start | bytes 2359296 | tf_op jit(solution)/shard_map/all_to_all | solution.py:77
  60.7 1.2 fusion.22
  61.8 0.2 copy-done.5
  62.0 1.3 fusion.18
  63.3 110.0 %all-reduce = (f32[256]{0:T(256)S(1)}, f32[128]{0:T(128)S(1)}, f32[128]{0:T(128)S(1)}) all-reduce(f32[256]{0:T(256)S(1)} %copy-done.10, f32[128]{0:T(128)S(1)} %copy-done.16, f32[128]{0:T(128)S(1)} %copy-done.15), channel_id=1, replica_groups=mesh['grp'=16,'shard'=48] {'grp','shard'}, use_global_device_ids=true, to_apply=%region_5.6 | all-reduce | flops 512 | bytes 4096 | tf_op jit(solution)/shard_map/psum | solution.py:81
  173.3 0.6 dynamic_slice.18
  173.9 0.6 dynamic_slice.19
  174.4 0.6 dynamic_slice.16
  175.0 0.5 broadcast.174
  175.5 1.4 reduce.5
  177.1 367.6 %all-reduce.4.cloned.1.call-done = (f32[512,256]{1,0:T(8,128)}, f32[256,128]{1,0:T(8,128)}) async-done(((f32[512,256]{1,0:T(8,128)}, f32[256,128]{1,0:T(8,128)}), (f32[512,256]{1,0:T(8,128)}, f32[256,128]{1,0:T(8,128)})) %all-reduce.4.cloned.1.call-update) | async-done | bytes 655376 | tf_op jit(solution)/shard_map/psum | solution.py:81
  544.7 1.3 constant_dynamic-slice_fusion
  546.0 1.4 constant_dynamic-slice_fusion.1
  547.4 16.7 %scatter_custom_fusion = f32[2048,128]{1,0:T(8,128)} fusion(s32[2304]{0:T(1024)S(1)} %fusion.26, f32[2304,128]{1,0:T(8,128)S(1)} %bitcast.34, f32[]{:T(128)} %constant.14.clone.1), kind=kCustom, calls=%fused_computation.31 | custom fusion | flops 294912 | bytes 1048580 | tf_op jit(solution)/shard_map/scatter-add | solution.py:80
  (46 shorter events, 0.6 us)
Async XLA Ops:
  7.2 30.1 %copy-start = (bf16[512,256]{1,0:T(8,128)(2,1)S(1)}, bf16[512,256]{1,0:T(8,128)(2,1)}, u32[]{:S(2)}) copy-start(bf16[512,256]{1,0:T(8,128)(2,1)} %param.18) | copy-start | bytes 786436
  7.2 0.9 copy-start.1
  8.1 8.7 %copy-start.13 = (s32[1,48]{1,0:T(1,128)S(1)}, s32[1,48]{1,0:T(1,128)}, u32[]{:S(2)}) copy-start(s32[1,48]{1,0:T(1,128)} %param.17) | copy-start | bytes 580
  8.1 28.6 %copy-start.9 = (bf16[8,128]{1,0:T(8,128)(2,1)S(1)}, bf16[8,128]{1,0:T(8,128)(2,1)}, u32[]{:S(2)}) copy-start(bf16[8,128]{1,0:T(8,128)(2,1)} %param.12) | copy-start | bytes 6148
  8.1 28.6 %copy-start.6 = (bf16[8,128,128]{2,1,0:T(8,128)(2,1)S(1)}, bf16[8,128,128]{2,1,0:T(8,128)(2,1)}, u32[]{:S(2)}) copy-start(bf16[8,128,128]{2,1,0:T(8,128)(2,1)} %param.13) | copy-start | bytes 786436
  8.1 28.6 %copy-start.8 = (f32[8,128]{1,0:T(8,128)S(1)}, f32[8,128]{1,0:T(8,128)}, u32[]{:S(2)}) copy-start(f32[8,128]{1,0:T(8,128)} %param.23) | copy-start | bytes 12292
  8.1 28.8 %copy-start.14 = (s32[8]{0:T(128)S(1)}, s32[8]{0:T(128)}, u32[]{:S(2)}) copy-start(s32[8]{0:T(128)} %param.14) | copy-start | bytes 100
  17.5 30.5 %all-to-all-start = ((s32[48,1,48]{2,1,0:T(1,128)}), s32[48,1,48]{2,1,0:T(1,128)}, u32[]{:S(2)}, u32[]{:S(2)}) async-start(s32[48,1,48]{2,1,0:T(1,128)} %compare_select_fusion.2), calls=%async_computation | async-start | bytes 49152 | tf_op jit(solution)/shard_map/all_to_all | solution.py:78
  37.0 0.7 copy-start.17
  37.2 1.0 copy-start.4
  37.7 0.8 copy-start.7
  37.7 0.8 copy-start.11
  37.7 0.8 copy-start.18
  40.6 0.8 copy-start.2
  48.0 12.6 %copy-start.12 = (f32[128]{0:T(128)S(1)}, f32[128]{0:T(128)}, u32[]{:S(2)}) copy-start(f32[128]{0:T(128)} %param.22) | copy-start | bytes 1540
  48.0 499.4 %all-to-all-start.1 = ((f32[48,48,128]{2,1,0:T(8,128)}), f32[48,48,128]{2,1,0:T(8,128)S(1)}, u32[]{:S(2)}, u32[]{:S(2)}) async-start(f32[48,48,128]{2,1,0:T(8,128)} %broadcast_select_fusion), calls=%async_computation.1 | async-start | bytes 2359296 | tf_op jit(solution)/shard_map/all_to_all | solution.py:77
  60.6 1.2 copy-start.3
  60.6 484.1 %all-reduce.4.cloned.1.call-start = ((), (), s32[]{:S(2)}) async-start(), calls=%async_computation.2 | async-start | bytes 1310720 | tf_op jit(solution)/shard_map/psum | solution.py:81
  60.6 1.3 copy-start.5
  62.0 1.3 copy-start.10
  62.0 1.3 copy-start.15
  62.0 1.3 copy-start.16
Sparse Core Ops, SparseCore 0:
  67.7 476.9 all-reduce.3
where the time goes:
time: 572 us; the launch traced here: 571 us
  waiting for transfers between devices  368 us (64%)
  blocking collectives  110 us (19%)
  starting transfers between devices  31.2 us (5%)
  other arithmetic  23 us (4%)
  local copies, waits for them, and re-layouts  19.6 us (3%)
  between operations  14.3 us (2%)
    psum x1, waiting for transfers between devices, shards(): lax.psum((grads[0], grads[1], grads[2], grads[3], grads[4]), ('grp', 'sha...  368 us
    psum x1, blocking collectives, shards(): lax.psum((grads[0], grads[1], grads[2], grads[3], grads[4]), ('grp', 'sha...  110 us
    all_to_all x1, starting transfers between devices, shards(): lax.all_to_all(dest, 'shard', split_axis=0, concat_axis=0, tiled=True)  18.5 us
    scatter-add x1, other arithmetic, shards(): table.at[got_dest.reshape(-1)].add(got_rows.reshape(-1, feature_width))  16.7 us
    all_to_all x1, starting transfers between devices, shards(): lax.all_to_all(rows, 'shard', split_axis=0, concat_axis=0, tiled=True)  12.6 us
  transfers between devices with their start and end apart: 3, of which 1 were waited for; matrix products, arithmetic and copies ran while one was open for 3% of the time, Pallas kernels for 0%

commit v1 on v0

--- a/solution.py
+++ b/solution.py
@@ -1,9 +1,19 @@
 import jax
 import jax.numpy as jnp
 from jax import lax
+from jax.experimental import pallas as pl
+from jax.experimental.pallas import tpu as pltpu
 from jax.sharding import PartitionSpec as P
 
 ROWS_DEV = 2048
+E = 128
+OWNERS = 48
+HALF = 24
+BLOCK = 32
+NX = 4
+PIECE = 6
+SLOTS = 1024
+VMEM_LIMIT = 48 * 1024 * 1024
 
 
 def local_terms(
@@ -48,6 +58,186 @@
     return (drow, (grad_w1, grad_b1, grad_w2, grad_b2, grad_w3))
 
 
+def iota(shape, dim):
+    return lax.broadcasted_iota(jnp.int32, shape, dim)
+
+
+def split(rows):
+    high = rows.astype(jnp.bfloat16)
+    low = (rows - high.astype(jnp.float32)).astype(jnp.bfloat16)
+    return jnp.concatenate([high, low], axis=1)
+
+
+def pack_kernel(me_ref, counts_ref, drow_ref, ids_ref, blocks_ref, send_ref, pick, source):
+    me = me_ref[0]
+    hot = jnp.int32(0)
+    for o in range(OWNERS):
+        hot = jnp.where(counts_ref[0, o] > HALF, jnp.int32(o), hot)
+
+    source[:, : 2 * E] = split(drow_ref[...])
+    ids = ids_ref[...] & (ROWS_DEV - 1)
+    id_columns = jnp.transpose(ids.astype(jnp.float32))
+    for b in range(8):
+        column = jnp.broadcast_to(id_columns[:, b : b + 1], (128, 128)).astype(jnp.int32)
+        source[b * 128 : (b + 1) * 128, 2 * E : 3 * E] = (column >> 8).astype(jnp.float32).astype(jnp.bfloat16)
+        source[b * 128 : (b + 1) * 128, 3 * E :] = (column & 255).astype(jnp.float32).astype(jnp.bfloat16)
+
+    slot = iota((8, SLOTS), 1).astype(jnp.float32)[:1]
+    eye = iota((HALF, OWNERS), 0) == iota((HALF, OWNERS), 1)
+    def one_hot(mask, row):
+        chosen = jnp.where(mask, row.astype(jnp.float32), 0.0)
+        column = jnp.sum(chosen, axis=1, keepdims=True)
+        return jnp.where(column == slot, 1.0, 0.0)
+    for o in range(0, OWNERS, 2):
+        pair = [one_hot(eye, blocks_ref[k : k + 1, :]) for k in (o, o + 1)]
+        pick[o * HALF : (o + 2) * HALF, :] = jnp.concatenate(pair, axis=0).astype(jnp.bfloat16)
+    r, lane = iota((32, OWNERS), 0), iota((32, OWNERS), 1)
+    late = (lane == HALF + PIECE * (r // 8) + r % 8) & (r % 8 < PIECE)
+    last = one_hot(late, blocks_ref[pl.ds(hot, 1), :])
+    pick[OWNERS * HALF :, :] = last.astype(jnp.bfloat16)
+
+    got = jnp.dot(pick[...], source[...], preferred_element_type=jnp.float32)
+
+    sub, lane = iota((HALF, E), 0), iota((HALF, E), 1)
+    place = lane - sub == (me % NX) * BLOCK
+    sub8, lane8 = iota((8, E), 0), iota((8, E), 1)
+    place8 = (lane8 - sub8 == (me % 16) * 8) & (sub8 < PIECE)
+    tails = []
+    for x in range(NX):
+        part = got[OWNERS * HALF + 8 * x : OWNERS * HALF + 8 * x + 8]
+        where_to = part[:, 2 * E : 3 * E] * 256.0 + part[:, 3 * E :] + 1.0
+        row = jnp.sum(jnp.where(place8, where_to, 0.0), axis=0, keepdims=True)
+        tails.append(jnp.where(sub8 < PIECE, part[:, :E] + part[:, E : 2 * E], row))
+    for o in range(OWNERS):
+        part = got[o * HALF : (o + 1) * HALF]
+        send_ref[o, :HALF, :] = part[:, :E] + part[:, E : 2 * E]
+        where_to = part[:, 2 * E : 3 * E] * 256.0 + part[:, 3 * E :] + 1.0
+        used = place & (sub < counts_ref[0, o])
+        row = jnp.sum(jnp.where(used, where_to, 0.0), axis=0, keepdims=True)
+        send_ref[o, HALF:, :] = jnp.where(sub8 == PIECE, row, tails[o % NX])
+
+
+def pack(me, counts, drow, ids, blocks):
+    whole = pl.BlockSpec(memory_space=pltpu.VMEM)
+    scalar = pl.BlockSpec(memory_space=pltpu.SMEM)
+    return pl.pallas_call(
+        pack_kernel,
+        out_shape=jax.ShapeDtypeStruct((OWNERS, BLOCK, E), jnp.float32),
+        in_specs=[scalar, scalar, whole, whole, whole],
+        out_specs=whole,
+        scratch_shapes=[
+            pltpu.VMEM((OWNERS * HALF + 32, SLOTS), jnp.bfloat16),
+            pltpu.VMEM((SLOTS, 4 * E), jnp.bfloat16),
+        ],
+        compiler_params=pltpu.CompilerParams(vmem_limit_bytes=VMEM_LIMIT),
+        cost_estimate=pl.CostEstimate(
+            flops=2 * 1184 * 1024 * 512, bytes_accessed=2_000_000, transcendentals=0
+        ),
+        name="pack",
+    )(me, counts, drow, ids, blocks)
+
+
+STEP = 512
+
+
+def add_kernel(me_ref, counts_ref, got_ref, late0_ref, late1_ref, late2_ref, table_ref, rows, dest):
+    groups = OWNERS // NX
+    for g in range(groups):
+        rows[g * 128 : (g + 1) * 128, :] = split(got_ref[g * 128 : (g + 1) * 128, :])
+        total = sum(got_ref[(NX * g + j) * BLOCK + HALF : (NX * g + j + 1) * BLOCK, :] for j in range(NX))
+        dest[:, g * 128 : (g + 1) * 128] = jnp.broadcast_to(total[PIECE : PIECE + 1, :], (8, E))
+
+    def product(t):
+        table_row = (iota((STEP, E), 0) + (t * STEP + 1)).astype(jnp.float32)
+        hits = [
+            jnp.where(table_row == dest[0:1, g * 128 : (g + 1) * 128], 1.0, 0.0).astype(jnp.bfloat16)
+            for g in range(groups)
+        ]
+        both = jnp.dot(jnp.concatenate(hits, axis=1), rows[...], preferred_element_type=jnp.float32)
+        return both[:, :E] + both[:, E:]
+
+    for t in range(ROWS_DEV // STEP):
+        table_ref[t * STEP : (t + 1) * STEP, :] = product(t)
+
+    @pl.when(counts_ref[0, me_ref[0]] > HALF)
+    def _():
+        for k in range(NX):
+            for g in range(3):
+                if k == 0:
+                    tiles = [
+                        got_ref[s * BLOCK + HALF : (s + 1) * BLOCK, :]
+                        for s in range(16 * g, 16 * g + 16)
+                    ]
+                else:
+                    late = (late0_ref, late1_ref, late2_ref)[k - 1]
+                    tiles = [late[s * 8 : s * 8 + 8, :] for s in range(16 * g, 16 * g + 16)]
+                at = (k * 3 + g) * 128
+                rows[at : at + 128, :] = split(jnp.concatenate(tiles, axis=0))
+                dest[:, at : at + 128] = jnp.broadcast_to(sum(tiles)[7:8, :], (8, E))
+        for t in range(ROWS_DEV // STEP):
+            table_ref[t * STEP : (t + 1) * STEP, :] += product(t)
+
+
+def add_rows(me, counts, got, late):
+    whole = pl.BlockSpec(memory_space=pltpu.VMEM)
+    scalar = pl.BlockSpec(memory_space=pltpu.SMEM)
+    return pl.pallas_call(
+        add_kernel,
+        out_shape=jax.ShapeDtypeStruct((ROWS_DEV, E), jnp.float32),
+        in_specs=[scalar, scalar, whole, whole, whole, whole],
+        out_specs=whole,
+        scratch_shapes=[
+            pltpu.VMEM((OWNERS * BLOCK, 2 * E), jnp.bfloat16),
+            pltpu.VMEM((8, OWNERS * BLOCK), jnp.float32),
+        ],
+        compiler_params=pltpu.CompilerParams(vmem_limit_bytes=VMEM_LIMIT),
+        cost_estimate=pl.CostEstimate(
+            flops=2 * 2048 * 1536 * 256, bytes_accessed=2_500_000, transcendentals=0
+        ),
+        name="add_rows",
+    )(me, counts, got, *late)
+
+
+def grp_swap(bit):
+    return [(g, g ^ bit) for g in range(16)]
+
+
+def shard_swap(bit):
+    return [(s, s ^ bit) for s in range(OWNERS)]
+
+
+def shard_turn(step):
+    return [(s, (s + step) % OWNERS) for s in range(OWNERS)]
+
+
+def x_turn(step):
+    return [(s, s // NX * NX + (s + step) % NX) for s in range(OWNERS)]
+
+
+def sum_grads(grads, g):
+    w1, b1, w2, b2, w3 = grads
+    small = jnp.concatenate([b1.reshape(16, 16), b2.reshape(16, 8), w3.reshape(16, 8)], axis=1)
+    small = jnp.pad(small[:, None, :], ((0, 0), (0, 7), (0, 96)))
+    part = jnp.concatenate(
+        [
+            w1[:, :E].reshape(16, 32, E),
+            w1[:, E:].reshape(16, 32, E),
+            w2.reshape(16, 16, E),
+            small,
+        ],
+        axis=1,
+    )
+    part = part.reshape(2, 2, 2, 2, 88, E).transpose(3, 2, 1, 0, 4, 5)
+    for k in range(4):
+        bit = (g >> k) & 1
+        keep = lax.dynamic_index_in_dim(part, bit, 0, False)
+        send = lax.dynamic_index_in_dim(part, 1 - bit, 0, False)
+        part = keep + lax.ppermute(send, "grp", grp_swap(1 << k))
+    for bit in (1, 2, 4, 8):
+        part = part + lax.ppermute(part, "shard", shard_swap(bit))
+    return part + lax.ppermute(part, "shard", shard_turn(16)) + lax.ppermute(part, "shard", shard_turn(32))
+
+
 def shards(
     target,
     history,
@@ -62,34 +252,25 @@
     attn_w3,
     pooled_gradient,
 ):
-    feature_width = history.shape[2]
+    g = lax.axis_index("grp")
+    me = lax.axis_index("shard").reshape(1)
     drow, grads = local_terms(
         target, history, lengths, pooled_gradient, attn_w1, attn_b1, attn_w2, attn_b2, attn_w3
     )
-    blocks = block_rows[0]
-    counts = block_counts[0]
-    capacity = blocks.shape[1]
-    used = jnp.arange(capacity, dtype=jnp.int32)[None, :] < counts[:, None]
-    rows = jnp.where(used[:, :, None], drow[blocks], 0.0)
-    dest = jnp.where(used, hist_ids.reshape(-1)[blocks] % ROWS_DEV, 0)
-    table = jnp.zeros((ROWS_DEV, feature_width), jnp.float32)
-    got_rows, got_dest = (
-        lax.all_to_all(rows, "shard", split_axis=0, concat_axis=0, tiled=True),
-        lax.all_to_all(dest, "shard", split_axis=0, concat_axis=0, tiled=True),
-    )
-    table = table.at[got_dest.reshape(-1)].add(got_rows.reshape(-1, feature_width))
-    totals = lax.psum((grads[0], grads[1], grads[2], grads[3], grads[4]), ("grp", "shard"))
-    groups = lax.axis_size("grp")
-    gindex = lax.axis_index("grp")
-    shares = tuple(
-        (
-            lax.dynamic_slice_in_dim(
-                arr, gindex * (arr.shape[0] // groups), arr.shape[0] // groups, 0
-            )
-            for arr in totals
-        )
-    )
-    return (table[None], shares[0], shares[1], shares[2], shares[3], shares[4])
+    send = pack(me, block_counts, drow, hist_ids, block_rows[0])
+    got = lax.all_to_all(send, "shard", split_axis=0, concat_axis=0, tiled=True)
+    slab = got[:, HALF:, :].reshape(OWNERS * 8, E)
+    late = [lax.ppermute(slab, "shard", x_turn(step)) for step in (1, 2, 3)]
+    table = add_rows(me, block_counts, got.reshape(OWNERS * BLOCK, E), late)
+    share = sum_grads(grads, g)
+    return (
+        table[None],
+        jnp.concatenate([share[:32], share[32:64]], axis=1),
+        share[80, :16],
+        share[64:80],
+        share[80, 16:24],
+        share[80, 24:32],
+    )
 
 
 def solution(mesh):

time: 572 us -> 128 us (0.22)
  the two profiles are of different devices: /device:TPU:6 before, /device:TPU:8 now
where the time goes in v1:
time: 128 us; the launch traced here: 127 us
  starting transfers between devices  70.5 us (55%)
  waiting for transfers between devices  36.4 us (28%)
  Pallas kernels  6.47 us (5%)
  other arithmetic  5.85 us (5%)
  local copies, waits for them, and re-layouts  4.04 us (3%)
  matrix products  2.84 us (2%)
    all_to_all x1, starting transfers between devices, shards(): got = lax.all_to_all(send, 'shard', split_axis=0, concat_axis=0, tiled=True)  18.3 us
    ppermute x4, starting transfers between devices, sum_grads(): part = part + lax.ppermute(part, 'shard', shard_swap(bit))  16.5 us
    ppermute x4, starting transfers between devices, sum_grads(): part = keep + lax.ppermute(send, 'grp', grp_swap(1 << k))  15.4 us
    ppermute x4, waiting for transfers between devices, sum_grads(): part = keep + lax.ppermute(send, 'grp', grp_swap(1 << k))  12.8 us
    ppermute x3, starting transfers between devices, shards(): late = [lax.ppermute(slab, 'shard', x_turn(step)) for step in (1, 2, 3)]  10.3 us
    ppermute x4, waiting for transfers between devices, sum_grads(): part = part + lax.ppermute(part, 'shard', shard_swap(bit))  9.61 us
    ppermute x1, starting transfers between devices, sum_grads(): lax.ppermute(part, 'shard', shard_turn(32))  8.08 us
    ppermute x1, waiting for transfers between devices, sum_grads(): lax.ppermute(part, 'shard', shard_turn(16))  7.18 us
  transfers between devices with their start and end apart: 14, of which 11 were waited for; matrix products, arithmetic and copies ran while one was open for 3% of the time, Pallas kernels for 2%

profile of v1, /device:TPU:8, one launch (start us, length us, event | category | flops | bytes accessed | tf_op | source)
XLA Modules:
  0.0 127.1 jit_solution(9119988888548603234)
XLA Ops:
  1.4 1.2 fusion.10
  2.6 0.7 bitcast_select_fusion
  4.0 1.1 pad_maximum_fusion
  8.4 0.8 copy-done.4
  9.2 2.0 %collective-permute-start.3 = (f32[2,2,2,88,128]{4,3,0,1,2:T(8,128)S(1)}, f32[2,2,2,88,128]{4,3,0,1,2:T(8,128)}, u32[]{:S(2)}, u32[]{:S(2)}) collective-permute-start(f32[2,2,2,88,128]{4,3,0,1,2:T(8,128)S(1)} %dynamic-slice_bitcast_fusion), channel_id=1, source_target_pairs={{0,48},{48,0},{96,144},{144,96},{192,240},{240,192},{288,336},{336... | collective-permute-start | bytes 1081352 | tf_op jit(solution)/shard_map/ppermute | solution.py:235
  12.1 3.1 %pack.1 = f32[48,32,128]{2,1,0:T(8,128)} custom-call(s32[1]{0:T(128)} %bitcast.me_ref, s32[1,48]{1,0:T(1,128)S(1)} %copy-done.3, f32[1024,128]{1,0:T(8,128)S(1)} %fusion.13.drow_ref, s32[8,128]{1,0:T(8,128)S(1)} %copy-done.2, s32[48,48]{1,0:T(8,128)S(1)} %bitcast.63), custom_call_target="tpu_custom_call" | custom-call | flops 1241513984 | bytes 2000000 | tf_op jit(solution)/shard_map/pack/pallas_call | solution.py:123
  15.3 18.3 %all-to-all-start = ((f32[48,32,128]{2,1,0:T(8,128)}), f32[48,32,128]{2,1,0:T(8,128)S(1)}, u32[]{:S(2)}, u32[]{:S(2)}) async-start(f32[48,32,128]{2,1,0:T(8,128)} %pack.1), calls=%async_computation | async-start | bytes 1572864 | tf_op jit(solution)/shard_map/all_to_all | solution.py:261
  33.6 1.0 bitcast_add_fusion
  34.6 2.4 %collective-permute-start.4 = (f32[2,2,88,128]{3,2,0,1:T(8,128)S(1)}, f32[2,2,88,128]{3,2,0,1:T(8,128)S(1)}, u32[]{:S(2)}, u32[]{:S(2)}) collective-permute-start(f32[2,2,88,128]{3,2,0,1:T(8,128)S(1)} %dynamic-slice_bitcast_fusion.1), channel_id=1, source_target_pairs={{0,96},{48,144},{96,0},{144,48},{192,288},{240,336},{288,192},{336... | collective-permute-start | bytes 540680 | tf_op jit(solution)/shard_map/ppermute | solution.py:235
  37.0 6.2 %collective-permute-done.4 = f32[2,2,88,128]{3,2,0,1:T(8,128)S(1)} collective-permute-done((f32[2,2,88,128]{3,2,0,1:T(8,128)S(1)}, f32[2,2,88,128]{3,2,0,1:T(8,128)S(1)}, u32[]{:S(2)}, u32[]{:S(2)}) %collective-permute-start.4) | collective-permute-done | bytes 180256 | tf_op jit(solution)/shard_map/ppermute | solution.py:235
  43.3 4.5 %collective-permute-start.5 = (f32[2,88,128]{2,1,0:T(8,128)S(1)}, f32[2,88,128]{2,1,0:T(8,128)S(1)}, u32[]{:S(2)}, u32[]{:S(2)}) collective-permute-start(f32[2,88,128]{2,1,0:T(8,128)S(1)} %dynamic-slice_bitcast_fusion.2), channel_id=1, source_target_pairs={{0,192},{48,240},{96,288},{144,336},{192,0},{240,48},{288,96},{336... | collective-permute-start | bytes 270344 | tf_op jit(solution)/shard_map/ppermute | solution.py:235
  47.8 3.2 %collective-permute-done.5 = f32[2,88,128]{2,1,0:T(8,128)S(1)} collective-permute-done((f32[2,88,128]{2,1,0:T(8,128)S(1)}, f32[2,88,128]{2,1,0:T(8,128)S(1)}, u32[]{:S(2)}, u32[]{:S(2)}) %collective-permute-start.5) | collective-permute-done | bytes 90144 | tf_op jit(solution)/shard_map/ppermute | solution.py:235
  51.0 6.5 %collective-permute-start.6 = (f32[88,128]{1,0:T(8,128)S(1)}, f32[88,128]{1,0:T(8,128)S(1)}, u32[]{:S(2)}, u32[]{:S(2)}) collective-permute-start(f32[88,128]{1,0:T(8,128)S(1)} %dynamic-slice_bitcast_fusion.3), channel_id=1, source_target_pairs={{0,384},{48,432},{96,480},{144,528},{192,576},{240,624},{288,672},... | collective-permute-start | bytes 135176 | tf_op jit(solution)/shard_map/ppermute | solution.py:235
  57.5 3.3 %collective-permute-done.6 = f32[88,128]{1,0:T(8,128)S(1)} collective-permute-done((f32[88,128]{1,0:T(8,128)S(1)}, f32[88,128]{1,0:T(8,128)S(1)}, u32[]{:S(2)}, u32[]{:S(2)}) %collective-permute-start.6) | collective-permute-done | bytes 45088 | tf_op jit(solution)/shard_map/ppermute | solution.py:235
  60.9 3.5 %collective-permute-start.7 = (f32[88,128]{1,0:T(8,128)S(1)}, f32[88,128]{1,0:T(8,128)S(1)}, u32[]{:S(2)}, u32[]{:S(2)}) collective-permute-start(f32[88,128]{1,0:T(8,128)S(1)} %bitcast_add_fusion.3), channel_id=1, source_target_pairs={{0,1},{1,0},{2,3},{3,2},{4,5},{5,4},{6,7},{7,6},{8,9},{9,8},{10,11... | collective-permute-start | bytes 135176 | tf_op jit(solution)/shard_map/ppermute | solution.py:237
  64.4 2.4 %collective-permute-done.7 = f32[88,128]{1,0:T(8,128)S(1)} collective-permute-done((f32[88,128]{1,0:T(8,128)S(1)}, f32[88,128]{1,0:T(8,128)S(1)}, u32[]{:S(2)}, u32[]{:S(2)}) %collective-permute-start.7) | collective-permute-done | bytes 45088 | tf_op jit(solution)/shard_map/ppermute | solution.py:237
  66.8 5.1 %collective-permute-start.8 = (f32[88,128]{1,0:T(8,128)S(1)}, f32[88,128]{1,0:T(8,128)S(1)}, u32[]{:S(2)}, u32[]{:S(2)}) collective-permute-start(f32[88,128]{1,0:T(8,128)S(1)} %add.112), channel_id=1, source_target_pairs={{0,2},{1,3},{2,0},{3,1},{4,6},{5,7},{6,4},{7,5},{8,10},{9,11},{10,... | collective-permute-start | bytes 135176 | tf_op jit(solution)/shard_map/ppermute | solution.py:237
  72.0 2.3 %collective-permute-done.8 = f32[88,128]{1,0:T(8,128)S(1)} collective-permute-done((f32[88,128]{1,0:T(8,128)S(1)}, f32[88,128]{1,0:T(8,128)S(1)}, u32[]{:S(2)}, u32[]{:S(2)}) %collective-permute-start.8) | collective-permute-done | bytes 45088 | tf_op jit(solution)/shard_map/ppermute | solution.py:237
  74.3 3.5 %collective-permute-start.9 = (f32[88,128]{1,0:T(8,128)S(1)}, f32[88,128]{1,0:T(8,128)S(1)}, u32[]{:S(2)}, u32[]{:S(2)}) collective-permute-start(f32[88,128]{1,0:T(8,128)S(1)} %add.113), channel_id=1, source_target_pairs={{0,4},{1,5},{2,6},{3,7},{4,0},{5,1},{6,2},{7,3},{8,12},{9,13},{10,... | collective-permute-start | bytes 135176 | tf_op jit(solution)/shard_map/ppermute | solution.py:237
  77.8 2.4 %collective-permute-done.9 = f32[88,128]{1,0:T(8,128)S(1)} collective-permute-done((f32[88,128]{1,0:T(8,128)S(1)}, f32[88,128]{1,0:T(8,128)S(1)}, u32[]{:S(2)}, u32[]{:S(2)}) %collective-permute-start.9) | collective-permute-done | bytes 45088 | tf_op jit(solution)/shard_map/ppermute | solution.py:237
  80.2 4.4 %collective-permute-start.10 = (f32[88,128]{1,0:T(8,128)S(1)}, f32[88,128]{1,0:T(8,128)S(1)}, u32[]{:S(2)}, u32[]{:S(2)}) collective-permute-start(f32[88,128]{1,0:T(8,128)S(1)} %add.114), channel_id=1, source_target_pairs={{0,8},{1,9},{2,10},{3,11},{4,12},{5,13},{6,14},{7,15},{8,0},{9,1},... | collective-permute-start | bytes 135176 | tf_op jit(solution)/shard_map/ppermute | solution.py:237
  84.6 2.4 %collective-permute-done.10 = f32[88,128]{1,0:T(8,128)S(1)} collective-permute-done((f32[88,128]{1,0:T(8,128)S(1)}, f32[88,128]{1,0:T(8,128)S(1)}, u32[]{:S(2)}, u32[]{:S(2)}) %collective-permute-start.10) | collective-permute-done | bytes 45088 | tf_op jit(solution)/shard_map/ppermute | solution.py:237
  87.1 8.1 %collective-permute-start.12 = (f32[88,128]{1,0:T(8,128)S(1)}, f32[88,128]{1,0:T(8,128)S(1)}, u32[]{:S(2)}, u32[]{:S(2)}) collective-permute-start(f32[88,128]{1,0:T(8,128)S(1)} %add.115), channel_id=1, source_target_pairs={{0,32},{1,33},{2,34},{3,35},{4,36},{5,37},{6,38},{7,39},{8,40},{9,... | collective-permute-start | bytes 135176 | tf_op jit(solution)/shard_map/ppermute | solution.py:238
  95.2 1.9 %collective-permute-start.11 = (f32[88,128]{1,0:T(8,128)S(1)}, f32[88,128]{1,0:T(8,128)S(1)}, u32[]{:S(2)}, u32[]{:S(2)}) collective-permute-start(f32[88,128]{1,0:T(8,128)S(1)} %add.115), channel_id=1, source_target_pairs={{0,16},{1,17},{2,18},{3,19},{4,20},{5,21},{6,22},{7,23},{8,24},{9,... | collective-permute-start | bytes 135176 | tf_op jit(solution)/shard_map/ppermute | solution.py:238
  97.1 0.7 collective-permute-done.12
  97.8 7.2 %collective-permute-done.11 = f32[88,128]{1,0:T(8,128)S(1)} collective-permute-done((f32[88,128]{1,0:T(8,128)S(1)}, f32[88,128]{1,0:T(8,128)S(1)}, u32[]{:S(2)}, u32[]{:S(2)}) %collective-permute-start.11) | collective-permute-done | bytes 45088 | tf_op jit(solution)/shard_map/ppermute | solution.py:238
  106.9 5.6 %collective-permute-start.2 = (f32[384,128]{1,0:T(8,128)S(1)}, f32[384,128]{1,0:T(8,128)S(1)}, u32[]{:S(2)}, u32[]{:S(2)}) collective-permute-start(f32[384,128]{1,0:T(8,128)S(1)} %slice_bitcast_fusion), channel_id=1, source_target_pairs={{0,3},{1,0},{2,1},{3,2},{4,7},{5,4},{6,5},{7,6},{8,11},{9,8},{10,9... | collective-permute-start | bytes 589832 | tf_op jit(solution)/shard_map/ppermute | solution.py:263
  112.5 2.5 %collective-permute-start.1 = (f32[384,128]{1,0:T(8,128)S(1)}, f32[384,128]{1,0:T(8,128)S(1)}, u32[]{:S(2)}, u32[]{:S(2)}) collective-permute-start(f32[384,128]{1,0:T(8,128)S(1)} %slice_bitcast_fusion), channel_id=1, source_target_pairs={{0,2},{1,3},{2,0},{3,1},{4,6},{5,7},{6,4},{7,5},{8,10},{9,11},{10,... | collective-permute-start | bytes 589832 | tf_op jit(solution)/shard_map/ppermute | solution.py:263
  115.0 2.2 %collective-permute-start = (f32[384,128]{1,0:T(8,128)S(1)}, f32[384,128]{1,0:T(8,128)S(1)}, u32[]{:S(2)}, u32[]{:S(2)}) collective-permute-start(f32[384,128]{1,0:T(8,128)S(1)} %slice_bitcast_fusion), channel_id=1, source_target_pairs={{0,1},{1,2},{2,3},{3,0},{4,5},{5,6},{6,7},{7,4},{8,9},{9,10},{10,1... | collective-permute-start | bytes 589832 | tf_op jit(solution)/shard_map/ppermute | solution.py:263
  117.7 3.8 %collective-permute-done.1.late1_ref = f32[384,128]{1,0:T(8,128)S(1)} collective-permute-done((f32[384,128]{1,0:T(8,128)S(1)}, f32[384,128]{1,0:T(8,128)S(1)}, u32[]{:S(2)}, u32[]{:S(2)}) %collective-permute-start.1) | collective-permute-done | bytes 196640 | tf_op jit(solution)/shard_map/ppermute | solution.py:263
  121.5 2.2 %collective-permute-done.late0_ref = f32[384,128]{1,0:T(8,128)S(1)} collective-permute-done((f32[384,128]{1,0:T(8,128)S(1)}, f32[384,128]{1,0:T(8,128)S(1)}, u32[]{:S(2)}, u32[]{:S(2)}) %collective-permute-start) | collective-permute-done | bytes 196640 | tf_op jit(solution)/shard_map/ppermute | solution.py:263
  123.8 3.3 %add_rows.1 = f32[2048,128]{1,0:T(8,128)} custom-call(s32[1]{0:T(128)} %bitcast.me_ref, s32[1,48]{1,0:T(1,128)S(1)} %copy-done.3, f32[1536,128]{1,0:T(8,128)S(1)} %bitcast.62, f32[384,128]{1,0:T(8,128)S(1)} %collective-permute-done.late0_ref, f32[384,128]{1,0:T(8,128)S(1)} %collective-permute-done.1.late1_ref, f32[384,128]{1,0:T(8,128)S(1)} %collective-permute-done.2.late2_ref), custom_call_target="tpu_custom_call" | custom-call | flops 1610612736 | bytes 2500000 | tf_op jit(solution)/shard_map/add_rows/pallas_call | solution.py:184
  (61 shorter events, 7.9 us)
Async XLA Ops:
  0.6 4.5 %copy-start = (bf16[512,256]{1,0:T(8,128)(2,1)S(1)}, bf16[512,256]{1,0:T(8,128)(2,1)}, u32[]{:S(2)}) copy-start(bf16[512,256]{1,0:T(8,128)(2,1)} %param.18) | copy-start | bytes 786436
  0.6 4.5 %copy-start.10 = (f32[256]{0:T(256)S(1)}, f32[256]{0:T(256)}, u32[]{:S(2)}) copy-start(f32[256]{0:T(256)} %param.19) | copy-start | bytes 3076
  5.1 0.8 copy-start.6
  5.1 0.8 copy-start.8
  5.1 0.8 copy-start.11
  8.3 0.9 copy-start.4
  8.4 3.4 %copy-start.9 = (s32[8]{0:T(128)S(1)}, s32[8]{0:T(128)}, u32[]{:S(2)}) copy-start(s32[8]{0:T(128)} %param.14) | copy-start | bytes 100
  8.4 3.5 %copy-start.7 = (f32[8,128]{1,0:T(8,128)S(1)}, f32[8,128]{1,0:T(8,128)}, u32[]{:S(2)}) copy-start(f32[8,128]{1,0:T(8,128)} %param.23) | copy-start | bytes 12292
  9.2 2.8 %copy-start.1 = (s32[1,48,48]{2,1,0:T(8,128)S(1)}, s32[1,48,48]{2,1,0:T(8,128)}, u32[]{:S(2)}) copy-start(s32[1,48,48]{2,1,0:T(8,128)} %param.16) | copy-start | bytes 27652
  9.2 2.8 %copy-start.2 = (s32[8,128]{1,0:T(8,128)S(1)}, s32[8,128]{1,0:T(8,128)}, u32[]{:S(2)}) copy-start(s32[8,128]{1,0:T(8,128)} %ids_ref.1) | copy-start | bytes 12292
  9.2 2.8 %copy-start.3 = (s32[1,48]{1,0:T(1,128)S(1)}, s32[1,48]{1,0:T(1,128)}, u32[]{:S(2)}) copy-start(s32[1,48]{1,0:T(1,128)} %counts_ref.3) | copy-start | bytes 580
  9.2 24.3 %collective-permute-start.3 = (f32[2,2,2,88,128]{4,3,0,1,2:T(8,128)S(1)}, f32[2,2,2,88,128]{4,3,0,1,2:T(8,128)}, u32[]{:S(2)}, u32[]{:S(2)}) collective-permute-start(f32[2,2,2,88,128]{4,3,0,1,2:T(8,128)S(1)} %dynamic-slice_bitcast_fusion), channel_id=1, source_target_pairs={{0,48},{48,0},{96,144},{144,96},{192,240},{240,192},{288,336},{336... | collective-permute-start | bytes 1081352 | tf_op jit(solution)/shard_map/ppermute | solution.py:235
  12.1 21.5 %copy-start.5 = (f32[2,2,2,2,88,128]{5,4,3,2,1,0:T(8,128)S(1)}, f32[2,2,2,2,88,128]{5,4,3,2,1,0:T(8,128)}, u32[]{:S(2)}) copy-start(f32[2,2,2,2,88,128]{5,4,3,2,1,0:T(8,128)} %copy-done.4) | copy-start | bytes 2162692
  15.3 91.6 %all-to-all-start = ((f32[48,32,128]{2,1,0:T(8,128)}), f32[48,32,128]{2,1,0:T(8,128)S(1)}, u32[]{:S(2)}, u32[]{:S(2)}) async-start(f32[48,32,128]{2,1,0:T(8,128)} %pack.1), calls=%async_computation | async-start | bytes 1572864 | tf_op jit(solution)/shard_map/all_to_all | solution.py:261
  34.6 8.6 %collective-permute-start.4 = (f32[2,2,88,128]{3,2,0,1:T(8,128)S(1)}, f32[2,2,88,128]{3,2,0,1:T(8,128)S(1)}, u32[]{:S(2)}, u32[]{:S(2)}) collective-permute-start(f32[2,2,88,128]{3,2,0,1:T(8,128)S(1)} %dynamic-slice_bitcast_fusion.1), channel_id=1, source_target_pairs={{0,96},{48,144},{96,0},{144,48},{192,288},{240,336},{288,192},{336... | collective-permute-start | bytes 540680 | tf_op jit(solution)/shard_map/ppermute | solution.py:235
  43.3 7.7 %collective-permute-start.5 = (f32[2,88,128]{2,1,0:T(8,128)S(1)}, f32[2,88,128]{2,1,0:T(8,128)S(1)}, u32[]{:S(2)}, u32[]{:S(2)}) collective-permute-start(f32[2,88,128]{2,1,0:T(8,128)S(1)} %dynamic-slice_bitcast_fusion.2), channel_id=1, source_target_pairs={{0,192},{48,240},{96,288},{144,336},{192,0},{240,48},{288,96},{336... | collective-permute-start | bytes 270344 | tf_op jit(solution)/shard_map/ppermute | solution.py:235
  51.0 9.8 %collective-permute-start.6 = (f32[88,128]{1,0:T(8,128)S(1)}, f32[88,128]{1,0:T(8,128)S(1)}, u32[]{:S(2)}, u32[]{:S(2)}) collective-permute-start(f32[88,128]{1,0:T(8,128)S(1)} %dynamic-slice_bitcast_fusion.3), channel_id=1, source_target_pairs={{0,384},{48,432},{96,480},{144,528},{192,576},{240,624},{288,672},... | collective-permute-start | bytes 135176 | tf_op jit(solution)/shard_map/ppermute | solution.py:235
  60.9 5.9 %collective-permute-start.7 = (f32[88,128]{1,0:T(8,128)S(1)}, f32[88,128]{1,0:T(8,128)S(1)}, u32[]{:S(2)}, u32[]{:S(2)}) collective-permute-start(f32[88,128]{1,0:T(8,128)S(1)} %bitcast_add_fusion.3), channel_id=1, source_target_pairs={{0,1},{1,0},{2,3},{3,2},{4,5},{5,4},{6,7},{7,6},{8,9},{9,8},{10,11... | collective-permute-start | bytes 135176 | tf_op jit(solution)/shard_map/ppermute | solution.py:237
  66.8 7.4 %collective-permute-start.8 = (f32[88,128]{1,0:T(8,128)S(1)}, f32[88,128]{1,0:T(8,128)S(1)}, u32[]{:S(2)}, u32[]{:S(2)}) collective-permute-start(f32[88,128]{1,0:T(8,128)S(1)} %add.112), channel_id=1, source_target_pairs={{0,2},{1,3},{2,0},{3,1},{4,6},{5,7},{6,4},{7,5},{8,10},{9,11},{10,... | collective-permute-start | bytes 135176 | tf_op jit(solution)/shard_map/ppermute | solution.py:237
  74.3 5.9 %collective-permute-start.9 = (f32[88,128]{1,0:T(8,128)S(1)}, f32[88,128]{1,0:T(8,128)S(1)}, u32[]{:S(2)}, u32[]{:S(2)}) collective-permute-start(f32[88,128]{1,0:T(8,128)S(1)} %add.113), channel_id=1, source_target_pairs={{0,4},{1,5},{2,6},{3,7},{4,0},{5,1},{6,2},{7,3},{8,12},{9,13},{10,... | collective-permute-start | bytes 135176 | tf_op jit(solution)/shard_map/ppermute | solution.py:237
  80.2 6.8 %collective-permute-start.10 = (f32[88,128]{1,0:T(8,128)S(1)}, f32[88,128]{1,0:T(8,128)S(1)}, u32[]{:S(2)}, u32[]{:S(2)}) collective-permute-start(f32[88,128]{1,0:T(8,128)S(1)} %add.114), channel_id=1, source_target_pairs={{0,8},{1,9},{2,10},{3,11},{4,12},{5,13},{6,14},{7,15},{8,0},{9,1},... | collective-permute-start | bytes 135176 | tf_op jit(solution)/shard_map/ppermute | solution.py:237
  87.1 10.8 %collective-permute-start.12 = (f32[88,128]{1,0:T(8,128)S(1)}, f32[88,128]{1,0:T(8,128)S(1)}, u32[]{:S(2)}, u32[]{:S(2)}) collective-permute-start(f32[88,128]{1,0:T(8,128)S(1)} %add.115), channel_id=1, source_target_pairs={{0,32},{1,33},{2,34},{3,35},{4,36},{5,37},{6,38},{7,39},{8,40},{9,... | collective-permute-start | bytes 135176 | tf_op jit(solution)/shard_map/ppermute | solution.py:238
  95.2 9.8 %collective-permute-start.11 = (f32[88,128]{1,0:T(8,128)S(1)}, f32[88,128]{1,0:T(8,128)S(1)}, u32[]{:S(2)}, u32[]{:S(2)}) collective-permute-start(f32[88,128]{1,0:T(8,128)S(1)} %add.115), channel_id=1, source_target_pairs={{0,16},{1,17},{2,18},{3,19},{4,20},{5,21},{6,22},{7,23},{8,24},{9,... | collective-permute-start | bytes 135176 | tf_op jit(solution)/shard_map/ppermute | solution.py:238
  106.9 10.8 %collective-permute-start.2 = (f32[384,128]{1,0:T(8,128)S(1)}, f32[384,128]{1,0:T(8,128)S(1)}, u32[]{:S(2)}, u32[]{:S(2)}) collective-permute-start(f32[384,128]{1,0:T(8,128)S(1)} %slice_bitcast_fusion), channel_id=1, source_target_pairs={{0,3},{1,0},{2,1},{3,2},{4,7},{5,4},{6,5},{7,6},{8,11},{9,8},{10,9... | collective-permute-start | bytes 589832 | tf_op jit(solution)/shard_map/ppermute | solution.py:263
  112.5 9.1 %collective-permute-start.1 = (f32[384,128]{1,0:T(8,128)S(1)}, f32[384,128]{1,0:T(8,128)S(1)}, u32[]{:S(2)}, u32[]{:S(2)}) collective-permute-start(f32[384,128]{1,0:T(8,128)S(1)} %slice_bitcast_fusion), channel_id=1, source_target_pairs={{0,2},{1,3},{2,0},{3,1},{4,6},{5,7},{6,4},{7,5},{8,10},{9,11},{10,... | collective-permute-start | bytes 589832 | tf_op jit(solution)/shard_map/ppermute | solution.py:263
  115.0 8.8 %collective-permute-start = (f32[384,128]{1,0:T(8,128)S(1)}, f32[384,128]{1,0:T(8,128)S(1)}, u32[]{:S(2)}, u32[]{:S(2)}) collective-permute-start(f32[384,128]{1,0:T(8,128)S(1)} %slice_bitcast_fusion), channel_id=1, source_target_pairs={{0,1},{1,2},{2,3},{3,0},{4,5},{5,6},{6,7},{7,4},{8,9},{9,10},{10,1... | collective-permute-start | bytes 589832 | tf_op jit(solution)/shard_map/ppermute | solution.py:263

commit v2 on v1

--- a/solution.py
+++ b/solution.py
@@ -13,49 +13,7 @@
 NX = 4
 PIECE = 6
 SLOTS = 1024
-VMEM_LIMIT = 48 * 1024 * 1024
-
-
-def local_terms(
-    target, history, lengths, pooled_gradient, attn_w1, attn_b1, attn_w2, attn_b2, attn_w3
-):
-    sample_count, slot_count, feature_width = history.shape
-    query = target.astype(jnp.float32)[:, None, :]
-    hist = history.astype(jnp.float32)
-    item_minus_target = (query - hist).astype(jnp.bfloat16)
-    item_times_target = (query * hist).astype(jnp.bfloat16)
-    query_tile = jnp.broadcast_to(target[:, None, :], history.shape)
-    feature_rows = jnp.concatenate(
-        [query_tile, history, item_minus_target, item_times_target], axis=-1
-    ).reshape(sample_count * slot_count, 4 * feature_width)
-    act1 = jax.nn.sigmoid(
-        jnp.dot(feature_rows, attn_w1, preferred_element_type=jnp.float32) + attn_b1
-    )
-    act1_low = act1.astype(jnp.bfloat16)
-    act2 = jax.nn.sigmoid(jnp.dot(act1_low, attn_w2, preferred_element_type=jnp.float32) + attn_b2)
-    live_mask = (jnp.arange(slot_count, dtype=jnp.int32)[None, :] < lengths[:, None]).reshape(-1)
-    attention_score = jnp.where(live_mask, jnp.sum(act2 * attn_w3, axis=-1), 0.0)
-    dscore = jnp.sum(pooled_gradient[:, None, :] * hist, axis=-1).reshape(-1)
-    dscore = jnp.where(live_mask, dscore, 0.0)
-    dz2_full = dscore[:, None] * attn_w3[None, :] * act2 * (1.0 - act2)
-    dz2 = dz2_full.astype(jnp.bfloat16)
-    grad_w3 = jnp.sum(dscore[:, None] * act2, axis=0)
-    grad_b2 = jnp.sum(dz2_full, axis=0)
-    grad_w2 = jnp.dot(act1_low.T, dz2, preferred_element_type=jnp.float32)
-    dz1_full = jnp.dot(dz2, attn_w2.T, preferred_element_type=jnp.float32) * act1 * (1.0 - act1)
-    dz1 = dz1_full.astype(jnp.bfloat16)
-    grad_b1 = jnp.sum(dz1_full, axis=0)
-    grad_w1 = jnp.dot(feature_rows.T, dz1, preferred_element_type=jnp.float32)
-    dfeat = jnp.dot(dz1, attn_w1.T, preferred_element_type=jnp.float32)
-    part_h = dfeat[:, feature_width : 2 * feature_width]
-    part_d = dfeat[:, 2 * feature_width : 3 * feature_width]
-    part_p = dfeat[:, 3 * feature_width :]
-    qflat = jnp.broadcast_to(query, hist.shape).reshape(-1, feature_width)
-    pooled_contribution = (
-        attention_score.reshape(sample_count, slot_count)[:, :, None] * pooled_gradient[:, None, :]
-    ).reshape(-1, feature_width)
-    drow = part_h - part_d + part_p * qflat + pooled_contribution
-    return (drow, (grad_w1, grad_b1, grad_w2, grad_b2, grad_w3))
+VMEM_LIMIT = 24 * 1024 * 1024
 
 
 def iota(shape, dim):
@@ -66,6 +24,109 @@
     high = rows.astype(jnp.bfloat16)
     low = (rows - high.astype(jnp.float32)).astype(jnp.bfloat16)
     return jnp.concatenate([high, low], axis=1)
+
+
+CHUNK = 256
+PART = 88
+
+
+def sigmoid(z):
+    return 0.5 * jnp.tanh(0.5 * z) + 0.5
+
+
+def places():
+    at = []
+    for g in range(16):
+        core, y0, y1, y2 = g & 1, (g >> 1) & 1, (g >> 2) & 1, (g >> 3) & 1
+        at.append(core * 8 + (y0 ^ y2) * 4 + (y1 ^ y2) * 2 + y2)
+    return at
+
+
+def dense_kernel(
+    lengths_ref, target_ref, hist_ref, pg_ref, w1_ref, b1_ref, w2_ref, b2_ref, w3_ref,
+    drow_ref, part_ref, feats, act1s, dz2s, dz1s,
+):
+    query = target_ref[...].astype(jnp.float32)
+    w1, w2, w3 = w1_ref[...], w2_ref[...], w3_ref[...]
+    grad_w3 = jnp.zeros((1, E), jnp.float32)
+    grad_b2 = jnp.zeros((1, E), jnp.float32)
+    grad_b1 = jnp.zeros((1, 2 * E), jnp.float32)
+    samples = CHUNK // 128
+    across = (((1,), (1,)), ((), ()))
+    down = (((0,), (0,)), ((), ()))
+    for c in range(SLOTS // CHUNK):
+        rows = slice(c * CHUNK, (c + 1) * CHUNK)
+        hist_low = hist_ref[rows, :]
+        hist = hist_low.astype(jnp.float32)
+        def spread(rows_of):
+            parts = [rows_of[b : b + 1, :] for b in range(c * samples, (c + 1) * samples)]
+            return jnp.concatenate([jnp.broadcast_to(v, (128, E)) for v in parts], axis=0)
+        q = spread(query)
+        pg = spread(pg_ref)
+        live = jnp.concatenate(
+            [iota((128, 1), 0) < lengths_ref[b] for b in range(c * samples, (c + 1) * samples)], axis=0
+        )
+        feat = jnp.concatenate(
+            [q.astype(jnp.bfloat16), hist_low, (q - hist).astype(jnp.bfloat16), (q * hist).astype(jnp.bfloat16)],
+            axis=1,
+        )
+        feats[rows, :] = feat
+        act1 = sigmoid(jnp.dot(feat, w1, preferred_element_type=jnp.float32) + b1_ref[...])
+        act1_low = act1.astype(jnp.bfloat16)
+        act1s[rows, :] = act1_low
+        act2 = sigmoid(jnp.dot(act1_low, w2, preferred_element_type=jnp.float32) + b2_ref[...])
+        score = jnp.where(live, jnp.sum(act2 * w3, axis=1, keepdims=True), 0.0)
+        dscore = jnp.where(live, jnp.sum(pg * hist, axis=1, keepdims=True), 0.0)
+        dact2 = dscore * act2
+        grad_w3 += jnp.sum(dact2, axis=0, keepdims=True)
+        dz2_full = dact2 * w3 * (1.0 - act2)
+        grad_b2 += jnp.sum(dz2_full, axis=0, keepdims=True)
+        dz2 = dz2_full.astype(jnp.bfloat16)
+        dz2s[rows, :] = dz2
+        back = lax.dot_general(dz2, w2, across, preferred_element_type=jnp.float32)
+        dz1_full = back * act1 * (1.0 - act1)
+        grad_b1 += jnp.sum(dz1_full, axis=0, keepdims=True)
+        dz1 = dz1_full.astype(jnp.bfloat16)
+        dz1s[rows, :] = dz1
+        dfeat = lax.dot_general(dz1, w1[E:, :], across, preferred_element_type=jnp.float32)
+        drow_ref[rows, :] = dfeat[:, :E] - dfeat[:, E : 2 * E] + dfeat[:, 2 * E :] * q + score * pg
+
+    grad_w1 = lax.dot_general(feats[...], dz1s[...], down, preferred_element_type=jnp.float32)
+    grad_w2 = lax.dot_general(act1s[...], dz2s[...], down, preferred_element_type=jnp.float32)
+    sub = iota((8, E), 0)
+    small = jnp.where(sub == 0, grad_b1[:, :E], jnp.where(sub == 1, grad_b1[:, E:], 0.0))
+    small = jnp.where(sub == 2, grad_b2, jnp.where(sub == 3, grad_w3, small))
+    for g, at in enumerate(places()):
+        base = at * PART
+        part_ref[base : base + 32, :] = grad_w1[32 * g : 32 * g + 32, :E]
+        part_ref[base + 32 : base + 64, :] = grad_w1[32 * g : 32 * g + 32, E:]
+        part_ref[base + 64 : base + 80, :] = grad_w2[16 * g : 16 * g + 16, :]
+        part_ref[base + 80 : base + 88, :] = small
+
+
+def dense(lengths, target, hist, pg, w1, b1, w2, b2, w3):
+    whole = pl.BlockSpec(memory_space=pltpu.VMEM)
+    scalar = pl.BlockSpec(memory_space=pltpu.SMEM)
+    return pl.pallas_call(
+        dense_kernel,
+        out_shape=[
+            jax.ShapeDtypeStruct((SLOTS, E), jnp.float32),
+            jax.ShapeDtypeStruct((16 * PART, E), jnp.float32),
+        ],
+        in_specs=[scalar] + [whole] * 8,
+        out_specs=[whole, whole],
+        scratch_shapes=[
+            pltpu.VMEM((SLOTS, 4 * E), jnp.bfloat16),
+            pltpu.VMEM((SLOTS, 2 * E), jnp.bfloat16),
+            pltpu.VMEM((SLOTS, E), jnp.bfloat16),
+            pltpu.VMEM((SLOTS, 2 * E), jnp.bfloat16),
+        ],
+        compiler_params=pltpu.CompilerParams(vmem_limit_bytes=VMEM_LIMIT),
+        cost_estimate=pl.CostEstimate(
+            flops=1_100_000_000, bytes_accessed=2_200_000, transcendentals=400_000
+        ),
+        name="dense",
+    )(lengths, target, hist, pg, w1, b1, w2, b2, w3)
 
 
 def pack_kernel(me_ref, counts_ref, drow_ref, ids_ref, blocks_ref, send_ref, pick, source):
@@ -138,9 +199,10 @@
 
 
 STEP = 512
-
-
-def add_kernel(me_ref, counts_ref, got_ref, late0_ref, late1_ref, late2_ref, table_ref, rows, dest):
+NEAR = PART + OWNERS * 8
+
+
+def add_kernel(me_ref, counts_ref, got_ref, near_ref, table_ref, rows, dest):
     groups = OWNERS // NX
     for g in range(groups):
         rows[g * 128 : (g + 1) * 128, :] = split(got_ref[g * 128 : (g + 1) * 128, :])
@@ -163,14 +225,8 @@
     def _():
         for k in range(NX):
             for g in range(3):
-                if k == 0:
-                    tiles = [
-                        got_ref[s * BLOCK + HALF : (s + 1) * BLOCK, :]
-                        for s in range(16 * g, 16 * g + 16)
-                    ]
-                else:
-                    late = (late0_ref, late1_ref, late2_ref)[k - 1]
-                    tiles = [late[s * 8 : s * 8 + 8, :] for s in range(16 * g, 16 * g + 16)]
+                base = k * NEAR + PART
+                tiles = [near_ref[base + t * 8 : base + t * 8 + 8, :] for t in range(16 * g, 16 * g + 16)]
                 at = (k * 3 + g) * 128
                 rows[at : at + 128, :] = split(jnp.concatenate(tiles, axis=0))
                 dest[:, at : at + 128] = jnp.broadcast_to(sum(tiles)[7:8, :], (8, E))
@@ -178,13 +234,13 @@
             table_ref[t * STEP : (t + 1) * STEP, :] += product(t)
 
 
-def add_rows(me, counts, got, late):
+def add_rows(me, counts, got, near):
     whole = pl.BlockSpec(memory_space=pltpu.VMEM)
     scalar = pl.BlockSpec(memory_space=pltpu.SMEM)
     return pl.pallas_call(
         add_kernel,
         out_shape=jax.ShapeDtypeStruct((ROWS_DEV, E), jnp.float32),
-        in_specs=[scalar, scalar, whole, whole, whole, whole],
+        in_specs=[scalar, scalar, whole, whole],
         out_specs=whole,
         scratch_shapes=[
             pltpu.VMEM((OWNERS * BLOCK, 2 * E), jnp.bfloat16),
@@ -195,47 +251,90 @@
             flops=2 * 2048 * 1536 * 256, bytes_accessed=2_500_000, transcendentals=0
         ),
         name="add_rows",
-    )(me, counts, got, *late)
-
-
-def grp_swap(bit):
-    return [(g, g ^ bit) for g in range(16)]
-
-
-def shard_swap(bit):
-    return [(s, s ^ bit) for s in range(OWNERS)]
-
-
-def shard_turn(step):
-    return [(s, (s + step) % OWNERS) for s in range(OWNERS)]
-
-
-def x_turn(step):
-    return [(s, s // NX * NX + (s + step) % NX) for s in range(OWNERS)]
-
-
-def sum_grads(grads, g):
-    w1, b1, w2, b2, w3 = grads
-    small = jnp.concatenate([b1.reshape(16, 16), b2.reshape(16, 8), w3.reshape(16, 8)], axis=1)
-    small = jnp.pad(small[:, None, :], ((0, 0), (0, 7), (0, 96)))
-    part = jnp.concatenate(
-        [
-            w1[:, :E].reshape(16, 32, E),
-            w1[:, E:].reshape(16, 32, E),
-            w2.reshape(16, 16, E),
-            small,
-        ],
-        axis=1,
-    )
-    part = part.reshape(2, 2, 2, 2, 88, E).transpose(3, 2, 1, 0, 4, 5)
-    for k in range(4):
-        bit = (g >> k) & 1
-        keep = lax.dynamic_index_in_dim(part, bit, 0, False)
-        send = lax.dynamic_index_in_dim(part, 1 - bit, 0, False)
-        part = keep + lax.ppermute(send, "grp", grp_swap(1 << k))
-    for bit in (1, 2, 4, 8):
-        part = part + lax.ppermute(part, "shard", shard_swap(bit))
-    return part + lax.ppermute(part, "shard", shard_turn(16)) + lax.ppermute(part, "shard", shard_turn(32))
+    )(me, counts, got, near)
+
+
+SWAPS = (1, 2, 4, 14)
+
+
+def grp_swap(bits):
+    return [(g, g ^ bits) for g in range(16)]
+
+
+X_GROUPS = [[z * NX + x for x in range(NX)] for z in range(OWNERS // NX)]
+Z_GROUPS = [[z * NX + x for z in range(OWNERS // NX)] for x in range(NX)]
+
+
+def join_kernel(keep_ref, there_ref, got_ref, near_ref):
+    part = keep_ref[...] + there_ref[...]
+    for x in range(NX):
+        near_ref[x, :PART, :] = part
+        for s in range(OWNERS):
+            near_ref[x, PART + s * 8 : PART + s * 8 + 8, :] = got_ref[s * BLOCK + HALF : (s + 1) * BLOCK, :]
+
+
+def join(keep, there, got):
+    whole = pl.BlockSpec(memory_space=pltpu.VMEM)
+    return pl.pallas_call(
+        join_kernel,
+        out_shape=jax.ShapeDtypeStruct((NX, NEAR, E), jnp.float32),
+        in_specs=[whole, whole, whole],
+        out_specs=whole,
+        compiler_params=pltpu.CompilerParams(vmem_limit_bytes=VMEM_LIMIT),
+        cost_estimate=pl.CostEstimate(flops=11264, bytes_accessed=2_000_000, transcendentals=0),
+        name="join",
+    )(keep, there, got)
+
+
+def spread_kernel(near_ref, out_ref):
+    part = near_ref[:PART, :]
+    for x in range(1, NX):
+        part += near_ref[x * NEAR : x * NEAR + PART, :]
+    for z in range(OWNERS // NX):
+        out_ref[z] = part
+
+
+def spread_sum(near):
+    whole = pl.BlockSpec(memory_space=pltpu.VMEM)
+    return pl.pallas_call(
+        spread_kernel,
+        out_shape=jax.ShapeDtypeStruct((OWNERS // NX, PART, E), jnp.float32),
+        in_specs=[whole],
+        out_specs=whole,
+        compiler_params=pltpu.CompilerParams(vmem_limit_bytes=VMEM_LIMIT),
+        cost_estimate=pl.CostEstimate(flops=33792, bytes_accessed=1_500_000, transcendentals=0),
+        name="spread_sum",
+    )(near)
+
+
+def final_kernel(g_ref, parts_ref, w1_ref, b1_ref, w2_ref, b2_ref, w3_ref):
+    total = parts_ref[0]
+    for z in range(1, OWNERS // NX):
+        total += parts_ref[z]
+    g = g_ref[0]
+    w1_ref[:, :E] = total[:32]
+    w1_ref[:, E:] = total[32:64]
+    w2_ref[...] = total[64:80]
+    small = total[80:88]
+    by16 = pltpu.roll(small, (128 - (g % 8) * 16) % 128, 1)
+    by8 = pltpu.roll(small, (128 - g * 8) % 128, 1)
+    b1_ref[...] = jnp.where(g < 8, by16[0:1, :16], by16[1:2, :16])
+    b2_ref[...] = by8[2:3, :8]
+    w3_ref[...] = by8[3:4, :8]
+
+
+def final(g, parts):
+    whole = pl.BlockSpec(memory_space=pltpu.VMEM)
+    shapes = ((32, 2 * E), (1, 16), (16, E), (1, 8), (1, 8))
+    return pl.pallas_call(
+        final_kernel,
+        out_shape=[jax.ShapeDtypeStruct(shape, jnp.float32) for shape in shapes],
+        in_specs=[pl.BlockSpec(memory_space=pltpu.SMEM), whole],
+        out_specs=[whole] * 5,
+        compiler_params=pltpu.CompilerParams(vmem_limit_bytes=VMEM_LIMIT),
+        cost_estimate=pl.CostEstimate(flops=135168, bytes_accessed=600_000, transcendentals=0),
+        name="final",
+    )(g, parts)
 
 
 def shards(
@@ -254,22 +353,44 @@
 ):
     g = lax.axis_index("grp")
     me = lax.axis_index("shard").reshape(1)
-    drow, grads = local_terms(
-        target, history, lengths, pooled_gradient, attn_w1, attn_b1, attn_w2, attn_b2, attn_w3
+    drow, part = dense(
+        lengths,
+        target,
+        history.reshape(SLOTS, E),
+        pooled_gradient,
+        attn_w1,
+        attn_b1.reshape(1, 2 * E),
+        attn_w2,
+        attn_b2.reshape(1, E),
+        attn_w3.reshape(1, E),
     )
     send = pack(me, block_counts, drow, hist_ids, block_rows[0])
     got = lax.all_to_all(send, "shard", split_axis=0, concat_axis=0, tiled=True)
-    slab = got[:, HALF:, :].reshape(OWNERS * 8, E)
-    late = [lax.ppermute(slab, "shard", x_turn(step)) for step in (1, 2, 3)]
-    table = add_rows(me, block_counts, got.reshape(OWNERS * BLOCK, E), late)
-    share = sum_grads(grads, g)
+    got = got.reshape(OWNERS * BLOCK, E)
+
+    part = part.reshape(2, 2, 2, 2, PART, E)
+    y2 = (g >> 3) & 1
+    bits = (g & 1, ((g >> 1) & 1) ^ y2, ((g >> 2) & 1) ^ y2, y2)
+    for bit, swap in zip(bits, SWAPS):
+        keep = lax.dynamic_index_in_dim(part, bit, 0, False)
+        send = lax.dynamic_index_in_dim(part, 1 - bit, 0, False)
+        there = lax.ppermute(send, "grp", grp_swap(swap))
+        part = join(keep, there, got) if swap == SWAPS[-1] else keep + there
+    near = lax.all_to_all(
+        part, "shard", split_axis=0, concat_axis=0, tiled=True, axis_index_groups=X_GROUPS
+    ).reshape(NX * NEAR, E)
+    parts = lax.all_to_all(
+        spread_sum(near), "shard", split_axis=0, concat_axis=0, tiled=True, axis_index_groups=Z_GROUPS
+    )
+    table = add_rows(me, block_counts, got, near)
+    grad_w1, grad_b1, grad_w2, grad_b2, grad_w3 = final(g.reshape(1), parts)
     return (
         table[None],
-        jnp.concatenate([share[:32], share[32:64]], axis=1),
-        share[80, :16],
-        share[64:80],
-        share[80, 16:24],
-        share[80, 24:32],
+        grad_w1,
+        grad_b1.reshape(16),
+        grad_w2,
+        grad_b2.reshape(8),
+        grad_w3.reshape(8),
     )
 
 

time: 128 us -> 108 us (0.84)
  starting transfers between devices: 70.5 us -> 39.1 us
  blocking collectives: 0 us -> 14.5 us
  other arithmetic: 5.85 us -> 0.08 us
  Pallas kernels: 6.47 us -> 11.4 us
  matrix products: 2.84 us -> 0 us
    ppermute x13 -> x4, starting transfers between devices: 52.2 us -> 14.6 us  [shards(): there = lax.ppermute(send, 'grp', grp_swap(swap))]
    ppermute x13 -> x4, waiting for transfers between devices: 36.4 us -> 14 us  [shards(): there = lax.ppermute(send, 'grp', grp_swap(swap))]
    all_to_all x0 -> x1, waiting for transfers between devices: none -> 18.7 us  [shards(): lax.all_to_all(spread_sum(near), 'shard', split_axis=0, concat_axis=0, ti...]
    all_to_all x0 -> x1, blocking collectives: none -> 14.5 us  [shards(): lax.all_to_all(part, 'shard', split_axis=0, concat_axis=0, tiled=True, ax...]
    all_to_all x0 -> x1, starting transfers between devices: none -> 6.23 us  [shards(): lax.all_to_all(spread_sum(near), 'shard', split_axis=0, concat_axis=0, ti...]
    pallas_call x0 -> x4, Pallas kernels: none -> 4.92 us  [the longest x1 3.32 us: dense(): pl.pallas_call(dense_kernel, out_shape=[jax.ShapeDtypeStruct((SLOTS, E),...]
    all_to_all x1, waiting for transfers between devices: 0.01 us -> 4.89 us  [shards(): got = lax.all_to_all(send, 'shard', split_axis=0, concat_axis=0, tiled=True)]
    unnamed x24, local copies, waits for them, and re-layouts: 1.23 us -> 4.11 us
  transfers between devices with their start and end apart: 14 -> 6, of which waited for: 11 -> 6; matrix products, arithmetic and copies ran while one was open for 3% -> 0% of each run, Pallas kernels for 2% -> 3%
where the time goes in v2:
time: 108 us
  starting transfers between devices  39.1 us (36%)
  waiting for transfers between devices  37.6 us (35%)
  blocking collectives  14.5 us (13%)
  Pallas kernels  11.4 us (11%)
  local copies, waits for them, and re-layouts  4.19 us (4%)
    all_to_all x1, waiting for transfers between devices, shards(): lax.all_to_all(spread_sum(near), 'shard', split_axis=0, concat_axis=0, ti...  18.7 us
    all_to_all x1, starting transfers between devices, shards(): got = lax.all_to_all(send, 'shard', split_axis=0, concat_axis=0, tiled=True)  18.3 us
    ppermute x4, starting transfers between devices, shards(): there = lax.ppermute(send, 'grp', grp_swap(swap))  14.6 us
    all_to_all x1, blocking collectives, shards(): lax.all_to_all(part, 'shard', split_axis=0, concat_axis=0, tiled=True, ax...  14.5 us
    ppermute x4, waiting for transfers between devices, shards(): there = lax.ppermute(send, 'grp', grp_swap(swap))  14 us
    all_to_all x1, starting transfers between devices, shards(): lax.all_to_all(spread_sum(near), 'shard', split_axis=0, concat_axis=0, ti...  6.23 us
    all_to_all x1, waiting for transfers between devices, shards(): got = lax.all_to_all(send, 'shard', split_axis=0, concat_axis=0, tiled=True)  4.89 us
    unnamed x24, local copies, waits for them, and re-layouts  4.11 us
  transfers between devices with their start and end apart: 6, of which 6 were waited for; matrix products, arithmetic and copies ran while one was open for 0% of the time, Pallas kernels for 3%

profile of v2, /device:TPU:8, one launch (start us, length us, event | category | flops | bytes accessed | tf_op | source)
XLA Modules:
  0.0 107.8 jit_solution(12703352905776188512)
XLA Ops:
  0.6 0.0 copy-start.9
  0.7 0.0 copy-start.10
  0.7 0.6 copy-done.9
  1.3 0.0 copy-done.10
  1.3 0.0 copy-done.4
  1.4 0.0 copy-done.6
  1.4 0.0 copy-done.7
  1.4 0.0 copy-done.8
  1.4 0.9 copy-done
  2.3 0.9 copy-done.1
  3.3 0.8 copy-done.2
  4.1 3.3 %dense.1 = (f32[1024,128]{1,0:T(8,128)S(1)}, f32[1408,128]{1,0:T(8,128)S(1)}) custom-call(s32[8]{0:T(128)S(1)} %copy-done.8, bf16[8,128]{1,0:T(8,128)(2,1)S(1)} %copy-done.6, bf16[1024,128]{1,0:T(8,128)(2,1)S(1)} %bitcast.36, f32[8,128]{1,0:T(8,128)S(1)} %copy-done.4, bf16[512,256]{1,0:T(8,128)(2,1)S(1)} %copy-done.1, f32[1,256]{1,0:T(1,128)S(1)} %bitcast.38, ...), custom_call_target="tpu_custom_call" | custom-call | flops 1100000000 | bytes 2200000 | tf_op jit(solution)/shard_map/dense/pallas_call | solution.py:110
  7.5 0.0 copy-start.11
  7.5 0.7 copy-done.5
  8.1 3.1 %pack.1 = f32[48,32,128]{2,1,0:T(8,128)} custom-call(s32[1]{0:T(128)} %bitcast.me_ref, s32[1,48]{1,0:T(1,128)S(1)} %copy-done.11, f32[1024,128]{1,0:T(8,128)S(1)} %get-tuple-element.13.drow_ref, s32[8,128]{1,0:T(8,128)S(1)} %copy-done.5, s32[48,48]{1,0:T(8,128)S(1)} %bitcast.37), custom_call_target="tpu_custom_call" | custom-call | flops 1241513984 | bytes 2000000 | tf_op jit(solution)/shard_map/pack/pallas_call | solution.py:184
  11.3 18.3 %all-to-all-start = ((f32[48,32,128]{2,1,0:T(8,128)}), f32[48,32,128]{2,1,0:T(8,128)S(1)}, u32[]{:S(2)}, u32[]{:S(2)}) async-start(f32[48,32,128]{2,1,0:T(8,128)} %pack.1), calls=%async_computation | async-start | bytes 1572864 | tf_op jit(solution)/shard_map/all_to_all | solution.py:368
  29.6 1.9 %collective-permute-start = (f32[2,2,2,88,128]{4,3,2,1,0:T(8,128)S(1)}, f32[2,2,2,88,128]{4,3,2,1,0:T(8,128)S(1)}, u32[]{:S(2)}, u32[]{:S(2)}) collective-permute-start(f32[2,2,2,88,128]{4,3,2,1,0:T(8,128)S(1)} %dynamic-slice_bitcast_fusion), channel_id=1, source_target_pairs={{0,48},{48,0},{96,144},{144,96},{192,240},{240,192},{288,336},{336... | collective-permute-start | bytes 1081352 | tf_op jit(solution)/shard_map/ppermute | solution.py:377
  31.6 1.6 %collective-permute-done = f32[2,2,2,88,128]{4,3,2,1,0:T(8,128)S(1)} collective-permute-done((f32[2,2,2,88,128]{4,3,2,1,0:T(8,128)S(1)}, f32[2,2,2,88,128]{4,3,2,1,0:T(8,128)S(1)}, u32[]{:S(2)}, u32[]{:S(2)}) %collective-permute-start) | collective-permute-done | bytes 360480 | tf_op jit(solution)/shard_map/ppermute | solution.py:377
  33.3 2.4 %collective-permute-start.1 = (f32[2,2,88,128]{3,2,1,0:T(8,128)S(1)}, f32[2,2,88,128]{3,2,1,0:T(8,128)S(1)}, u32[]{:S(2)}, u32[]{:S(2)}) collective-permute-start(f32[2,2,88,128]{3,2,1,0:T(8,128)S(1)} %dynamic-slice_bitcast_fusion.1), channel_id=1, source_target_pairs={{0,96},{48,144},{96,0},{144,48},{192,288},{240,336},{288,192},{336... | collective-permute-start | bytes 540680 | tf_op jit(solution)/shard_map/ppermute | solution.py:377
  35.7 6.1 %collective-permute-done.1 = f32[2,2,88,128]{3,2,1,0:T(8,128)S(1)} collective-permute-done((f32[2,2,88,128]{3,2,1,0:T(8,128)S(1)}, f32[2,2,88,128]{3,2,1,0:T(8,128)S(1)}, u32[]{:S(2)}, u32[]{:S(2)}) %collective-permute-start.1) | collective-permute-done | bytes 180256 | tf_op jit(solution)/shard_map/ppermute | solution.py:377
  41.8 4.5 %collective-permute-start.2 = (f32[2,88,128]{2,1,0:T(8,128)S(1)}, f32[2,88,128]{2,1,0:T(8,128)S(1)}, u32[]{:S(2)}, u32[]{:S(2)}) collective-permute-start(f32[2,88,128]{2,1,0:T(8,128)S(1)} %dynamic-slice_bitcast_fusion.2), channel_id=1, source_target_pairs={{0,192},{48,240},{96,288},{144,336},{192,0},{240,48},{288,96},{336... | collective-permute-start | bytes 270344 | tf_op jit(solution)/shard_map/ppermute | solution.py:377
  46.3 3.1 %collective-permute-done.2 = f32[2,88,128]{2,1,0:T(8,128)S(1)} collective-permute-done((f32[2,88,128]{2,1,0:T(8,128)S(1)}, f32[2,88,128]{2,1,0:T(8,128)S(1)}, u32[]{:S(2)}, u32[]{:S(2)}) %collective-permute-start.2) | collective-permute-done | bytes 90144 | tf_op jit(solution)/shard_map/ppermute | solution.py:377
  49.5 5.8 %collective-permute-start.3 = (f32[88,128]{1,0:T(8,128)S(1)}, f32[88,128]{1,0:T(8,128)S(1)}, u32[]{:S(2)}, u32[]{:S(2)}) collective-permute-start(f32[88,128]{1,0:T(8,128)S(1)} %get-tuple-element.20), channel_id=1, source_target_pairs={{0,672},{48,720},{96,576},{144,624},{192,480},{240,528},{288,384},... | collective-permute-start | bytes 135176 | tf_op jit(solution)/shard_map/ppermute | solution.py:377
  55.3 3.1 %collective-permute-done.3.there_ref = f32[88,128]{1,0:T(8,128)S(1)} collective-permute-done((f32[88,128]{1,0:T(8,128)S(1)}, f32[88,128]{1,0:T(8,128)S(1)}, u32[]{:S(2)}, u32[]{:S(2)}) %collective-permute-start.3) | collective-permute-done | bytes 45088 | tf_op jit(solution)/shard_map/ppermute | solution.py:377
  58.5 4.9 %all-to-all-done = f32[48,32,128]{2,1,0:T(8,128)S(1)} async-done(((f32[48,32,128]{2,1,0:T(8,128)}), f32[48,32,128]{2,1,0:T(8,128)S(1)}, u32[]{:S(2)}, u32[]{:S(2)}) %all-to-all-start) | async-done | bytes 786464 | tf_op jit(solution)/shard_map/all_to_all | solution.py:368
  63.4 0.1 join.1
  63.4 14.5 %all_to_all.15 = f32[4,472,128]{2,1,0:T(8,128)S(1)} all-to-all(f32[4,472,128]{2,1,0:T(8,128)S(1)} %join.1), channel_id=1, replica_groups={{0,1,2,3},{4,5,6,7},{8,9,10,11},{12,13,14,15},{16,17,18,19},{20,21,22,2..., dimensions={0} | all-to-all | bytes 1933312 | tf_op jit(solution)/shard_map/all_to_all | solution.py:379
  77.9 0.8 spread_sum.1
  78.8 6.2 %all-to-all-start.2 = ((f32[12,88,128]{2,1,0:T(8,128)}), f32[12,88,128]{2,1,0:T(8,128)S(1)}, u32[]{:S(2)}, u32[]{:S(2)}) async-start(f32[12,88,128]{2,1,0:T(8,128)} %spread_sum.1), calls=%async_computation.2 | async-start | bytes 1081344 | tf_op jit(solution)/shard_map/all_to_all | solution.py:382
  85.0 3.3 %add_rows.1 = f32[2048,128]{1,0:T(8,128)} custom-call(s32[1]{0:T(128)} %bitcast.me_ref, s32[1,48]{1,0:T(1,128)S(1)} %copy-done.11, f32[1536,128]{1,0:T(8,128)S(1)} %bitcast.33, f32[1888,128]{1,0:T(8,128)S(1)} %bitcast.31), custom_call_target="tpu_custom_call" | custom-call | flops 1610612736 | bytes 2500000 | tf_op jit(solution)/shard_map/add_rows/pallas_call | solution.py:240
  88.3 18.7 %all-to-all-done.2.parts_ref = f32[12,88,128]{2,1,0:T(8,128)S(1)} async-done(((f32[12,88,128]{2,1,0:T(8,128)}), f32[12,88,128]{2,1,0:T(8,128)S(1)}, u32[]{:S(2)}, u32[]{:S(2)}) %all-to-all-start.2) | async-done | bytes 540704 | tf_op jit(solution)/shard_map/all_to_all | solution.py:382
  107.1 0.7 final.1
  (18 shorter events, 0.2 us)
Async XLA Ops:
  0.6 0.7 copy-start.9
  0.7 0.7 copy-start.10
  0.7 0.7 copy-start.4
  0.7 0.7 copy-start.6
  0.7 0.7 copy-start.7
  0.7 0.7 copy-start.8
  1.4 1.0 copy-start
  2.3 0.9 copy-start.1
  3.3 0.8 copy-start.2
  4.1 3.3 %copy-start.3 = (s32[1,48,48]{2,1,0:T(8,128)S(1)}, s32[1,48,48]{2,1,0:T(8,128)}, u32[]{:S(2)}) copy-start(s32[1,48,48]{2,1,0:T(8,128)} %param.16) | copy-start | bytes 27652
  7.5 0.7 copy-start.5
  7.5 0.7 copy-start.11
  11.3 52.1 %all-to-all-start = ((f32[48,32,128]{2,1,0:T(8,128)}), f32[48,32,128]{2,1,0:T(8,128)S(1)}, u32[]{:S(2)}, u32[]{:S(2)}) async-start(f32[48,32,128]{2,1,0:T(8,128)} %pack.1), calls=%async_computation | async-start | bytes 1572864 | tf_op jit(solution)/shard_map/all_to_all | solution.py:368
  29.6 3.6 %collective-permute-start = (f32[2,2,2,88,128]{4,3,2,1,0:T(8,128)S(1)}, f32[2,2,2,88,128]{4,3,2,1,0:T(8,128)S(1)}, u32[]{:S(2)}, u32[]{:S(2)}) collective-permute-start(f32[2,2,2,88,128]{4,3,2,1,0:T(8,128)S(1)} %dynamic-slice_bitcast_fusion), channel_id=1, source_target_pairs={{0,48},{48,0},{96,144},{144,96},{192,240},{240,192},{288,336},{336... | collective-permute-start | bytes 1081352 | tf_op jit(solution)/shard_map/ppermute | solution.py:377
  33.3 8.5 %collective-permute-start.1 = (f32[2,2,88,128]{3,2,1,0:T(8,128)S(1)}, f32[2,2,88,128]{3,2,1,0:T(8,128)S(1)}, u32[]{:S(2)}, u32[]{:S(2)}) collective-permute-start(f32[2,2,88,128]{3,2,1,0:T(8,128)S(1)} %dynamic-slice_bitcast_fusion.1), channel_id=1, source_target_pairs={{0,96},{48,144},{96,0},{144,48},{192,288},{240,336},{288,192},{336... | collective-permute-start | bytes 540680 | tf_op jit(solution)/shard_map/ppermute | solution.py:377
  41.8 7.7 %collective-permute-start.2 = (f32[2,88,128]{2,1,0:T(8,128)S(1)}, f32[2,88,128]{2,1,0:T(8,128)S(1)}, u32[]{:S(2)}, u32[]{:S(2)}) collective-permute-start(f32[2,88,128]{2,1,0:T(8,128)S(1)} %dynamic-slice_bitcast_fusion.2), channel_id=1, source_target_pairs={{0,192},{48,240},{96,288},{144,336},{192,0},{240,48},{288,96},{336... | collective-permute-start | bytes 270344 | tf_op jit(solution)/shard_map/ppermute | solution.py:377
  49.5 8.9 %collective-permute-start.3 = (f32[88,128]{1,0:T(8,128)S(1)}, f32[88,128]{1,0:T(8,128)S(1)}, u32[]{:S(2)}, u32[]{:S(2)}) collective-permute-start(f32[88,128]{1,0:T(8,128)S(1)} %get-tuple-element.20), channel_id=1, source_target_pairs={{0,672},{48,720},{96,576},{144,624},{192,480},{240,528},{288,384},... | collective-permute-start | bytes 135176 | tf_op jit(solution)/shard_map/ppermute | solution.py:377
  78.8 28.3 %all-to-all-start.2 = ((f32[12,88,128]{2,1,0:T(8,128)}), f32[12,88,128]{2,1,0:T(8,128)S(1)}, u32[]{:S(2)}, u32[]{:S(2)}) async-start(f32[12,88,128]{2,1,0:T(8,128)} %spread_sum.1), calls=%async_computation.2 | async-start | bytes 1081344 | tf_op jit(solution)/shard_map/all_to_all | solution.py:382

commit v3 on v2

--- a/solution.py
+++ b/solution.py
@@ -27,7 +27,8 @@
 
 
 CHUNK = 256
-PART = 88
+QUARTER = 24
+PART = NX * QUARTER
 
 
 def sigmoid(z):
@@ -38,14 +39,23 @@
     at = []
     for g in range(16):
         core, y0, y1, y2 = g & 1, (g >> 1) & 1, (g >> 2) & 1, (g >> 3) & 1
-        at.append(core * 8 + (y0 ^ y2) * 4 + (y1 ^ y2) * 2 + y2)
+        at.append((y0 ^ y2) * 8 + core * 4 + (y1 ^ y2) * 2 + y2)
     return at
 
 
 def dense_kernel(
-    lengths_ref, target_ref, hist_ref, pg_ref, w1_ref, b1_ref, w2_ref, b2_ref, w3_ref,
-    drow_ref, part_ref, feats, act1s, dz2s, dz1s,
+    lengths_ref, target_in, hist_in, pg_in, w1_in, b1_in, w2_in, b2_in, w3_in,
+    drow_ref, part_ref,
+    target_ref, hist_ref, pg_ref, w1_ref, b1_ref, w2_ref, b2_ref, w3_ref,
+    feats, act1s, dz2s, dz1s, sems,
 ):
+    inputs = (hist_in, w1_in, target_in, b1_in, w2_in, b2_in, w3_in, pg_in)
+    held = (hist_ref, w1_ref, target_ref, b1_ref, w2_ref, b2_ref, w3_ref, pg_ref)
+    copies = [pltpu.make_async_copy(a, b, sems.at[k]) for k, (a, b) in enumerate(zip(inputs, held))]
+    for copy in copies:
+        copy.start()
+    for copy in copies:
+        copy.wait()
     query = target_ref[...].astype(jnp.float32)
     w1, w2, w3 = w1_ref[...], w2_ref[...], w3_ref[...]
     grad_w3 = jnp.zeros((1, E), jnp.float32)
@@ -97,11 +107,16 @@
     small = jnp.where(sub == 0, grad_b1[:, :E], jnp.where(sub == 1, grad_b1[:, E:], 0.0))
     small = jnp.where(sub == 2, grad_b2, jnp.where(sub == 3, grad_w3, small))
     for g, at in enumerate(places()):
-        base = at * PART
-        part_ref[base : base + 32, :] = grad_w1[32 * g : 32 * g + 32, :E]
-        part_ref[base + 32 : base + 64, :] = grad_w1[32 * g : 32 * g + 32, E:]
-        part_ref[base + 64 : base + 80, :] = grad_w2[16 * g : 16 * g + 16, :]
-        part_ref[base + 80 : base + 88, :] = small
+        for k in range(NX):
+            base = at * PART + k * QUARTER
+            top = 32 * g + 16 * (k % 2)
+            side = E * (k // 2)
+            part_ref[base : base + 16, :] = grad_w1[top : top + 16, side : side + E]
+            if k < 2:
+                last = grad_w2[16 * g + 8 * k : 16 * g + 8 * k + 8, :]
+            else:
+                last = small
+            part_ref[base + 16 : base + 24, :] = last
 
 
 def dense(lengths, target, hist, pg, w1, b1, w2, b2, w3):
@@ -113,13 +128,15 @@
             jax.ShapeDtypeStruct((SLOTS, E), jnp.float32),
             jax.ShapeDtypeStruct((16 * PART, E), jnp.float32),
         ],
-        in_specs=[scalar] + [whole] * 8,
+        in_specs=[scalar] + [pl.BlockSpec(memory_space=pltpu.HBM)] * 8,
         out_specs=[whole, whole],
-        scratch_shapes=[
+        scratch_shapes=[pltpu.VMEM(v.shape, v.dtype) for v in (target, hist, pg, w1, b1, w2, b2, w3)]
+        + [
             pltpu.VMEM((SLOTS, 4 * E), jnp.bfloat16),
             pltpu.VMEM((SLOTS, 2 * E), jnp.bfloat16),
             pltpu.VMEM((SLOTS, E), jnp.bfloat16),
             pltpu.VMEM((SLOTS, 2 * E), jnp.bfloat16),
+            pltpu.SemaphoreType.DMA((8,)),
         ],
         compiler_params=pltpu.CompilerParams(vmem_limit_bytes=VMEM_LIMIT),
         cost_estimate=pl.CostEstimate(
@@ -129,13 +146,23 @@
     )(lengths, target, hist, pg, w1, b1, w2, b2, w3)
 
 
-def pack_kernel(me_ref, counts_ref, drow_ref, ids_ref, blocks_ref, send_ref, pick, source):
+def pack_kernel(
+    me_ref, counts_ref, drow_ref, ids_in, blocks_in, send_ref, ids_ref, blocks_ref, pick, source, sems
+):
+    copies = [
+        pltpu.make_async_copy(ids_in, ids_ref, sems.at[0]),
+        pltpu.make_async_copy(blocks_in, blocks_ref, sems.at[1]),
+    ]
+    for copy in copies:
+        copy.start()
     me = me_ref[0]
     hot = jnp.int32(0)
     for o in range(OWNERS):
         hot = jnp.where(counts_ref[0, o] > HALF, jnp.int32(o), hot)
 
     source[:, : 2 * E] = split(drow_ref[...])
+    for copy in copies:
+        copy.wait()
     ids = ids_ref[...] & (ROWS_DEV - 1)
     id_columns = jnp.transpose(ids.astype(jnp.float32))
     for b in range(8):
@@ -184,11 +211,14 @@
     return pl.pallas_call(
         pack_kernel,
         out_shape=jax.ShapeDtypeStruct((OWNERS, BLOCK, E), jnp.float32),
-        in_specs=[scalar, scalar, whole, whole, whole],
+        in_specs=[scalar, scalar, whole] + [pl.BlockSpec(memory_space=pltpu.HBM)] * 2,
         out_specs=whole,
         scratch_shapes=[
+            pltpu.VMEM(ids.shape, ids.dtype),
+            pltpu.VMEM(blocks.shape, blocks.dtype),
             pltpu.VMEM((OWNERS * HALF + 32, SLOTS), jnp.bfloat16),
             pltpu.VMEM((SLOTS, 4 * E), jnp.bfloat16),
+            pltpu.SemaphoreType.DMA((2,)),
         ],
         compiler_params=pltpu.CompilerParams(vmem_limit_bytes=VMEM_LIMIT),
         cost_estimate=pl.CostEstimate(
@@ -199,10 +229,9 @@
 
 
 STEP = 512
-NEAR = PART + OWNERS * 8
-
-
-def add_kernel(me_ref, counts_ref, got_ref, near_ref, table_ref, rows, dest):
+
+
+def add_kernel(me_ref, counts_ref, got_ref, own_ref, late0_ref, late1_ref, late2_ref, table_ref, rows, dest):
     groups = OWNERS // NX
     for g in range(groups):
         rows[g * 128 : (g + 1) * 128, :] = split(got_ref[g * 128 : (g + 1) * 128, :])
@@ -225,8 +254,8 @@
     def _():
         for k in range(NX):
             for g in range(3):
-                base = k * NEAR + PART
-                tiles = [near_ref[base + t * 8 : base + t * 8 + 8, :] for t in range(16 * g, 16 * g + 16)]
+                late = (own_ref, late0_ref, late1_ref, late2_ref)[k]
+                tiles = [late[t * 8 : t * 8 + 8, :] for t in range(16 * g, 16 * g + 16)]
                 at = (k * 3 + g) * 128
                 rows[at : at + 128, :] = split(jnp.concatenate(tiles, axis=0))
                 dest[:, at : at + 128] = jnp.broadcast_to(sum(tiles)[7:8, :], (8, E))
@@ -234,13 +263,13 @@
             table_ref[t * STEP : (t + 1) * STEP, :] += product(t)
 
 
-def add_rows(me, counts, got, near):
+def add_rows(me, counts, got, late):
     whole = pl.BlockSpec(memory_space=pltpu.VMEM)
     scalar = pl.BlockSpec(memory_space=pltpu.SMEM)
     return pl.pallas_call(
         add_kernel,
         out_shape=jax.ShapeDtypeStruct((ROWS_DEV, E), jnp.float32),
-        in_specs=[scalar, scalar, whole, whole],
+        in_specs=[scalar, scalar] + [whole] * 5,
         out_specs=whole,
         scratch_shapes=[
             pltpu.VMEM((OWNERS * BLOCK, 2 * E), jnp.bfloat16),
@@ -251,71 +280,78 @@
             flops=2 * 2048 * 1536 * 256, bytes_accessed=2_500_000, transcendentals=0
         ),
         name="add_rows",
-    )(me, counts, got, near)
-
-
-SWAPS = (1, 2, 4, 14)
-
-
-def grp_swap(bits):
-    return [(g, g ^ bits) for g in range(16)]
-
-
-X_GROUPS = [[z * NX + x for x in range(NX)] for z in range(OWNERS // NX)]
-Z_GROUPS = [[z * NX + x for z in range(OWNERS // NX)] for x in range(NX)]
-
-
-def join_kernel(keep_ref, there_ref, got_ref, near_ref):
+    )(me, counts, got, *late)
+
+
+GRP_SWAPS = (2, 1, 4, 14)
+X_SWAPS = (1, 3)
+NZ = OWNERS // NX
+X_GROUPS = [[z * NX + x for x in range(NX)] for z in range(NZ)]
+Z_GROUPS = [[z * NX + x for z in range(NZ)] for x in range(NX)]
+
+
+def swap(value, axis, bits):
+    size = lax.axis_size(axis)
+    return lax.ppermute(value, axis, [(i, i ^ bits) for i in range(size)])
+
+
+def join_kernel(keep_ref, there_ref, got_ref, copies_ref, slab_ref):
     part = keep_ref[...] + there_ref[...]
-    for x in range(NX):
-        near_ref[x, :PART, :] = part
-        for s in range(OWNERS):
-            near_ref[x, PART + s * 8 : PART + s * 8 + 8, :] = got_ref[s * BLOCK + HALF : (s + 1) * BLOCK, :]
+    for z in range(NZ):
+        copies_ref[z] = part
+    for s in range(OWNERS):
+        slab_ref[s * 8 : s * 8 + 8, :] = got_ref[s * BLOCK + HALF : (s + 1) * BLOCK, :]
 
 
 def join(keep, there, got):
     whole = pl.BlockSpec(memory_space=pltpu.VMEM)
     return pl.pallas_call(
         join_kernel,
-        out_shape=jax.ShapeDtypeStruct((NX, NEAR, E), jnp.float32),
+        out_shape=[
+            jax.ShapeDtypeStruct((NZ, QUARTER, E), jnp.float32),
+            jax.ShapeDtypeStruct((OWNERS * 8, E), jnp.float32),
+        ],
         in_specs=[whole, whole, whole],
-        out_specs=whole,
-        compiler_params=pltpu.CompilerParams(vmem_limit_bytes=VMEM_LIMIT),
-        cost_estimate=pl.CostEstimate(flops=11264, bytes_accessed=2_000_000, transcendentals=0),
+        out_specs=[whole, whole],
+        compiler_params=pltpu.CompilerParams(vmem_limit_bytes=VMEM_LIMIT),
+        cost_estimate=pl.CostEstimate(flops=3072, bytes_accessed=1_300_000, transcendentals=0),
         name="join",
     )(keep, there, got)
 
 
-def spread_kernel(near_ref, out_ref):
-    part = near_ref[:PART, :]
-    for x in range(1, NX):
-        part += near_ref[x * NEAR : x * NEAR + PART, :]
-    for z in range(OWNERS // NX):
-        out_ref[z] = part
-
-
-def spread_sum(near):
+def spread_kernel(parts_ref, out_ref):
+    part = parts_ref[0]
+    for z in range(1, NZ):
+        part += parts_ref[z]
+    for x in range(NX):
+        out_ref[x] = part
+
+
+def spread_sum(parts):
     whole = pl.BlockSpec(memory_space=pltpu.VMEM)
     return pl.pallas_call(
         spread_kernel,
-        out_shape=jax.ShapeDtypeStruct((OWNERS // NX, PART, E), jnp.float32),
+        out_shape=jax.ShapeDtypeStruct((NX, QUARTER, E), jnp.float32),
         in_specs=[whole],
         out_specs=whole,
         compiler_params=pltpu.CompilerParams(vmem_limit_bytes=VMEM_LIMIT),
-        cost_estimate=pl.CostEstimate(flops=33792, bytes_accessed=1_500_000, transcendentals=0),
+        cost_estimate=pl.CostEstimate(flops=33792, bytes_accessed=200_000, transcendentals=0),
         name="spread_sum",
-    )(near)
-
-
-def final_kernel(g_ref, parts_ref, w1_ref, b1_ref, w2_ref, b2_ref, w3_ref):
-    total = parts_ref[0]
-    for z in range(1, OWNERS // NX):
-        total += parts_ref[z]
+    )(parts)
+
+
+HOLDER = (0, 3, 1, 2)
+
+
+def final_kernel(g_ref, total_ref, w1_ref, b1_ref, w2_ref, b2_ref, w3_ref):
+    quarters = [total_ref[x] for x in HOLDER]
+    for k in range(NX):
+        top, side = 16 * (k % 2), E * (k // 2)
+        w1_ref[top : top + 16, side : side + E] = quarters[k][:16]
+    w2_ref[:8, :] = quarters[0][16:]
+    w2_ref[8:, :] = quarters[1][16:]
     g = g_ref[0]
-    w1_ref[:, :E] = total[:32]
-    w1_ref[:, E:] = total[32:64]
-    w2_ref[...] = total[64:80]
-    small = total[80:88]
+    small = quarters[2][16:]
     by16 = pltpu.roll(small, (128 - (g % 8) * 16) % 128, 1)
     by8 = pltpu.roll(small, (128 - g * 8) % 128, 1)
     b1_ref[...] = jnp.where(g < 8, by16[0:1, :16], by16[1:2, :16])
@@ -323,7 +359,7 @@
     w3_ref[...] = by8[3:4, :8]
 
 
-def final(g, parts):
+def final(g, total):
     whole = pl.BlockSpec(memory_space=pltpu.VMEM)
     shapes = ((32, 2 * E), (1, 16), (16, E), (1, 8), (1, 8))
     return pl.pallas_call(
@@ -332,9 +368,9 @@
         in_specs=[pl.BlockSpec(memory_space=pltpu.SMEM), whole],
         out_specs=[whole] * 5,
         compiler_params=pltpu.CompilerParams(vmem_limit_bytes=VMEM_LIMIT),
-        cost_estimate=pl.CostEstimate(flops=135168, bytes_accessed=600_000, transcendentals=0),
+        cost_estimate=pl.CostEstimate(flops=1024, bytes_accessed=100_000, transcendentals=0),
         name="final",
-    )(g, parts)
+    )(g, total)
 
 
 def shards(
@@ -368,22 +404,29 @@
     got = lax.all_to_all(send, "shard", split_axis=0, concat_axis=0, tiled=True)
     got = got.reshape(OWNERS * BLOCK, E)
 
-    part = part.reshape(2, 2, 2, 2, PART, E)
+    part = part.reshape(2, 2, 2, 2, 2, 2, QUARTER, E)
     y2 = (g >> 3) & 1
-    bits = (g & 1, ((g >> 1) & 1) ^ y2, ((g >> 2) & 1) ^ y2, y2)
-    for bit, swap in zip(bits, SWAPS):
+    x1 = (me[0] >> 1) & 1
+    bits = (((g >> 1) & 1) ^ y2, g & 1, ((g >> 2) & 1) ^ y2, y2, (me[0] & 1) ^ x1, x1)
+    steps = [("grp", k) for k in GRP_SWAPS] + [("shard", k) for k in X_SWAPS]
+    for bit, (axis, k) in zip(bits, steps):
         keep = lax.dynamic_index_in_dim(part, bit, 0, False)
-        send = lax.dynamic_index_in_dim(part, 1 - bit, 0, False)
-        there = lax.ppermute(send, "grp", grp_swap(swap))
-        part = join(keep, there, got) if swap == SWAPS[-1] else keep + there
-    near = lax.all_to_all(
-        part, "shard", split_axis=0, concat_axis=0, tiled=True, axis_index_groups=X_GROUPS
-    ).reshape(NX * NEAR, E)
+        away = lax.dynamic_index_in_dim(part, 1 - bit, 0, False)
+        there = swap(away, axis, k)
+        part = keep + there
+    copies, slab = join(keep, there, got)
     parts = lax.all_to_all(
-        spread_sum(near), "shard", split_axis=0, concat_axis=0, tiled=True, axis_index_groups=Z_GROUPS
-    )
-    table = add_rows(me, block_counts, got, near)
-    grad_w1, grad_b1, grad_w2, grad_b2, grad_w3 = final(g.reshape(1), parts)
+        copies, "shard", split_axis=0, concat_axis=0, tiled=True, axis_index_groups=Z_GROUPS
+    )
+    total = lax.all_to_all(
+        spread_sum(parts), "shard", split_axis=0, concat_axis=0, tiled=True, axis_index_groups=X_GROUPS
+    )
+    late = [slab]
+    for turn in (1, 2, 3):
+        pairs = [(s, s // NX * NX + (s + turn) % NX) for s in range(OWNERS)]
+        late.append(lax.ppermute(slab, "shard", pairs))
+    table = add_rows(me, block_counts, got, late)
+    grad_w1, grad_b1, grad_w2, grad_b2, grad_w3 = final(g.reshape(1), total)
     return (
         table[None],
         grad_w1,

time: 108 us -> 101 us (0.935)
  the two profiles are of different devices: /device:TPU:8 before, /device:TPU:2 now
where the time goes in v3:
time: 101 us; the launch traced here: 99.9 us
  starting transfers between devices  65.4 us (65%)
  waiting for transfers between devices  15.4 us (15%)
  Pallas kernels  13.9 us (14%)
  local copies, waits for them, and re-layouts  4.21 us (4%)
    ppermute x6, starting transfers between devices, swap(): return lax.ppermute(value, axis, [(i, i ^ bits) for i in range(size)])  20.5 us
    all_to_all x1, starting transfers between devices, shards(): got = lax.all_to_all(send, 'shard', split_axis=0, concat_axis=0, tiled=True)  18.5 us
    ppermute x6, waiting for transfers between devices, swap(): return lax.ppermute(value, axis, [(i, i ^ bits) for i in range(size)])  15.3 us
    ppermute x3, starting transfers between devices, shards(): late.append(lax.ppermute(slab, 'shard', pairs))  11.6 us
    all_to_all x1, starting transfers between devices, shards(): lax.all_to_all(copies, 'shard', split_axis=0, concat_axis=0, tiled=True,...  8.8 us
    all_to_all x1, starting transfers between devices, shards(): lax.all_to_all(spread_sum(parts), 'shard', split_axis=0, concat_axis=0, t...  5.93 us
    pallas_call x1, Pallas kernels, add_rows(): pl.pallas_call(add_kernel, out_shape=jax.ShapeDtypeStruct((ROWS_DEV, E),...  5.14 us
    unnamed x24, local copies, waits for them, and re-layouts  4.1 us
  transfers between devices with their start and end apart: 12, of which 5 were waited for; matrix products, arithmetic and copies ran while one was open for 0% of the time, Pallas kernels for 9%

profile of v3, /device:TPU:2, one launch (start us, length us, event | category | flops | bytes accessed | tf_op | source)
XLA Modules:
  0.0 99.9 jit_solution(1989078593771870208)
XLA Ops:
  0.7 0.6 copy-done.9
  1.3 0.0 copy-done.10
  1.3 0.0 copy-done.4
  1.4 0.0 copy-done.7
  1.4 0.9 copy-done
  2.3 0.9 copy-done.1
  3.3 0.8 copy-done.2
  4.1 3.5 %dense.1 = (f32[1024,128]{1,0:T(8,128)S(1)}, f32[1536,128]{1,0:T(8,128)S(1)}) custom-call(s32[8]{0:T(128)S(1)} %copy-done.8, bf16[8,128]{1,0:T(8,128)(2,1)S(1)} %copy-done.6, bf16[1024,128]{1,0:T(8,128)(2,1)S(1)} %bitcast.41, f32[8,128]{1,0:T(8,128)S(1)} %copy-done.4, bf16[512,256]{1,0:T(8,128)(2,1)S(1)} %copy-done.1, f32[1,256]{1,0:T(1,128)S(1)} %bitcast.43, ...), custom_call_target="tpu_custom_call" | custom-call | flops 1100000000 | bytes 2200000 | tf_op jit(solution)/shard_map/dense/pallas_call | solution.py:125
  7.7 3.5 %collective-permute-start = (f32[2,2,2,2,2,24,128]{6,5,4,3,2,1,0:T(8,128)S(1)}, f32[2,2,2,2,2,24,128]{6,5,4,3,2,1,0:T(8,128)S(1)}, u32[]{:S(2)}, u32[]{:S(2)}) collective-permute-start(f32[2,2,2,2,2,24,128]{6,5,4,3,2,1,0:T(8,128)S(1)} %dynamic-slice_bitcast_fusion), channel_id=1, source_target_pairs={{0,96},{48,144},{96,0},{144,48},{192,288},{240,336},{288,192},{336... | collective-permute-start | bytes 1179656 | tf_op jit(solution)/shard_map/ppermute | solution.py:295
  11.3 0.7 copy-done.5
  11.9 3.3 %pack.1 = f32[48,32,128]{2,1,0:T(8,128)} custom-call(s32[1]{0:T(128)} %bitcast.me_ref, s32[1,48]{1,0:T(1,128)S(1)} %copy-done.11, f32[1024,128]{1,0:T(8,128)S(1)} %get-tuple-element.15.drow_ref, s32[8,128]{1,0:T(8,128)S(1)} %copy-done.5, s32[48,48]{1,0:T(8,128)S(1)} %bitcast.42), custom_call_target="tpu_custom_call" | custom-call | flops 1241513984 | bytes 2000000 | tf_op jit(solution)/shard_map/pack/pallas_call | solution.py:211
  15.2 18.5 %all-to-all-start = ((f32[48,32,128]{2,1,0:T(8,128)}), f32[48,32,128]{2,1,0:T(8,128)S(1)}, u32[]{:S(2)}, u32[]{:S(2)}) async-start(f32[48,32,128]{2,1,0:T(8,128)} %pack.1), calls=%async_computation | async-start | bytes 1572864 | tf_op jit(solution)/shard_map/all_to_all | solution.py:404
  33.7 0.1 bitcast_add_fusion
  33.8 1.9 %collective-permute-start.1 = (f32[2,2,2,2,24,128]{5,4,3,2,1,0:T(8,128)S(1)}, f32[2,2,2,2,24,128]{5,4,3,2,1,0:T(8,128)S(1)}, u32[]{:S(2)}, u32[]{:S(2)}) collective-permute-start(f32[2,2,2,2,24,128]{5,4,3,2,1,0:T(8,128)S(1)} %dynamic-slice_bitcast_fusion.1), channel_id=1, source_target_pairs={{0,48},{48,0},{96,144},{144,96},{192,240},{240,192},{288,336},{336... | collective-permute-start | bytes 589832 | tf_op jit(solution)/shard_map/ppermute | solution.py:295
  35.7 1.4 %collective-permute-done.1 = f32[2,2,2,2,24,128]{5,4,3,2,1,0:T(8,128)S(1)} collective-permute-done((f32[2,2,2,2,24,128]{5,4,3,2,1,0:T(8,128)S(1)}, f32[2,2,2,2,24,128]{5,4,3,2,1,0:T(8,128)S(1)}, u32[]{:S(2)}, u32[]{:S(2)}) %collective-permute-start.1) | collective-permute-done | bytes 196640 | tf_op jit(solution)/shard_map/ppermute | solution.py:295
  37.2 4.5 %collective-permute-start.2 = (f32[2,2,2,24,128]{4,3,2,1,0:T(8,128)S(1)}, f32[2,2,2,24,128]{4,3,2,1,0:T(8,128)S(1)}, u32[]{:S(2)}, u32[]{:S(2)}) collective-permute-start(f32[2,2,2,24,128]{4,3,2,1,0:T(8,128)S(1)} %dynamic-slice_bitcast_fusion.2), channel_id=1, source_target_pairs={{0,192},{48,240},{96,288},{144,336},{192,0},{240,48},{288,96},{336... | collective-permute-start | bytes 294920 | tf_op jit(solution)/shard_map/ppermute | solution.py:295
  41.7 5.1 %collective-permute-done.2 = f32[2,2,2,24,128]{4,3,2,1,0:T(8,128)S(1)} collective-permute-done((f32[2,2,2,24,128]{4,3,2,1,0:T(8,128)S(1)}, f32[2,2,2,24,128]{4,3,2,1,0:T(8,128)S(1)}, u32[]{:S(2)}, u32[]{:S(2)}) %collective-permute-start.2) | collective-permute-done | bytes 98336 | tf_op jit(solution)/shard_map/ppermute | solution.py:295
  46.8 5.3 %collective-permute-start.3 = (f32[2,2,24,128]{3,2,1,0:T(8,128)S(1)}, f32[2,2,24,128]{3,2,1,0:T(8,128)S(1)}, u32[]{:S(2)}, u32[]{:S(2)}) collective-permute-start(f32[2,2,24,128]{3,2,1,0:T(8,128)S(1)} %dynamic-slice_bitcast_fusion.3), channel_id=1, source_target_pairs={{0,672},{48,720},{96,576},{144,624},{192,480},{240,528},{288,384},... | collective-permute-start | bytes 147464 | tf_op jit(solution)/shard_map/ppermute | solution.py:295
  52.1 2.5 %collective-permute-done.3 = f32[2,2,24,128]{3,2,1,0:T(8,128)S(1)} collective-permute-done((f32[2,2,24,128]{3,2,1,0:T(8,128)S(1)}, f32[2,2,24,128]{3,2,1,0:T(8,128)S(1)}, u32[]{:S(2)}, u32[]{:S(2)}) %collective-permute-start.3) | collective-permute-done | bytes 49184 | tf_op jit(solution)/shard_map/ppermute | solution.py:295
  54.7 2.3 %collective-permute-start.4 = (f32[2,24,128]{2,1,0:T(8,128)S(1)}, f32[2,24,128]{2,1,0:T(8,128)S(1)}, u32[]{:S(2)}, u32[]{:S(2)}) collective-permute-start(f32[2,24,128]{2,1,0:T(8,128)S(1)} %dynamic-slice_bitcast_fusion.4), channel_id=1, source_target_pairs={{0,1},{1,0},{2,3},{3,2},{4,5},{5,4},{6,7},{7,6},{8,9},{9,8},{10,11... | collective-permute-start | bytes 73736 | tf_op jit(solution)/shard_map/ppermute | solution.py:295
  57.0 3.8 %collective-permute-done.4 = f32[2,24,128]{2,1,0:T(8,128)S(1)} collective-permute-done((f32[2,24,128]{2,1,0:T(8,128)S(1)}, f32[2,24,128]{2,1,0:T(8,128)S(1)}, u32[]{:S(2)}, u32[]{:S(2)}) %collective-permute-start.4) | collective-permute-done | bytes 24608 | tf_op jit(solution)/shard_map/ppermute | solution.py:295
  60.8 3.1 %collective-permute-start.5 = (f32[24,128]{1,0:T(8,128)S(1)}, f32[24,128]{1,0:T(8,128)S(1)}, u32[]{:S(2)}, u32[]{:S(2)}) collective-permute-start(f32[24,128]{1,0:T(8,128)S(1)} %get-tuple-element.24), channel_id=1, source_target_pairs={{0,3},{1,2},{2,1},{3,0},{4,7},{5,6},{6,5},{7,4},{8,11},{9,10},{10,... | collective-permute-start | bytes 36872 | tf_op jit(solution)/shard_map/ppermute | solution.py:295
  63.9 2.5 %collective-permute-done.5.there_ref = f32[24,128]{1,0:T(8,128)S(1)} collective-permute-done((f32[24,128]{1,0:T(8,128)S(1)}, f32[24,128]{1,0:T(8,128)S(1)}, u32[]{:S(2)}, u32[]{:S(2)}) %collective-permute-start.5) | collective-permute-done | bytes 12320 | tf_op jit(solution)/shard_map/ppermute | solution.py:295
  66.4 0.7 join.1
  67.1 8.8 %all-to-all-start.1 = ((f32[12,24,128]{2,1,0:T(8,128)}), f32[12,24,128]{2,1,0:T(8,128)S(1)}, u32[]{:S(2)}, u32[]{:S(2)}) async-start(f32[12,24,128]{2,1,0:T(8,128)} %get-tuple-element.18), calls=%async_computation.1 | async-start | bytes 294912 | tf_op jit(solution)/shard_map/all_to_all | solution.py:418
  75.9 3.9 %collective-permute-start.8 = (f32[384,128]{1,0:T(8,128)S(1)}, f32[384,128]{1,0:T(8,128)S(1)}, u32[]{:S(2)}, u32[]{:S(2)}) collective-permute-start(f32[384,128]{1,0:T(8,128)S(1)} %get-tuple-element.17.own_ref), channel_id=1, source_target_pairs={{0,3},{1,0},{2,1},{3,2},{4,7},{5,4},{6,5},{7,6},{8,11},{9,8},{10,9... | collective-permute-start | bytes 589832 | tf_op jit(solution)/shard_map/ppermute | solution.py:427
  79.7 3.3 %collective-permute-start.7 = (f32[384,128]{1,0:T(8,128)S(1)}, f32[384,128]{1,0:T(8,128)S(1)}, u32[]{:S(2)}, u32[]{:S(2)}) collective-permute-start(f32[384,128]{1,0:T(8,128)S(1)} %get-tuple-element.17.own_ref), channel_id=1, source_target_pairs={{0,2},{1,3},{2,0},{3,1},{4,6},{5,7},{6,4},{7,5},{8,10},{9,11},{10,... | collective-permute-start | bytes 589832 | tf_op jit(solution)/shard_map/ppermute | solution.py:427
  83.0 4.5 %collective-permute-start.6 = (f32[384,128]{1,0:T(8,128)S(1)}, f32[384,128]{1,0:T(8,128)S(1)}, u32[]{:S(2)}, u32[]{:S(2)}) collective-permute-start(f32[384,128]{1,0:T(8,128)S(1)} %get-tuple-element.17.own_ref), channel_id=1, source_target_pairs={{0,1},{1,2},{2,3},{3,0},{4,5},{5,6},{6,7},{7,4},{8,9},{9,10},{10,1... | collective-permute-start | bytes 589832 | tf_op jit(solution)/shard_map/ppermute | solution.py:427
  87.5 0.6 spread_sum.1
  88.2 5.9 %all-to-all-start.2 = ((f32[4,24,128]{2,1,0:T(8,128)}), f32[4,24,128]{2,1,0:T(8,128)S(1)}, u32[]{:S(2)}, u32[]{:S(2)}) async-start(f32[4,24,128]{2,1,0:T(8,128)} %spread_sum.1), calls=%async_computation.2 | async-start | bytes 98304 | tf_op jit(solution)/shard_map/all_to_all | solution.py:421
  94.1 5.1 %add_rows.1 = f32[2048,128]{1,0:T(8,128)} custom-call(s32[1]{0:T(128)} %bitcast.me_ref, s32[1,48]{1,0:T(1,128)S(1)} %copy-done.11, f32[1536,128]{1,0:T(8,128)S(1)} %bitcast.38, f32[384,128]{1,0:T(8,128)S(1)} %get-tuple-element.17.own_ref, f32[384,128]{1,0:T(8,128)S(1)} %collective-permute-done.6.late0_ref, f32[384,128]{1,0:T(8,128)S(1)} %collective-permute-done.7.late1_ref, ...), custom_call_target="tpu_custom_call" | custom-call | flops 1610612736 | bytes 2500000 | tf_op jit(solution)/shard_map/add_rows/pallas_call | solution.py:269
  99.3 0.7 final.1
  (33 shorter events, 0.2 us)
Async XLA Ops:
  0.6 0.7 copy-start.9
  0.7 0.7 copy-start.10
  0.7 0.7 copy-start.4
  0.7 0.7 copy-start.6
  0.7 0.7 copy-start.7
  0.7 0.7 copy-start.8
  1.4 1.0 copy-start
  2.3 0.9 copy-start.1
  3.3 0.8 copy-start.2
  7.7 3.6 %copy-start.3 = (s32[1,48,48]{2,1,0:T(8,128)S(1)}, s32[1,48,48]{2,1,0:T(8,128)}, u32[]{:S(2)}) copy-start(s32[1,48,48]{2,1,0:T(8,128)} %param.16) | copy-start | bytes 27652
  7.7 26.0 %collective-permute-start = (f32[2,2,2,2,2,24,128]{6,5,4,3,2,1,0:T(8,128)S(1)}, f32[2,2,2,2,2,24,128]{6,5,4,3,2,1,0:T(8,128)S(1)}, u32[]{:S(2)}, u32[]{:S(2)}) collective-permute-start(f32[2,2,2,2,2,24,128]{6,5,4,3,2,1,0:T(8,128)S(1)} %dynamic-slice_bitcast_fusion), channel_id=1, source_target_pairs={{0,96},{48,144},{96,0},{144,48},{192,288},{240,336},{288,192},{336... | collective-permute-start | bytes 1179656 | tf_op jit(solution)/shard_map/ppermute | solution.py:295
  11.2 0.7 copy-start.5
  11.2 0.7 copy-start.11
  15.2 51.2 %all-to-all-start = ((f32[48,32,128]{2,1,0:T(8,128)}), f32[48,32,128]{2,1,0:T(8,128)S(1)}, u32[]{:S(2)}, u32[]{:S(2)}) async-start(f32[48,32,128]{2,1,0:T(8,128)} %pack.1), calls=%async_computation | async-start | bytes 1572864 | tf_op jit(solution)/shard_map/all_to_all | solution.py:404
  33.8 3.3 %collective-permute-start.1 = (f32[2,2,2,2,24,128]{5,4,3,2,1,0:T(8,128)S(1)}, f32[2,2,2,2,24,128]{5,4,3,2,1,0:T(8,128)S(1)}, u32[]{:S(2)}, u32[]{:S(2)}) collective-permute-start(f32[2,2,2,2,24,128]{5,4,3,2,1,0:T(8,128)S(1)} %dynamic-slice_bitcast_fusion.1), channel_id=1, source_target_pairs={{0,48},{48,0},{96,144},{144,96},{192,240},{240,192},{288,336},{336... | collective-permute-start | bytes 589832 | tf_op jit(solution)/shard_map/ppermute | solution.py:295
  37.2 9.6 %collective-permute-start.2 = (f32[2,2,2,24,128]{4,3,2,1,0:T(8,128)S(1)}, f32[2,2,2,24,128]{4,3,2,1,0:T(8,128)S(1)}, u32[]{:S(2)}, u32[]{:S(2)}) collective-permute-start(f32[2,2,2,24,128]{4,3,2,1,0:T(8,128)S(1)} %dynamic-slice_bitcast_fusion.2), channel_id=1, source_target_pairs={{0,192},{48,240},{96,288},{144,336},{192,0},{240,48},{288,96},{336... | collective-permute-start | bytes 294920 | tf_op jit(solution)/shard_map/ppermute | solution.py:295
  46.8 7.8 %collective-permute-start.3 = (f32[2,2,24,128]{3,2,1,0:T(8,128)S(1)}, f32[2,2,24,128]{3,2,1,0:T(8,128)S(1)}, u32[]{:S(2)}, u32[]{:S(2)}) collective-permute-start(f32[2,2,24,128]{3,2,1,0:T(8,128)S(1)} %dynamic-slice_bitcast_fusion.3), channel_id=1, source_target_pairs={{0,672},{48,720},{96,576},{144,624},{192,480},{240,528},{288,384},... | collective-permute-start | bytes 147464 | tf_op jit(solution)/shard_map/ppermute | solution.py:295
  54.7 6.1 %collective-permute-start.4 = (f32[2,24,128]{2,1,0:T(8,128)S(1)}, f32[2,24,128]{2,1,0:T(8,128)S(1)}, u32[]{:S(2)}, u32[]{:S(2)}) collective-permute-start(f32[2,24,128]{2,1,0:T(8,128)S(1)} %dynamic-slice_bitcast_fusion.4), channel_id=1, source_target_pairs={{0,1},{1,0},{2,3},{3,2},{4,5},{5,4},{6,7},{7,6},{8,9},{9,8},{10,11... | collective-permute-start | bytes 73736 | tf_op jit(solution)/shard_map/ppermute | solution.py:295
  60.8 5.6 %collective-permute-start.5 = (f32[24,128]{1,0:T(8,128)S(1)}, f32[24,128]{1,0:T(8,128)S(1)}, u32[]{:S(2)}, u32[]{:S(2)}) collective-permute-start(f32[24,128]{1,0:T(8,128)S(1)} %get-tuple-element.24), channel_id=1, source_target_pairs={{0,3},{1,2},{2,1},{3,0},{4,7},{5,6},{6,5},{7,4},{8,11},{9,10},{10,... | collective-permute-start | bytes 36872 | tf_op jit(solution)/shard_map/ppermute | solution.py:295
  67.1 20.5 %all-to-all-start.1 = ((f32[12,24,128]{2,1,0:T(8,128)}), f32[12,24,128]{2,1,0:T(8,128)S(1)}, u32[]{:S(2)}, u32[]{:S(2)}) async-start(f32[12,24,128]{2,1,0:T(8,128)} %get-tuple-element.18), calls=%async_computation.1 | async-start | bytes 294912 | tf_op jit(solution)/shard_map/all_to_all | solution.py:418
  75.9 18.2 %collective-permute-start.8 = (f32[384,128]{1,0:T(8,128)S(1)}, f32[384,128]{1,0:T(8,128)S(1)}, u32[]{:S(2)}, u32[]{:S(2)}) collective-permute-start(f32[384,128]{1,0:T(8,128)S(1)} %get-tuple-element.17.own_ref), channel_id=1, source_target_pairs={{0,3},{1,0},{2,1},{3,2},{4,7},{5,4},{6,5},{7,6},{8,11},{9,8},{10,9... | collective-permute-start | bytes 589832 | tf_op jit(solution)/shard_map/ppermute | solution.py:427
  79.7 14.4 %collective-permute-start.7 = (f32[384,128]{1,0:T(8,128)S(1)}, f32[384,128]{1,0:T(8,128)S(1)}, u32[]{:S(2)}, u32[]{:S(2)}) collective-permute-start(f32[384,128]{1,0:T(8,128)S(1)} %get-tuple-element.17.own_ref), channel_id=1, source_target_pairs={{0,2},{1,3},{2,0},{3,1},{4,6},{5,7},{6,4},{7,5},{8,10},{9,11},{10,... | collective-permute-start | bytes 589832 | tf_op jit(solution)/shard_map/ppermute | solution.py:427
  83.0 11.1 %collective-permute-start.6 = (f32[384,128]{1,0:T(8,128)S(1)}, f32[384,128]{1,0:T(8,128)S(1)}, u32[]{:S(2)}, u32[]{:S(2)}) collective-permute-start(f32[384,128]{1,0:T(8,128)S(1)} %get-tuple-element.17.own_ref), channel_id=1, source_target_pairs={{0,1},{1,2},{2,3},{3,0},{4,5},{5,6},{6,7},{7,4},{8,9},{9,10},{10,1... | collective-permute-start | bytes 589832 | tf_op jit(solution)/shard_map/ppermute | solution.py:427
  88.2 11.1 %all-to-all-start.2 = ((f32[4,24,128]{2,1,0:T(8,128)}), f32[4,24,128]{2,1,0:T(8,128)S(1)}, u32[]{:S(2)}, u32[]{:S(2)}) async-start(f32[4,24,128]{2,1,0:T(8,128)} %spread_sum.1), calls=%async_computation.2 | async-start | bytes 98304 | tf_op jit(solution)/shard_map/all_to_all | solution.py:421

commit v4 on v3

--- a/solution.py
+++ b/solution.py
@@ -16,6 +16,10 @@
 VMEM_LIMIT = 24 * 1024 * 1024
 
 
+def in_hbm(*values):
+    return [pltpu.with_memory_space_constraint(v, pltpu.HBM) for v in values]
+
+
 def iota(shape, dim):
     return lax.broadcasted_iota(jnp.int32, shape, dim)
 
@@ -44,13 +48,13 @@
 
 
 def dense_kernel(
-    lengths_ref, target_in, hist_in, pg_in, w1_in, b1_in, w2_in, b2_in, w3_in,
-    drow_ref, part_ref,
-    target_ref, hist_ref, pg_ref, w1_ref, b1_ref, w2_ref, b2_ref, w3_ref,
+    lengths_in, target_in, hist_in, pg_in, w1_in, b1_in, w2_in, b2_in, w3_in, ids_in, blocks_in,
+    drow_ref, part_ref, ids_ref, blocks_ref,
+    lengths_ref, target_ref, hist_ref, pg_ref, w1_ref, b1_ref, w2_ref, b2_ref, w3_ref,
     feats, act1s, dz2s, dz1s, sems,
 ):
-    inputs = (hist_in, w1_in, target_in, b1_in, w2_in, b2_in, w3_in, pg_in)
-    held = (hist_ref, w1_ref, target_ref, b1_ref, w2_ref, b2_ref, w3_ref, pg_ref)
+    inputs = (hist_in, w1_in, target_in, b1_in, w2_in, b2_in, w3_in, pg_in, lengths_in, ids_in, blocks_in)
+    held = (hist_ref, w1_ref, target_ref, b1_ref, w2_ref, b2_ref, w3_ref, pg_ref, lengths_ref, ids_ref, blocks_ref)
     copies = [pltpu.make_async_copy(a, b, sems.at[k]) for k, (a, b) in enumerate(zip(inputs, held))]
     for copy in copies:
         copy.start()
@@ -119,50 +123,43 @@
             part_ref[base + 16 : base + 24, :] = last
 
 
-def dense(lengths, target, hist, pg, w1, b1, w2, b2, w3):
-    whole = pl.BlockSpec(memory_space=pltpu.VMEM)
-    scalar = pl.BlockSpec(memory_space=pltpu.SMEM)
+def dense(lengths, target, hist, pg, w1, b1, w2, b2, w3, ids, blocks):
+    whole = pl.BlockSpec(memory_space=pltpu.VMEM)
     return pl.pallas_call(
         dense_kernel,
         out_shape=[
             jax.ShapeDtypeStruct((SLOTS, E), jnp.float32),
             jax.ShapeDtypeStruct((16 * PART, E), jnp.float32),
+            jax.ShapeDtypeStruct(ids.shape, ids.dtype),
+            jax.ShapeDtypeStruct(blocks.shape, blocks.dtype),
         ],
-        in_specs=[scalar] + [pl.BlockSpec(memory_space=pltpu.HBM)] * 8,
-        out_specs=[whole, whole],
-        scratch_shapes=[pltpu.VMEM(v.shape, v.dtype) for v in (target, hist, pg, w1, b1, w2, b2, w3)]
+        in_specs=[pl.BlockSpec(memory_space=pltpu.HBM)] * 11,
+        out_specs=[whole] * 4,
+        scratch_shapes=[pltpu.SMEM(lengths.shape, lengths.dtype)]
+        + [pltpu.VMEM(v.shape, v.dtype) for v in (target, hist, pg, w1, b1, w2, b2, w3)]
         + [
             pltpu.VMEM((SLOTS, 4 * E), jnp.bfloat16),
             pltpu.VMEM((SLOTS, 2 * E), jnp.bfloat16),
             pltpu.VMEM((SLOTS, E), jnp.bfloat16),
             pltpu.VMEM((SLOTS, 2 * E), jnp.bfloat16),
-            pltpu.SemaphoreType.DMA((8,)),
+            pltpu.SemaphoreType.DMA((11,)),
         ],
         compiler_params=pltpu.CompilerParams(vmem_limit_bytes=VMEM_LIMIT),
         cost_estimate=pl.CostEstimate(
             flops=1_100_000_000, bytes_accessed=2_200_000, transcendentals=400_000
         ),
         name="dense",
-    )(lengths, target, hist, pg, w1, b1, w2, b2, w3)
+    )(*in_hbm(lengths, target, hist, pg, w1, b1, w2, b2, w3, ids, blocks))
 
 
 def pack_kernel(
-    me_ref, counts_ref, drow_ref, ids_in, blocks_in, send_ref, ids_ref, blocks_ref, pick, source, sems
+    me_ref, counts_in, drow_ref, ids_ref, blocks_ref, send_ref, counts_ref, pick, source, sem
 ):
-    copies = [
-        pltpu.make_async_copy(ids_in, ids_ref, sems.at[0]),
-        pltpu.make_async_copy(blocks_in, blocks_ref, sems.at[1]),
-    ]
-    for copy in copies:
-        copy.start()
+    fetch = pltpu.make_async_copy(counts_in, counts_ref, sem)
+    fetch.start()
     me = me_ref[0]
-    hot = jnp.int32(0)
-    for o in range(OWNERS):
-        hot = jnp.where(counts_ref[0, o] > HALF, jnp.int32(o), hot)
 
     source[:, : 2 * E] = split(drow_ref[...])
-    for copy in copies:
-        copy.wait()
     ids = ids_ref[...] & (ROWS_DEV - 1)
     id_columns = jnp.transpose(ids.astype(jnp.float32))
     for b in range(8):
@@ -179,6 +176,10 @@
     for o in range(0, OWNERS, 2):
         pair = [one_hot(eye, blocks_ref[k : k + 1, :]) for k in (o, o + 1)]
         pick[o * HALF : (o + 2) * HALF, :] = jnp.concatenate(pair, axis=0).astype(jnp.bfloat16)
+    fetch.wait()
+    hot = jnp.int32(0)
+    for o in range(OWNERS):
+        hot = jnp.where(counts_ref[0, o] > HALF, jnp.int32(o), hot)
     r, lane = iota((32, OWNERS), 0), iota((32, OWNERS), 1)
     late = (lane == HALF + PIECE * (r // 8) + r % 8) & (r % 8 < PIECE)
     last = one_hot(late, blocks_ref[pl.ds(hot, 1), :])
@@ -211,21 +212,20 @@
     return pl.pallas_call(
         pack_kernel,
         out_shape=jax.ShapeDtypeStruct((OWNERS, BLOCK, E), jnp.float32),
-        in_specs=[scalar, scalar, whole] + [pl.BlockSpec(memory_space=pltpu.HBM)] * 2,
+        in_specs=[scalar, pl.BlockSpec(memory_space=pltpu.HBM), whole, whole, whole],
         out_specs=whole,
         scratch_shapes=[
-            pltpu.VMEM(ids.shape, ids.dtype),
-            pltpu.VMEM(blocks.shape, blocks.dtype),
+            pltpu.SMEM(counts.shape, counts.dtype),
             pltpu.VMEM((OWNERS * HALF + 32, SLOTS), jnp.bfloat16),
             pltpu.VMEM((SLOTS, 4 * E), jnp.bfloat16),
-            pltpu.SemaphoreType.DMA((2,)),
+            pltpu.SemaphoreType.DMA(()),
         ],
         compiler_params=pltpu.CompilerParams(vmem_limit_bytes=VMEM_LIMIT),
         cost_estimate=pl.CostEstimate(
             flops=2 * 1184 * 1024 * 512, bytes_accessed=2_000_000, transcendentals=0
         ),
         name="pack",
-    )(me, counts, drow, ids, blocks)
+    )(me, *in_hbm(counts), drow, ids, blocks)
 
 
 STEP = 512
@@ -284,9 +284,8 @@
 
 
 GRP_SWAPS = (2, 1, 4, 14)
-X_SWAPS = (1, 3)
+SIDE = 2 * QUARTER
 NZ = OWNERS // NX
-X_GROUPS = [[z * NX + x for x in range(NX)] for z in range(NZ)]
 Z_GROUPS = [[z * NX + x for z in range(NZ)] for x in range(NX)]
 
 
@@ -308,7 +307,7 @@
     return pl.pallas_call(
         join_kernel,
         out_shape=[
-            jax.ShapeDtypeStruct((NZ, QUARTER, E), jnp.float32),
+            jax.ShapeDtypeStruct((NZ, SIDE, E), jnp.float32),
             jax.ShapeDtypeStruct((OWNERS * 8, E), jnp.float32),
         ],
         in_specs=[whole, whole, whole],
@@ -319,38 +318,36 @@
     )(keep, there, got)
 
 
-def spread_kernel(parts_ref, out_ref):
+def add_kernel_z(parts_ref, out_ref):
     part = parts_ref[0]
     for z in range(1, NZ):
         part += parts_ref[z]
-    for x in range(NX):
-        out_ref[x] = part
-
-
-def spread_sum(parts):
-    whole = pl.BlockSpec(memory_space=pltpu.VMEM)
-    return pl.pallas_call(
-        spread_kernel,
-        out_shape=jax.ShapeDtypeStruct((NX, QUARTER, E), jnp.float32),
+    out_ref[...] = part
+
+
+def add_parts(parts):
+    whole = pl.BlockSpec(memory_space=pltpu.VMEM)
+    return pl.pallas_call(
+        add_kernel_z,
+        out_shape=jax.ShapeDtypeStruct((SIDE, E), jnp.float32),
         in_specs=[whole],
         out_specs=whole,
         compiler_params=pltpu.CompilerParams(vmem_limit_bytes=VMEM_LIMIT),
-        cost_estimate=pl.CostEstimate(flops=33792, bytes_accessed=200_000, transcendentals=0),
-        name="spread_sum",
+        cost_estimate=pl.CostEstimate(flops=67584, bytes_accessed=320_000, transcendentals=0),
+        name="add_parts",
     )(parts)
 
 
-HOLDER = (0, 3, 1, 2)
-
-
-def final_kernel(g_ref, total_ref, w1_ref, b1_ref, w2_ref, b2_ref, w3_ref):
-    quarters = [total_ref[x] for x in HOLDER]
+def final_kernel(place_ref, mine_ref, other_ref, w1_ref, b1_ref, w2_ref, b2_ref, w3_ref):
+    g, first = place_ref[0], place_ref[1] == 0
+    mine, other = mine_ref[...], other_ref[...]
+    low, high = jnp.where(first, mine, other), jnp.where(first, other, mine)
+    quarters = [low[:QUARTER], low[QUARTER:], high[:QUARTER], high[QUARTER:]]
     for k in range(NX):
         top, side = 16 * (k % 2), E * (k // 2)
         w1_ref[top : top + 16, side : side + E] = quarters[k][:16]
     w2_ref[:8, :] = quarters[0][16:]
     w2_ref[8:, :] = quarters[1][16:]
-    g = g_ref[0]
     small = quarters[2][16:]
     by16 = pltpu.roll(small, (128 - (g % 8) * 16) % 128, 1)
     by8 = pltpu.roll(small, (128 - g * 8) % 128, 1)
@@ -359,18 +356,18 @@
     w3_ref[...] = by8[3:4, :8]
 
 
-def final(g, total):
+def final(place, mine, other):
     whole = pl.BlockSpec(memory_space=pltpu.VMEM)
     shapes = ((32, 2 * E), (1, 16), (16, E), (1, 8), (1, 8))
     return pl.pallas_call(
         final_kernel,
         out_shape=[jax.ShapeDtypeStruct(shape, jnp.float32) for shape in shapes],
-        in_specs=[pl.BlockSpec(memory_space=pltpu.SMEM), whole],
+        in_specs=[pl.BlockSpec(memory_space=pltpu.SMEM), whole, whole],
         out_specs=[whole] * 5,
         compiler_params=pltpu.CompilerParams(vmem_limit_bytes=VMEM_LIMIT),
         cost_estimate=pl.CostEstimate(flops=1024, bytes_accessed=100_000, transcendentals=0),
         name="final",
-    )(g, total)
+    )(place, mine, other)
 
 
 def shards(
@@ -389,7 +386,7 @@
 ):
     g = lax.axis_index("grp")
     me = lax.axis_index("shard").reshape(1)
-    drow, part = dense(
+    drow, part, ids, blocks = dense(
         lengths,
         target,
         history.reshape(SLOTS, E),
@@ -399,34 +396,33 @@
         attn_w2,
         attn_b2.reshape(1, E),
         attn_w3.reshape(1, E),
+        hist_ids,
+        block_rows[0],
     )
-    send = pack(me, block_counts, drow, hist_ids, block_rows[0])
+    send = pack(me, block_counts, drow, ids, blocks)
     got = lax.all_to_all(send, "shard", split_axis=0, concat_axis=0, tiled=True)
     got = got.reshape(OWNERS * BLOCK, E)
 
-    part = part.reshape(2, 2, 2, 2, 2, 2, QUARTER, E)
+    part = part.reshape(2, 2, 2, 2, 2, SIDE, E)
     y2 = (g >> 3) & 1
-    x1 = (me[0] >> 1) & 1
-    bits = (((g >> 1) & 1) ^ y2, g & 1, ((g >> 2) & 1) ^ y2, y2, (me[0] & 1) ^ x1, x1)
-    steps = [("grp", k) for k in GRP_SWAPS] + [("shard", k) for k in X_SWAPS]
-    for bit, (axis, k) in zip(bits, steps):
+    side = (me[0] ^ (me[0] >> 1)) & 1
+    bits = (((g >> 1) & 1) ^ y2, g & 1, ((g >> 2) & 1) ^ y2, y2, side)
+    for bit, (axis, k) in zip(bits, [("grp", k) for k in GRP_SWAPS] + [("shard", 1)]):
         keep = lax.dynamic_index_in_dim(part, bit, 0, False)
         away = lax.dynamic_index_in_dim(part, 1 - bit, 0, False)
-        there = swap(away, axis, k)
-        part = keep + there
-    copies, slab = join(keep, there, got)
+        part = keep + swap(away, axis, k)
+    copies, slab = join(part, swap(part, "shard", 3), got)
     parts = lax.all_to_all(
         copies, "shard", split_axis=0, concat_axis=0, tiled=True, axis_index_groups=Z_GROUPS
     )
-    total = lax.all_to_all(
-        spread_sum(parts), "shard", split_axis=0, concat_axis=0, tiled=True, axis_index_groups=X_GROUPS
-    )
+    total = add_parts(parts)
+    other = swap(total, "shard", 1)
     late = [slab]
     for turn in (1, 2, 3):
         pairs = [(s, s // NX * NX + (s + turn) % NX) for s in range(OWNERS)]
         late.append(lax.ppermute(slab, "shard", pairs))
     table = add_rows(me, block_counts, got, late)
-    grad_w1, grad_b1, grad_w2, grad_b2, grad_w3 = final(g.reshape(1), total)
+    grad_w1, grad_b1, grad_w2, grad_b2, grad_w3 = final(jnp.stack([g, side]), total, other)
     return (
         table[None],
         grad_w1,

time: 101 us -> 97.7 us (0.967)
  the two profiles are of different devices: /device:TPU:2 before, /device:TPU:60 now
where the time goes in v4:
time: 97.7 us; the launch traced here: 97.1 us
  starting transfers between devices  58.5 us (60%)
  waiting for transfers between devices  23.4 us (24%)
  Pallas kernels  14 us (14%)
    ppermute x7, starting transfers between devices, swap(): return lax.ppermute(value, axis, [(i, i ^ bits) for i in range(size)])  20.7 us
    all_to_all x1, starting transfers between devices, shards(): got = lax.all_to_all(send, 'shard', split_axis=0, concat_axis=0, tiled=True)  18.5 us
    ppermute x7, waiting for transfers between devices, swap(): return lax.ppermute(value, axis, [(i, i ^ bits) for i in range(size)])  18.5 us
    ppermute x3, starting transfers between devices, shards(): late.append(lax.ppermute(slab, 'shard', pairs))  10.2 us
    all_to_all x1, starting transfers between devices, shards(): lax.all_to_all(copies, 'shard', split_axis=0, concat_axis=0, tiled=True,...  9.13 us
    pallas_call x1, Pallas kernels, add_rows(): pl.pallas_call(add_kernel, out_shape=jax.ShapeDtypeStruct((ROWS_DEV, E),...  5.13 us
    all_to_all x1, waiting for transfers between devices, shards(): lax.all_to_all(copies, 'shard', split_axis=0, concat_axis=0, tiled=True,...  4.95 us
    pallas_call x1, Pallas kernels, dense(): pl.pallas_call(dense_kernel, out_shape=[jax.ShapeDtypeStruct((SLOTS, E),...  3.91 us
  transfers between devices with their start and end apart: 12, of which 6 were waited for; matrix products, arithmetic and copies ran while one was open for 0% of the time, Pallas kernels for 8%

profile of v4, /device:TPU:60, one launch (start us, length us, event | category | flops | bytes accessed | tf_op | source)
XLA Modules:
  0.0 97.1 jit_solution(7843832206485638486)
XLA Ops:
  0.7 3.9 %dense.1 = (f32[1024,128]{1,0:T(8,128)S(1)}, f32[1536,128]{1,0:T(8,128)S(1)}, s32[8,128]{1,0:T(8,128)S(1)}, s32[48,48]{1,0:T(8,128)S(1)}) custom-call(s32[8]{0:T(128)} %lengths_in.1, bf16[8,128]{1,0:T(8,128)(2,1)} %target_in.1, bf16[1024,128]{1,0:T(8,128)(2,1)} %bitcast.38, f32[8,128]{1,0:T(8,128)} %pg_in.1, bf16[512,256]{1,0:T(8,128)(2,1)} %w1_in.1, ...), custom_call_target="tpu_custom_call" | custom-call | flops 1100000000 | bytes 2200000 | tf_op jit(solution)/shard_map/dense/pallas_call | solution.py:128
  4.6 3.3 %collective-permute-start = (f32[2,2,2,2,48,128]{5,4,3,2,1,0:T(8,128)S(1)}, f32[2,2,2,2,48,128]{5,4,3,2,1,0:T(8,128)S(1)}, u32[]{:S(2)}, u32[]{:S(2)}) collective-permute-start(f32[2,2,2,2,48,128]{5,4,3,2,1,0:T(8,128)S(1)} %dynamic-slice_bitcast_fusion), channel_id=1, source_target_pairs={{0,96},{48,144},{96,0},{144,48},{192,288},{240,336},{288,192},{336... | collective-permute-start | bytes 1179656 | tf_op jit(solution)/shard_map/ppermute | solution.py:294
  7.9 3.0 %pack.1 = f32[48,32,128]{2,1,0:T(8,128)} custom-call(s32[1]{0:T(128)} %bitcast.me_ref, s32[1,48]{1,0:T(1,128)} %counts_ref.1, f32[1024,128]{1,0:T(8,128)S(1)} %get-tuple-element.17.drow_ref, s32[8,128]{1,0:T(8,128)S(1)} %get-tuple-element.18.ids_ref, s32[48,48]{1,0:T(8,128)S(1)} %get-tuple-element.19.blocks_ref), custom_call_target="tpu_custom_call" | custom-call | flops 1241513984 | bytes 2000000 | tf_op jit(solution)/shard_map/pack/pallas_call | solution.py:212
  10.9 18.5 %all-to-all-start = ((f32[48,32,128]{2,1,0:T(8,128)}), f32[48,32,128]{2,1,0:T(8,128)S(1)}, u32[]{:S(2)}, u32[]{:S(2)}) async-start(f32[48,32,128]{2,1,0:T(8,128)} %pack.1), calls=%async_computation | async-start | bytes 1572864 | tf_op jit(solution)/shard_map/all_to_all | solution.py:403
  29.4 0.0 collective-permute-done
  29.5 1.9 %collective-permute-start.1 = (f32[2,2,2,48,128]{4,3,2,1,0:T(8,128)S(1)}, f32[2,2,2,48,128]{4,3,2,1,0:T(8,128)S(1)}, u32[]{:S(2)}, u32[]{:S(2)}) collective-permute-start(f32[2,2,2,48,128]{4,3,2,1,0:T(8,128)S(1)} %dynamic-slice_bitcast_fusion.1), channel_id=1, source_target_pairs={{0,48},{48,0},{96,144},{144,96},{192,240},{240,192},{288,336},{336... | collective-permute-start | bytes 589832 | tf_op jit(solution)/shard_map/ppermute | solution.py:294
  31.4 1.4 %collective-permute-done.1 = f32[2,2,2,48,128]{4,3,2,1,0:T(8,128)S(1)} collective-permute-done((f32[2,2,2,48,128]{4,3,2,1,0:T(8,128)S(1)}, f32[2,2,2,48,128]{4,3,2,1,0:T(8,128)S(1)}, u32[]{:S(2)}, u32[]{:S(2)}) %collective-permute-start.1) | collective-permute-done | bytes 196640 | tf_op jit(solution)/shard_map/ppermute | solution.py:294
  32.9 4.0 %collective-permute-start.2 = (f32[2,2,48,128]{3,2,1,0:T(8,128)S(1)}, f32[2,2,48,128]{3,2,1,0:T(8,128)S(1)}, u32[]{:S(2)}, u32[]{:S(2)}) collective-permute-start(f32[2,2,48,128]{3,2,1,0:T(8,128)S(1)} %dynamic-slice_bitcast_fusion.2), channel_id=1, source_target_pairs={{0,192},{48,240},{96,288},{144,336},{192,0},{240,48},{288,96},{336... | collective-permute-start | bytes 294920 | tf_op jit(solution)/shard_map/ppermute | solution.py:294
  36.9 5.7 %collective-permute-done.2 = f32[2,2,48,128]{3,2,1,0:T(8,128)S(1)} collective-permute-done((f32[2,2,48,128]{3,2,1,0:T(8,128)S(1)}, f32[2,2,48,128]{3,2,1,0:T(8,128)S(1)}, u32[]{:S(2)}, u32[]{:S(2)}) %collective-permute-start.2) | collective-permute-done | bytes 98336 | tf_op jit(solution)/shard_map/ppermute | solution.py:294
  42.6 1.9 %collective-permute-start.3 = (f32[2,48,128]{2,1,0:T(8,128)S(1)}, f32[2,48,128]{2,1,0:T(8,128)S(1)}, u32[]{:S(2)}, u32[]{:S(2)}) collective-permute-start(f32[2,48,128]{2,1,0:T(8,128)S(1)} %dynamic-slice_bitcast_fusion.3), channel_id=1, source_target_pairs={{0,672},{48,720},{96,576},{144,624},{192,480},{240,528},{288,384},... | collective-permute-start | bytes 147464 | tf_op jit(solution)/shard_map/ppermute | solution.py:294
  44.6 5.6 %collective-permute-done.3 = f32[2,48,128]{2,1,0:T(8,128)S(1)} collective-permute-done((f32[2,48,128]{2,1,0:T(8,128)S(1)}, f32[2,48,128]{2,1,0:T(8,128)S(1)}, u32[]{:S(2)}, u32[]{:S(2)}) %collective-permute-start.3) | collective-permute-done | bytes 49184 | tf_op jit(solution)/shard_map/ppermute | solution.py:294
  50.2 3.1 %collective-permute-start.4 = (f32[48,128]{1,0:T(8,128)S(1)}, f32[48,128]{1,0:T(8,128)S(1)}, u32[]{:S(2)}, u32[]{:S(2)}) collective-permute-start(f32[48,128]{1,0:T(8,128)S(1)} %dynamic-slice_bitcast_fusion.4), channel_id=1, source_target_pairs={{0,1},{1,0},{2,3},{3,2},{4,5},{5,4},{6,7},{7,6},{8,9},{9,8},{10,11... | collective-permute-start | bytes 73736 | tf_op jit(solution)/shard_map/ppermute | solution.py:294
  53.2 2.7 %collective-permute-done.4 = f32[48,128]{1,0:T(8,128)S(1)} collective-permute-done((f32[48,128]{1,0:T(8,128)S(1)}, f32[48,128]{1,0:T(8,128)S(1)}, u32[]{:S(2)}, u32[]{:S(2)}) %collective-permute-start.4) | collective-permute-done | bytes 24608 | tf_op jit(solution)/shard_map/ppermute | solution.py:294
  55.9 2.5 %collective-permute-start.5 = (f32[48,128]{1,0:T(8,128)S(1)}, f32[48,128]{1,0:T(8,128)S(1)}, u32[]{:S(2)}, u32[]{:S(2)}) collective-permute-start(f32[48,128]{1,0:T(8,128)S(1)} %bitcast_add_fusion.4.keep_ref), channel_id=1, source_target_pairs={{0,3},{1,2},{2,1},{3,0},{4,7},{5,6},{6,5},{7,4},{8,11},{9,10},{10,... | collective-permute-start | bytes 73736 | tf_op jit(solution)/shard_map/ppermute | solution.py:294
  58.5 3.2 %collective-permute-done.5.there_ref = f32[48,128]{1,0:T(8,128)S(1)} collective-permute-done((f32[48,128]{1,0:T(8,128)S(1)}, f32[48,128]{1,0:T(8,128)S(1)}, u32[]{:S(2)}, u32[]{:S(2)}) %collective-permute-start.5) | collective-permute-done | bytes 24608 | tf_op jit(solution)/shard_map/ppermute | solution.py:294
  61.6 0.0 all-to-all-done
  61.6 0.7 join.1
  62.4 9.1 %all-to-all-start.1 = ((f32[12,48,128]{2,1,0:T(8,128)}), f32[12,48,128]{2,1,0:T(8,128)S(1)}, u32[]{:S(2)}, u32[]{:S(2)}) async-start(f32[12,48,128]{2,1,0:T(8,128)} %get-tuple-element.22), calls=%async_computation.1 | async-start | bytes 589824 | tf_op jit(solution)/shard_map/all_to_all | solution.py:415
  71.5 2.5 %collective-permute-start.8 = (f32[384,128]{1,0:T(8,128)S(1)}, f32[384,128]{1,0:T(8,128)S(1)}, u32[]{:S(2)}, u32[]{:S(2)}) collective-permute-start(f32[384,128]{1,0:T(8,128)S(1)} %get-tuple-element.21.own_ref), channel_id=1, source_target_pairs={{0,3},{1,0},{2,1},{3,2},{4,7},{5,4},{6,5},{7,6},{8,11},{9,8},{10,9... | collective-permute-start | bytes 589832 | tf_op jit(solution)/shard_map/ppermute | solution.py:423
  74.0 5.8 %collective-permute-start.7 = (f32[384,128]{1,0:T(8,128)S(1)}, f32[384,128]{1,0:T(8,128)S(1)}, u32[]{:S(2)}, u32[]{:S(2)}) collective-permute-start(f32[384,128]{1,0:T(8,128)S(1)} %get-tuple-element.21.own_ref), channel_id=1, source_target_pairs={{0,2},{1,3},{2,0},{3,1},{4,6},{5,7},{6,4},{7,5},{8,10},{9,11},{10,... | collective-permute-start | bytes 589832 | tf_op jit(solution)/shard_map/ppermute | solution.py:423
  79.8 1.9 %collective-permute-start.6 = (f32[384,128]{1,0:T(8,128)S(1)}, f32[384,128]{1,0:T(8,128)S(1)}, u32[]{:S(2)}, u32[]{:S(2)}) collective-permute-start(f32[384,128]{1,0:T(8,128)S(1)} %get-tuple-element.21.own_ref), channel_id=1, source_target_pairs={{0,1},{1,2},{2,3},{3,0},{4,5},{5,6},{6,7},{7,4},{8,9},{9,10},{10,1... | collective-permute-start | bytes 589832 | tf_op jit(solution)/shard_map/ppermute | solution.py:423
  81.7 0.1 pad_add_fusion.place_ref
  81.8 0.0 copy-start
  81.8 5.0 %all-to-all-done.1.parts_ref = f32[12,48,128]{2,1,0:T(8,128)S(1)} async-done(((f32[12,48,128]{2,1,0:T(8,128)}), f32[12,48,128]{2,1,0:T(8,128)S(1)}, u32[]{:S(2)}, u32[]{:S(2)}) %all-to-all-start.1) | async-done | bytes 294944 | tf_op jit(solution)/shard_map/all_to_all | solution.py:415
  86.8 4.0 %collective-permute-start.9 = (f32[48,128]{1,0:T(8,128)S(1)}, f32[48,128]{1,0:T(8,128)S(1)}, u32[]{:S(2)}, u32[]{:S(2)}) collective-permute-start(f32[48,128]{1,0:T(8,128)S(1)} %add_parts.1.mine_ref), channel_id=1, source_target_pairs={{0,1},{1,0},{2,3},{3,2},{4,5},{5,4},{6,7},{7,6},{8,9},{9,8},{10,11... | collective-permute-start | bytes 73736 | tf_op jit(solution)/shard_map/ppermute | solution.py:294
  90.7 0.0 collective-permute-done.8.late2_ref
  90.7 0.0 collective-permute-done.7.late1_ref
  90.8 0.0 collective-permute-done.6.late0_ref
  90.8 0.0 copy-done
  90.8 5.1 %add_rows.1 = f32[2048,128]{1,0:T(8,128)} custom-call(s32[1]{0:T(128)} %bitcast.me_ref, s32[1,48]{1,0:T(1,128)S(1)} %copy-done, f32[1536,128]{1,0:T(8,128)S(1)} %bitcast.35, f32[384,128]{1,0:T(8,128)S(1)} %get-tuple-element.21.own_ref, f32[384,128]{1,0:T(8,128)S(1)} %collective-permute-done.6.late0_ref, f32[384,128]{1,0:T(8,128)S(1)} %collective-permute-done.7.late1_ref, ...), custom_call_target="tpu_custom_call" | custom-call | flops 1610612736 | bytes 2500000 | tf_op jit(solution)/shard_map/add_rows/pallas_call | solution.py:269
  95.9 0.0 collective-permute-done.9.other_ref
  95.9 1.2 %final.1 = (f32[32,256]{1,0:T(8,128)}, f32[1,16]{1,0:T(1,128)}, f32[16,128]{1,0:T(8,128)}, f32[1,8]{1,0:T(1,128)}, f32[1,8]{1,0:T(1,128)}) custom-call(s32[2]{0:T(128)S(1)} %pad_add_fusion.place_ref, f32[48,128]{1,0:T(8,128)S(1)} %add_parts.1.mine_ref, f32[48,128]{1,0:T(8,128)S(1)} %collective-permute-done.9.other_ref), custom_call_target="tpu_custom_call" | custom-call | flops 1024 | bytes 100000 | tf_op jit(solution)/shard_map/final/pallas_call | solution.py:362
  (11 shorter events, 0.2 us)
Async XLA Ops:
  4.6 24.8 %collective-permute-start = (f32[2,2,2,2,48,128]{5,4,3,2,1,0:T(8,128)S(1)}, f32[2,2,2,2,48,128]{5,4,3,2,1,0:T(8,128)S(1)}, u32[]{:S(2)}, u32[]{:S(2)}) collective-permute-start(f32[2,2,2,2,48,128]{5,4,3,2,1,0:T(8,128)S(1)} %dynamic-slice_bitcast_fusion), channel_id=1, source_target_pairs={{0,96},{48,144},{96,0},{144,48},{192,288},{240,336},{288,192},{336... | collective-permute-start | bytes 1179656 | tf_op jit(solution)/shard_map/ppermute | solution.py:294
  10.9 50.7 %all-to-all-start = ((f32[48,32,128]{2,1,0:T(8,128)}), f32[48,32,128]{2,1,0:T(8,128)S(1)}, u32[]{:S(2)}, u32[]{:S(2)}) async-start(f32[48,32,128]{2,1,0:T(8,128)} %pack.1), calls=%async_computation | async-start | bytes 1572864 | tf_op jit(solution)/shard_map/all_to_all | solution.py:403
  29.5 3.3 %collective-permute-start.1 = (f32[2,2,2,48,128]{4,3,2,1,0:T(8,128)S(1)}, f32[2,2,2,48,128]{4,3,2,1,0:T(8,128)S(1)}, u32[]{:S(2)}, u32[]{:S(2)}) collective-permute-start(f32[2,2,2,48,128]{4,3,2,1,0:T(8,128)S(1)} %dynamic-slice_bitcast_fusion.1), channel_id=1, source_target_pairs={{0,48},{48,0},{96,144},{144,96},{192,240},{240,192},{288,336},{336... | collective-permute-start | bytes 589832 | tf_op jit(solution)/shard_map/ppermute | solution.py:294
  32.9 9.7 %collective-permute-start.2 = (f32[2,2,48,128]{3,2,1,0:T(8,128)S(1)}, f32[2,2,48,128]{3,2,1,0:T(8,128)S(1)}, u32[]{:S(2)}, u32[]{:S(2)}) collective-permute-start(f32[2,2,48,128]{3,2,1,0:T(8,128)S(1)} %dynamic-slice_bitcast_fusion.2), channel_id=1, source_target_pairs={{0,192},{48,240},{96,288},{144,336},{192,0},{240,48},{288,96},{336... | collective-permute-start | bytes 294920 | tf_op jit(solution)/shard_map/ppermute | solution.py:294
  42.6 7.5 %collective-permute-start.3 = (f32[2,48,128]{2,1,0:T(8,128)S(1)}, f32[2,48,128]{2,1,0:T(8,128)S(1)}, u32[]{:S(2)}, u32[]{:S(2)}) collective-permute-start(f32[2,48,128]{2,1,0:T(8,128)S(1)} %dynamic-slice_bitcast_fusion.3), channel_id=1, source_target_pairs={{0,672},{48,720},{96,576},{144,624},{192,480},{240,528},{288,384},... | collective-permute-start | bytes 147464 | tf_op jit(solution)/shard_map/ppermute | solution.py:294
  50.2 5.7 %collective-permute-start.4 = (f32[48,128]{1,0:T(8,128)S(1)}, f32[48,128]{1,0:T(8,128)S(1)}, u32[]{:S(2)}, u32[]{:S(2)}) collective-permute-start(f32[48,128]{1,0:T(8,128)S(1)} %dynamic-slice_bitcast_fusion.4), channel_id=1, source_target_pairs={{0,1},{1,0},{2,3},{3,2},{4,5},{5,4},{6,7},{7,6},{8,9},{9,8},{10,11... | collective-permute-start | bytes 73736 | tf_op jit(solution)/shard_map/ppermute | solution.py:294
  55.9 5.7 %collective-permute-start.5 = (f32[48,128]{1,0:T(8,128)S(1)}, f32[48,128]{1,0:T(8,128)S(1)}, u32[]{:S(2)}, u32[]{:S(2)}) collective-permute-start(f32[48,128]{1,0:T(8,128)S(1)} %bitcast_add_fusion.4.keep_ref), channel_id=1, source_target_pairs={{0,3},{1,2},{2,1},{3,0},{4,7},{5,6},{6,5},{7,4},{8,11},{9,10},{10,... | collective-permute-start | bytes 73736 | tf_op jit(solution)/shard_map/ppermute | solution.py:294
  62.4 24.4 %all-to-all-start.1 = ((f32[12,48,128]{2,1,0:T(8,128)}), f32[12,48,128]{2,1,0:T(8,128)S(1)}, u32[]{:S(2)}, u32[]{:S(2)}) async-start(f32[12,48,128]{2,1,0:T(8,128)} %get-tuple-element.22), calls=%async_computation.1 | async-start | bytes 589824 | tf_op jit(solution)/shard_map/all_to_all | solution.py:415
  71.5 19.2 %collective-permute-start.8 = (f32[384,128]{1,0:T(8,128)S(1)}, f32[384,128]{1,0:T(8,128)S(1)}, u32[]{:S(2)}, u32[]{:S(2)}) collective-permute-start(f32[384,128]{1,0:T(8,128)S(1)} %get-tuple-element.21.own_ref), channel_id=1, source_target_pairs={{0,3},{1,0},{2,1},{3,2},{4,7},{5,4},{6,5},{7,6},{8,11},{9,8},{10,9... | collective-permute-start | bytes 589832 | tf_op jit(solution)/shard_map/ppermute | solution.py:423
  74.0 16.8 %collective-permute-start.7 = (f32[384,128]{1,0:T(8,128)S(1)}, f32[384,128]{1,0:T(8,128)S(1)}, u32[]{:S(2)}, u32[]{:S(2)}) collective-permute-start(f32[384,128]{1,0:T(8,128)S(1)} %get-tuple-element.21.own_ref), channel_id=1, source_target_pairs={{0,2},{1,3},{2,0},{3,1},{4,6},{5,7},{6,4},{7,5},{8,10},{9,11},{10,... | collective-permute-start | bytes 589832 | tf_op jit(solution)/shard_map/ppermute | solution.py:423
  79.8 11.0 %collective-permute-start.6 = (f32[384,128]{1,0:T(8,128)S(1)}, f32[384,128]{1,0:T(8,128)S(1)}, u32[]{:S(2)}, u32[]{:S(2)}) collective-permute-start(f32[384,128]{1,0:T(8,128)S(1)} %get-tuple-element.21.own_ref), channel_id=1, source_target_pairs={{0,1},{1,2},{2,3},{3,0},{4,5},{5,6},{6,7},{7,4},{8,9},{9,10},{10,1... | collective-permute-start | bytes 589832 | tf_op jit(solution)/shard_map/ppermute | solution.py:423
  81.8 9.0 %copy-start = (s32[1,48]{1,0:T(1,128)S(1)}, s32[1,48]{1,0:T(1,128)}, u32[]{:S(2)}) copy-start(s32[1,48]{1,0:T(1,128)} %counts_ref.1) | copy-start | bytes 580
  86.8 9.1 %collective-permute-start.9 = (f32[48,128]{1,0:T(8,128)S(1)}, f32[48,128]{1,0:T(8,128)S(1)}, u32[]{:S(2)}, u32[]{:S(2)}) collective-permute-start(f32[48,128]{1,0:T(8,128)S(1)} %add_parts.1.mine_ref), channel_id=1, source_target_pairs={{0,1},{1,0},{2,3},{3,2},{4,5},{5,4},{6,7},{7,6},{8,9},{9,8},{10,11... | collective-permute-start | bytes 73736 | tf_op jit(solution)/shard_map/ppermute | solution.py:294

commit v5 on v4

--- a/solution.py
+++ b/solution.py
@@ -30,7 +30,7 @@
     return jnp.concatenate([high, low], axis=1)
 
 
-CHUNK = 256
+CHUNK = 512
 QUARTER = 24
 PART = NX * QUARTER
 
@@ -231,56 +231,91 @@
 STEP = 512
 
 
-def add_kernel(me_ref, counts_ref, got_ref, own_ref, late0_ref, late1_ref, late2_ref, table_ref, rows, dest):
-    groups = OWNERS // NX
-    for g in range(groups):
+def product(t, dest, rows):
+    table_row = (iota((STEP, E), 0) + (t * STEP + 1)).astype(jnp.float32)
+    hits = [
+        jnp.where(table_row == dest[0:1, k : k + 128], 1.0, 0.0).astype(jnp.bfloat16)
+        for k in range(0, OWNERS * BLOCK, 128)
+    ]
+    both = jnp.dot(jnp.concatenate(hits, axis=1), rows[...], preferred_element_type=jnp.float32)
+    return both[:, :E] + both[:, E:]
+
+
+SCATTER_SCRATCH = [
+    pltpu.VMEM((OWNERS * BLOCK, 2 * E), jnp.bfloat16),
+    pltpu.VMEM((8, OWNERS * BLOCK), jnp.float32),
+]
+SCATTER_COST = pl.CostEstimate(flops=2 * 2048 * 1536 * 256, bytes_accessed=2_500_000, transcendentals=0)
+
+
+def add_main_kernel(got_ref, table_ref, rows, dest):
+    for g in range(OWNERS // NX):
         rows[g * 128 : (g + 1) * 128, :] = split(got_ref[g * 128 : (g + 1) * 128, :])
         total = sum(got_ref[(NX * g + j) * BLOCK + HALF : (NX * g + j + 1) * BLOCK, :] for j in range(NX))
         dest[:, g * 128 : (g + 1) * 128] = jnp.broadcast_to(total[PIECE : PIECE + 1, :], (8, E))
-
-    def product(t):
-        table_row = (iota((STEP, E), 0) + (t * STEP + 1)).astype(jnp.float32)
-        hits = [
-            jnp.where(table_row == dest[0:1, g * 128 : (g + 1) * 128], 1.0, 0.0).astype(jnp.bfloat16)
-            for g in range(groups)
-        ]
-        both = jnp.dot(jnp.concatenate(hits, axis=1), rows[...], preferred_element_type=jnp.float32)
-        return both[:, :E] + both[:, E:]
-
     for t in range(ROWS_DEV // STEP):
-        table_ref[t * STEP : (t + 1) * STEP, :] = product(t)
-
+        table_ref[t * STEP : (t + 1) * STEP, :] = product(t, dest, rows)
+
+
+def add_main(got):
+    whole = pl.BlockSpec(memory_space=pltpu.VMEM)
+    return pl.pallas_call(
+        add_main_kernel,
+        out_shape=jax.ShapeDtypeStruct((ROWS_DEV, E), jnp.float32),
+        in_specs=[whole],
+        out_specs=whole,
+        scratch_shapes=SCATTER_SCRATCH,
+        compiler_params=pltpu.CompilerParams(vmem_limit_bytes=VMEM_LIMIT),
+        cost_estimate=SCATTER_COST,
+        name="add_main",
+    )(got)
+
+
+def add_late_kernel(
+    me_ref, counts_ref, table_in, own_in, late0_in, late1_in, late2_in, table_out,
+    table, late, rows, dest, sems,
+):
     @pl.when(counts_ref[0, me_ref[0]] > HALF)
     def _():
+        slabs = (own_in, late0_in, late1_in, late2_in)
+        fetches = [pltpu.make_async_copy(slabs[k], late.at[k], sems.at[k]) for k in range(NX)]
+        fetches.append(pltpu.make_async_copy(table_in, table, sems.at[NX]))
+        for fetch in fetches:
+            fetch.start()
+        for fetch in fetches:
+            fetch.wait()
         for k in range(NX):
             for g in range(3):
-                late = (own_ref, late0_ref, late1_ref, late2_ref)[k]
-                tiles = [late[t * 8 : t * 8 + 8, :] for t in range(16 * g, 16 * g + 16)]
+                tiles = [late[k, s * 8 : s * 8 + 8, :] for s in range(16 * g, 16 * g + 16)]
                 at = (k * 3 + g) * 128
                 rows[at : at + 128, :] = split(jnp.concatenate(tiles, axis=0))
                 dest[:, at : at + 128] = jnp.broadcast_to(sum(tiles)[7:8, :], (8, E))
         for t in range(ROWS_DEV // STEP):
-            table_ref[t * STEP : (t + 1) * STEP, :] += product(t)
-
-
-def add_rows(me, counts, got, late):
-    whole = pl.BlockSpec(memory_space=pltpu.VMEM)
+            table[t * STEP : (t + 1) * STEP, :] += product(t, dest, rows)
+        write = pltpu.make_async_copy(table, table_out, sems.at[NX])
+        write.start()
+        write.wait()
+
+
+def add_late(me, counts, table, late):
     scalar = pl.BlockSpec(memory_space=pltpu.SMEM)
-    return pl.pallas_call(
-        add_kernel,
+    anywhere = pl.BlockSpec(memory_space=pl.ANY)
+    return pl.pallas_call(
+        add_late_kernel,
         out_shape=jax.ShapeDtypeStruct((ROWS_DEV, E), jnp.float32),
-        in_specs=[scalar, scalar] + [whole] * 5,
-        out_specs=whole,
+        in_specs=[scalar, scalar] + [anywhere] * 5,
+        out_specs=anywhere,
         scratch_shapes=[
-            pltpu.VMEM((OWNERS * BLOCK, 2 * E), jnp.bfloat16),
-            pltpu.VMEM((8, OWNERS * BLOCK), jnp.float32),
-        ],
-        compiler_params=pltpu.CompilerParams(vmem_limit_bytes=VMEM_LIMIT),
-        cost_estimate=pl.CostEstimate(
-            flops=2 * 2048 * 1536 * 256, bytes_accessed=2_500_000, transcendentals=0
-        ),
-        name="add_rows",
-    )(me, counts, got, *late)
+            pltpu.VMEM((ROWS_DEV, E), jnp.float32),
+            pltpu.VMEM((NX, OWNERS * 8, E), jnp.float32),
+        ]
+        + SCATTER_SCRATCH
+        + [pltpu.SemaphoreType.DMA((NX + 1,))],
+        input_output_aliases={2: 0},
+        compiler_params=pltpu.CompilerParams(vmem_limit_bytes=VMEM_LIMIT),
+        cost_estimate=SCATTER_COST,
+        name="add_late",
+    )(me, counts, table, *late)
 
 
 GRP_SWAPS = (2, 1, 4, 14)
@@ -421,7 +456,7 @@
     for turn in (1, 2, 3):
         pairs = [(s, s // NX * NX + (s + turn) % NX) for s in range(OWNERS)]
         late.append(lax.ppermute(slab, "shard", pairs))
-    table = add_rows(me, block_counts, got, late)
+    table = add_late(me, block_counts, add_main(got), late)
     grad_w1, grad_b1, grad_w2, grad_b2, grad_w3 = final(jnp.stack([g, side]), total, other)
     return (
         table[None],

time: 97.7 us -> 97.1 us (level)
  the two profiles are of different devices: /device:TPU:60 before, /device:TPU:20 now
where the time goes in v5:
time: 97.1 us; the launch traced here: 96.5 us
  starting transfers between devices  61.2 us (63%)
  waiting for transfers between devices  17.6 us (18%)
  Pallas kernels  16.5 us (17%)
    ppermute x7, starting transfers between devices, swap(): return lax.ppermute(value, axis, [(i, i ^ bits) for i in range(size)])  23.4 us
    all_to_all x1, starting transfers between devices, shards(): got = lax.all_to_all(send, 'shard', split_axis=0, concat_axis=0, tiled=True)  18.5 us
    ppermute x7, waiting for transfers between devices, swap(): return lax.ppermute(value, axis, [(i, i ^ bits) for i in range(size)])  15.8 us
    ppermute x3, starting transfers between devices, shards(): late.append(lax.ppermute(slab, 'shard', pairs))  10.1 us
    all_to_all x1, starting transfers between devices, shards(): lax.all_to_all(copies, 'shard', split_axis=0, concat_axis=0, tiled=True,...  9.23 us
    pallas_call x1, Pallas kernels, add_late(): pl.pallas_call(add_late_kernel, out_shape=jax.ShapeDtypeStruct((ROWS_DEV,...  5.61 us
    pallas_call x1, Pallas kernels, dense(): pl.pallas_call(dense_kernel, out_shape=[jax.ShapeDtypeStruct((SLOTS, E),...  3.09 us
    pallas_call x1, Pallas kernels, pack(): pl.pallas_call(pack_kernel, out_shape=jax.ShapeDtypeStruct((OWNERS, BLOCK...  3 us
  transfers between devices with their start and end apart: 12, of which 7 were waited for; matrix products, arithmetic and copies ran while one was open for 0% of the time, Pallas kernels for 12%

profile of v5, /device:TPU:20, one launch (start us, length us, event | category | flops | bytes accessed | tf_op | source)
XLA Modules:
  0.0 96.5 jit_solution(14453994711361990618)
XLA Ops:
  0.7 3.1 %dense.1 = (f32[1024,128]{1,0:T(8,128)S(1)}, f32[1536,128]{1,0:T(8,128)S(1)}, s32[8,128]{1,0:T(8,128)S(1)}, s32[48,48]{1,0:T(8,128)S(1)}) custom-call(s32[8]{0:T(128)} %lengths_in.1, bf16[8,128]{1,0:T(8,128)(2,1)} %target_in.1, bf16[1024,128]{1,0:T(8,128)(2,1)} %bitcast.38, f32[8,128]{1,0:T(8,128)} %pg_in.1, bf16[512,256]{1,0:T(8,128)(2,1)} %w1_in.1, ...), custom_call_target="tpu_custom_call" | custom-call | flops 1100000000 | bytes 2200000 | tf_op jit(solution)/shard_map/dense/pallas_call | solution.py:128
  3.8 3.5 %collective-permute-start = (f32[2,2,2,2,48,128]{5,4,3,2,1,0:T(8,128)S(1)}, f32[2,2,2,2,48,128]{5,4,3,2,1,0:T(8,128)S(1)}, u32[]{:S(2)}, u32[]{:S(2)}) collective-permute-start(f32[2,2,2,2,48,128]{5,4,3,2,1,0:T(8,128)S(1)} %dynamic-slice_bitcast_fusion), channel_id=1, source_target_pairs={{0,96},{48,144},{96,0},{144,48},{192,288},{240,336},{288,192},{336... | collective-permute-start | bytes 1179656 | tf_op jit(solution)/shard_map/ppermute | solution.py:329
  7.3 3.0 %pack.1 = f32[48,32,128]{2,1,0:T(8,128)} custom-call(s32[1]{0:T(128)} %bitcast.me_ref, s32[1,48]{1,0:T(1,128)} %counts_ref.1, f32[1024,128]{1,0:T(8,128)S(1)} %get-tuple-element.17.drow_ref, s32[8,128]{1,0:T(8,128)S(1)} %get-tuple-element.18.ids_ref, s32[48,48]{1,0:T(8,128)S(1)} %get-tuple-element.19.blocks_ref), custom_call_target="tpu_custom_call" | custom-call | flops 1241513984 | bytes 2000000 | tf_op jit(solution)/shard_map/pack/pallas_call | solution.py:212
  10.3 18.5 %all-to-all-start = ((f32[48,32,128]{2,1,0:T(8,128)}), f32[48,32,128]{2,1,0:T(8,128)S(1)}, u32[]{:S(2)}, u32[]{:S(2)}) async-start(f32[48,32,128]{2,1,0:T(8,128)} %pack.1), calls=%async_computation | async-start | bytes 1572864 | tf_op jit(solution)/shard_map/all_to_all | solution.py:438
  28.8 0.0 collective-permute-done
  28.9 1.9 %collective-permute-start.1 = (f32[2,2,2,48,128]{4,3,2,1,0:T(8,128)S(1)}, f32[2,2,2,48,128]{4,3,2,1,0:T(8,128)S(1)}, u32[]{:S(2)}, u32[]{:S(2)}) collective-permute-start(f32[2,2,2,48,128]{4,3,2,1,0:T(8,128)S(1)} %dynamic-slice_bitcast_fusion.1), channel_id=1, source_target_pairs={{0,48},{48,0},{96,144},{144,96},{192,240},{240,192},{288,336},{336... | collective-permute-start | bytes 589832 | tf_op jit(solution)/shard_map/ppermute | solution.py:329
  30.8 1.4 %collective-permute-done.1 = f32[2,2,2,48,128]{4,3,2,1,0:T(8,128)S(1)} collective-permute-done((f32[2,2,2,48,128]{4,3,2,1,0:T(8,128)S(1)}, f32[2,2,2,48,128]{4,3,2,1,0:T(8,128)S(1)}, u32[]{:S(2)}, u32[]{:S(2)}) %collective-permute-start.1) | collective-permute-done | bytes 196640 | tf_op jit(solution)/shard_map/ppermute | solution.py:329
  32.3 2.2 %collective-permute-start.2 = (f32[2,2,48,128]{3,2,1,0:T(8,128)S(1)}, f32[2,2,48,128]{3,2,1,0:T(8,128)S(1)}, u32[]{:S(2)}, u32[]{:S(2)}) collective-permute-start(f32[2,2,48,128]{3,2,1,0:T(8,128)S(1)} %dynamic-slice_bitcast_fusion.2), channel_id=1, source_target_pairs={{0,192},{48,240},{96,288},{144,336},{192,0},{240,48},{288,96},{336... | collective-permute-start | bytes 294920 | tf_op jit(solution)/shard_map/ppermute | solution.py:329
  34.5 5.5 %collective-permute-done.2 = f32[2,2,48,128]{3,2,1,0:T(8,128)S(1)} collective-permute-done((f32[2,2,48,128]{3,2,1,0:T(8,128)S(1)}, f32[2,2,48,128]{3,2,1,0:T(8,128)S(1)}, u32[]{:S(2)}, u32[]{:S(2)}) %collective-permute-start.2) | collective-permute-done | bytes 98336 | tf_op jit(solution)/shard_map/ppermute | solution.py:329
  40.0 5.6 %collective-permute-start.3 = (f32[2,48,128]{2,1,0:T(8,128)S(1)}, f32[2,48,128]{2,1,0:T(8,128)S(1)}, u32[]{:S(2)}, u32[]{:S(2)}) collective-permute-start(f32[2,48,128]{2,1,0:T(8,128)S(1)} %dynamic-slice_bitcast_fusion.3), channel_id=1, source_target_pairs={{0,672},{48,720},{96,576},{144,624},{192,480},{240,528},{288,384},... | collective-permute-start | bytes 147464 | tf_op jit(solution)/shard_map/ppermute | solution.py:329
  45.6 3.4 %collective-permute-done.3 = f32[2,48,128]{2,1,0:T(8,128)S(1)} collective-permute-done((f32[2,48,128]{2,1,0:T(8,128)S(1)}, f32[2,48,128]{2,1,0:T(8,128)S(1)}, u32[]{:S(2)}, u32[]{:S(2)}) %collective-permute-start.3) | collective-permute-done | bytes 49184 | tf_op jit(solution)/shard_map/ppermute | solution.py:329
  49.1 3.1 %collective-permute-start.4 = (f32[48,128]{1,0:T(8,128)S(1)}, f32[48,128]{1,0:T(8,128)S(1)}, u32[]{:S(2)}, u32[]{:S(2)}) collective-permute-start(f32[48,128]{1,0:T(8,128)S(1)} %dynamic-slice_bitcast_fusion.4), channel_id=1, source_target_pairs={{0,1},{1,0},{2,3},{3,2},{4,5},{5,4},{6,7},{7,6},{8,9},{9,8},{10,11... | collective-permute-start | bytes 73736 | tf_op jit(solution)/shard_map/ppermute | solution.py:329
  52.2 2.6 %collective-permute-done.4 = f32[48,128]{1,0:T(8,128)S(1)} collective-permute-done((f32[48,128]{1,0:T(8,128)S(1)}, f32[48,128]{1,0:T(8,128)S(1)}, u32[]{:S(2)}, u32[]{:S(2)}) %collective-permute-start.4) | collective-permute-done | bytes 24608 | tf_op jit(solution)/shard_map/ppermute | solution.py:329
  54.8 2.8 %collective-permute-start.5 = (f32[48,128]{1,0:T(8,128)S(1)}, f32[48,128]{1,0:T(8,128)S(1)}, u32[]{:S(2)}, u32[]{:S(2)}) collective-permute-start(f32[48,128]{1,0:T(8,128)S(1)} %bitcast_add_fusion.4.keep_ref), channel_id=1, source_target_pairs={{0,3},{1,2},{2,1},{3,0},{4,7},{5,6},{6,5},{7,4},{8,11},{9,10},{10,... | collective-permute-start | bytes 73736 | tf_op jit(solution)/shard_map/ppermute | solution.py:329
  57.7 2.9 %collective-permute-done.5.there_ref = f32[48,128]{1,0:T(8,128)S(1)} collective-permute-done((f32[48,128]{1,0:T(8,128)S(1)}, f32[48,128]{1,0:T(8,128)S(1)}, u32[]{:S(2)}, u32[]{:S(2)}) %collective-permute-start.5) | collective-permute-done | bytes 24608 | tf_op jit(solution)/shard_map/ppermute | solution.py:329
  60.6 0.3 all-to-all-done
  60.9 0.7 join.1
  61.6 9.2 %all-to-all-start.1 = ((f32[12,48,128]{2,1,0:T(8,128)}), f32[12,48,128]{2,1,0:T(8,128)S(1)}, u32[]{:S(2)}, u32[]{:S(2)}) async-start(f32[12,48,128]{2,1,0:T(8,128)} %get-tuple-element.22), calls=%async_computation.1 | async-start | bytes 589824 | tf_op jit(solution)/shard_map/all_to_all | solution.py:450
  70.9 2.1 %collective-permute-start.8 = (f32[384,128]{1,0:T(8,128)S(1)}, f32[384,128]{1,0:T(8,128)S(1)}, u32[]{:S(2)}, u32[]{:S(2)}) collective-permute-start(f32[384,128]{1,0:T(8,128)S(1)} %get-tuple-element.21.own_in), channel_id=1, source_target_pairs={{0,3},{1,0},{2,1},{3,2},{4,7},{5,4},{6,5},{7,6},{8,11},{9,8},{10,9... | collective-permute-start | bytes 589832 | tf_op jit(solution)/shard_map/ppermute | solution.py:458
  72.9 5.8 %collective-permute-start.7 = (f32[384,128]{1,0:T(8,128)S(1)}, f32[384,128]{1,0:T(8,128)S(1)}, u32[]{:S(2)}, u32[]{:S(2)}) collective-permute-start(f32[384,128]{1,0:T(8,128)S(1)} %get-tuple-element.21.own_in), channel_id=1, source_target_pairs={{0,2},{1,3},{2,0},{3,1},{4,6},{5,7},{6,4},{7,5},{8,10},{9,11},{10,... | collective-permute-start | bytes 589832 | tf_op jit(solution)/shard_map/ppermute | solution.py:458
  78.8 2.2 %collective-permute-start.6 = (f32[384,128]{1,0:T(8,128)S(1)}, f32[384,128]{1,0:T(8,128)S(1)}, u32[]{:S(2)}, u32[]{:S(2)}) collective-permute-start(f32[384,128]{1,0:T(8,128)S(1)} %get-tuple-element.21.own_in), channel_id=1, source_target_pairs={{0,1},{1,2},{2,3},{3,0},{4,5},{5,6},{6,7},{7,4},{8,9},{9,10},{10,1... | collective-permute-start | bytes 589832 | tf_op jit(solution)/shard_map/ppermute | solution.py:458
  81.0 0.1 pad_add_fusion.place_ref
  81.1 2.8 %add_main.1.table_in = f32[2048,128]{1,0:T(8,128)} custom-call(f32[1536,128]{1,0:T(8,128)S(1)} %bitcast.35), custom_call_target="tpu_custom_call" | custom-call | flops 1610612736 | bytes 2500000 | tf_op jit(solution)/shard_map/add_main/pallas_call | solution.py:262
  83.9 1.5 %all-to-all-done.1.parts_ref = f32[12,48,128]{2,1,0:T(8,128)S(1)} async-done(((f32[12,48,128]{2,1,0:T(8,128)}), f32[12,48,128]{2,1,0:T(8,128)S(1)}, u32[]{:S(2)}, u32[]{:S(2)}) %all-to-all-start.1) | async-done | bytes 294944 | tf_op jit(solution)/shard_map/all_to_all | solution.py:450
  85.3 4.3 %collective-permute-start.9 = (f32[48,128]{1,0:T(8,128)S(1)}, f32[48,128]{1,0:T(8,128)S(1)}, u32[]{:S(2)}, u32[]{:S(2)}) collective-permute-start(f32[48,128]{1,0:T(8,128)S(1)} %add_parts.1.mine_ref), channel_id=1, source_target_pairs={{0,1},{1,0},{2,3},{3,2},{4,5},{5,4},{6,7},{7,6},{8,9},{9,8},{10,11... | collective-permute-start | bytes 73736 | tf_op jit(solution)/shard_map/ppermute | solution.py:329
  89.6 0.0 collective-permute-done.8.late2_in
  89.6 0.0 collective-permute-done.7.late1_in
  89.6 0.0 collective-permute-done.6.late0_in
  89.6 0.0 copy-done
  89.6 5.6 %add_late.1 = f32[2048,128]{1,0:T(8,128)} custom-call(s32[1]{0:T(128)} %bitcast.me_ref, s32[1,48]{1,0:T(1,128)S(1)} %copy-done, f32[2048,128]{1,0:T(8,128)} %add_main.1.table_in, f32[384,128]{1,0:T(8,128)S(1)} %get-tuple-element.21.own_in, f32[384,128]{1,0:T(8,128)S(1)} %collective-permute-done.6.late0_in, ...), custom_call_target="tpu_custom_call", output_to_operand_aliasing={{}: (2, {})} | custom-call | flops 1610612736 | bytes 2500000 | tf_op jit(solution)/shard_map/add_late/pallas_call | solution.py:303
  95.3 0.0 collective-permute-done.9.other_ref
  95.3 1.2 %final.1 = (f32[32,256]{1,0:T(8,128)}, f32[1,16]{1,0:T(1,128)}, f32[16,128]{1,0:T(8,128)}, f32[1,8]{1,0:T(1,128)}, f32[1,8]{1,0:T(1,128)}) custom-call(s32[2]{0:T(128)S(1)} %pad_add_fusion.place_ref, f32[48,128]{1,0:T(8,128)S(1)} %add_parts.1.mine_ref, f32[48,128]{1,0:T(8,128)S(1)} %collective-permute-done.9.other_ref), custom_call_target="tpu_custom_call" | custom-call | flops 1024 | bytes 100000 | tf_op jit(solution)/shard_map/final/pallas_call | solution.py:397
  (12 shorter events, 0.2 us)
Async XLA Ops:
  3.8 25.0 %collective-permute-start = (f32[2,2,2,2,48,128]{5,4,3,2,1,0:T(8,128)S(1)}, f32[2,2,2,2,48,128]{5,4,3,2,1,0:T(8,128)S(1)}, u32[]{:S(2)}, u32[]{:S(2)}) collective-permute-start(f32[2,2,2,2,48,128]{5,4,3,2,1,0:T(8,128)S(1)} %dynamic-slice_bitcast_fusion), channel_id=1, source_target_pairs={{0,96},{48,144},{96,0},{144,48},{192,288},{240,336},{288,192},{336... | collective-permute-start | bytes 1179656 | tf_op jit(solution)/shard_map/ppermute | solution.py:329
  10.3 50.6 %all-to-all-start = ((f32[48,32,128]{2,1,0:T(8,128)}), f32[48,32,128]{2,1,0:T(8,128)S(1)}, u32[]{:S(2)}, u32[]{:S(2)}) async-start(f32[48,32,128]{2,1,0:T(8,128)} %pack.1), calls=%async_computation | async-start | bytes 1572864 | tf_op jit(solution)/shard_map/all_to_all | solution.py:438
  28.9 3.3 %collective-permute-start.1 = (f32[2,2,2,48,128]{4,3,2,1,0:T(8,128)S(1)}, f32[2,2,2,48,128]{4,3,2,1,0:T(8,128)S(1)}, u32[]{:S(2)}, u32[]{:S(2)}) collective-permute-start(f32[2,2,2,48,128]{4,3,2,1,0:T(8,128)S(1)} %dynamic-slice_bitcast_fusion.1), channel_id=1, source_target_pairs={{0,48},{48,0},{96,144},{144,96},{192,240},{240,192},{288,336},{336... | collective-permute-start | bytes 589832 | tf_op jit(solution)/shard_map/ppermute | solution.py:329
  32.3 7.7 %collective-permute-start.2 = (f32[2,2,48,128]{3,2,1,0:T(8,128)S(1)}, f32[2,2,48,128]{3,2,1,0:T(8,128)S(1)}, u32[]{:S(2)}, u32[]{:S(2)}) collective-permute-start(f32[2,2,48,128]{3,2,1,0:T(8,128)S(1)} %dynamic-slice_bitcast_fusion.2), channel_id=1, source_target_pairs={{0,192},{48,240},{96,288},{144,336},{192,0},{240,48},{288,96},{336... | collective-permute-start | bytes 294920 | tf_op jit(solution)/shard_map/ppermute | solution.py:329
  40.0 9.0 %collective-permute-start.3 = (f32[2,48,128]{2,1,0:T(8,128)S(1)}, f32[2,48,128]{2,1,0:T(8,128)S(1)}, u32[]{:S(2)}, u32[]{:S(2)}) collective-permute-start(f32[2,48,128]{2,1,0:T(8,128)S(1)} %dynamic-slice_bitcast_fusion.3), channel_id=1, source_target_pairs={{0,672},{48,720},{96,576},{144,624},{192,480},{240,528},{288,384},... | collective-permute-start | bytes 147464 | tf_op jit(solution)/shard_map/ppermute | solution.py:329
  49.1 5.7 %collective-permute-start.4 = (f32[48,128]{1,0:T(8,128)S(1)}, f32[48,128]{1,0:T(8,128)S(1)}, u32[]{:S(2)}, u32[]{:S(2)}) collective-permute-start(f32[48,128]{1,0:T(8,128)S(1)} %dynamic-slice_bitcast_fusion.4), channel_id=1, source_target_pairs={{0,1},{1,0},{2,3},{3,2},{4,5},{5,4},{6,7},{7,6},{8,9},{9,8},{10,11... | collective-permute-start | bytes 73736 | tf_op jit(solution)/shard_map/ppermute | solution.py:329
  54.8 5.7 %collective-permute-start.5 = (f32[48,128]{1,0:T(8,128)S(1)}, f32[48,128]{1,0:T(8,128)S(1)}, u32[]{:S(2)}, u32[]{:S(2)}) collective-permute-start(f32[48,128]{1,0:T(8,128)S(1)} %bitcast_add_fusion.4.keep_ref), channel_id=1, source_target_pairs={{0,3},{1,2},{2,1},{3,0},{4,7},{5,6},{6,5},{7,4},{8,11},{9,10},{10,... | collective-permute-start | bytes 73736 | tf_op jit(solution)/shard_map/ppermute | solution.py:329
  61.6 23.7 %all-to-all-start.1 = ((f32[12,48,128]{2,1,0:T(8,128)}), f32[12,48,128]{2,1,0:T(8,128)S(1)}, u32[]{:S(2)}, u32[]{:S(2)}) async-start(f32[12,48,128]{2,1,0:T(8,128)} %get-tuple-element.22), calls=%async_computation.1 | async-start | bytes 589824 | tf_op jit(solution)/shard_map/all_to_all | solution.py:450
  70.9 18.8 %collective-permute-start.8 = (f32[384,128]{1,0:T(8,128)S(1)}, f32[384,128]{1,0:T(8,128)S(1)}, u32[]{:S(2)}, u32[]{:S(2)}) collective-permute-start(f32[384,128]{1,0:T(8,128)S(1)} %get-tuple-element.21.own_in), channel_id=1, source_target_pairs={{0,3},{1,0},{2,1},{3,2},{4,7},{5,4},{6,5},{7,6},{8,11},{9,8},{10,9... | collective-permute-start | bytes 589832 | tf_op jit(solution)/shard_map/ppermute | solution.py:458
  72.9 16.7 %collective-permute-start.7 = (f32[384,128]{1,0:T(8,128)S(1)}, f32[384,128]{1,0:T(8,128)S(1)}, u32[]{:S(2)}, u32[]{:S(2)}) collective-permute-start(f32[384,128]{1,0:T(8,128)S(1)} %get-tuple-element.21.own_in), channel_id=1, source_target_pairs={{0,2},{1,3},{2,0},{3,1},{4,6},{5,7},{6,4},{7,5},{8,10},{9,11},{10,... | collective-permute-start | bytes 589832 | tf_op jit(solution)/shard_map/ppermute | solution.py:458
  78.8 10.9 %collective-permute-start.6 = (f32[384,128]{1,0:T(8,128)S(1)}, f32[384,128]{1,0:T(8,128)S(1)}, u32[]{:S(2)}, u32[]{:S(2)}) collective-permute-start(f32[384,128]{1,0:T(8,128)S(1)} %get-tuple-element.21.own_in), channel_id=1, source_target_pairs={{0,1},{1,2},{2,3},{3,0},{4,5},{5,6},{6,7},{7,4},{8,9},{9,10},{10,1... | collective-permute-start | bytes 589832 | tf_op jit(solution)/shard_map/ppermute | solution.py:458
  83.8 5.8 %copy-start = (s32[1,48]{1,0:T(1,128)S(1)}, s32[1,48]{1,0:T(1,128)}, u32[]{:S(2)}) copy-start(s32[1,48]{1,0:T(1,128)} %counts_ref.1) | copy-start | bytes 580
  85.3 9.9 %collective-permute-start.9 = (f32[48,128]{1,0:T(8,128)S(1)}, f32[48,128]{1,0:T(8,128)S(1)}, u32[]{:S(2)}, u32[]{:S(2)}) collective-permute-start(f32[48,128]{1,0:T(8,128)S(1)} %add_parts.1.mine_ref), channel_id=1, source_target_pairs={{0,1},{1,0},{2,3},{3,2},{4,5},{5,4},{6,7},{7,6},{8,9},{9,8},{10,11... | collective-permute-start | bytes 73736 | tf_op jit(solution)/shard_map/ppermute | solution.py:329

commit v6 on v5

--- a/solution.py
+++ b/solution.py
@@ -32,6 +32,7 @@
 
 CHUNK = 512
 QUARTER = 24
+SIDE = 2 * QUARTER
 PART = NX * QUARTER
 
 
@@ -39,12 +40,9 @@
     return 0.5 * jnp.tanh(0.5 * z) + 0.5
 
 
-def places():
-    at = []
-    for g in range(16):
-        core, y0, y1, y2 = g & 1, (g >> 1) & 1, (g >> 2) & 1, (g >> 3) & 1
-        at.append((y0 ^ y2) * 8 + core * 4 + (y1 ^ y2) * 2 + y2)
-    return at
+def place(g, side):
+    core, y0, y1, y2 = g & 1, (g >> 1) & 1, (g >> 2) & 1, (g >> 3) & 1
+    return y0 * 16 + core * 8 + side * 4 + (y1 ^ y2) * 2 + y2
 
 
 def dense_kernel(
@@ -110,9 +108,9 @@
     sub = iota((8, E), 0)
     small = jnp.where(sub == 0, grad_b1[:, :E], jnp.where(sub == 1, grad_b1[:, E:], 0.0))
     small = jnp.where(sub == 2, grad_b2, jnp.where(sub == 3, grad_w3, small))
-    for g, at in enumerate(places()):
+    for g in range(16):
         for k in range(NX):
-            base = at * PART + k * QUARTER
+            base = place(g, k // 2) * SIDE + (k % 2) * QUARTER
             top = 32 * g + 16 * (k % 2)
             side = E * (k // 2)
             part_ref[base : base + 16, :] = grad_w1[top : top + 16, side : side + E]
@@ -318,8 +316,7 @@
     )(me, counts, table, *late)
 
 
-GRP_SWAPS = (2, 1, 4, 14)
-SIDE = 2 * QUARTER
+STEPS = (("grp", 2), ("grp", 1), ("shard", 1), ("grp", 4), ("grp", 12))
 NZ = OWNERS // NX
 Z_GROUPS = [[z * NX + x for z in range(NZ)] for x in range(NX)]
 
@@ -373,8 +370,8 @@
     )(parts)
 
 
-def final_kernel(place_ref, mine_ref, other_ref, w1_ref, b1_ref, w2_ref, b2_ref, w3_ref):
-    g, first = place_ref[0], place_ref[1] == 0
+def final_kernel(g_ref, side_ref, mine_ref, other_ref, w1_ref, b1_ref, w2_ref, b2_ref, w3_ref):
+    g, first = g_ref[0], side_ref[0] == 0
     mine, other = mine_ref[...], other_ref[...]
     low, high = jnp.where(first, mine, other), jnp.where(first, other, mine)
     quarters = [low[:QUARTER], low[QUARTER:], high[:QUARTER], high[QUARTER:]]
@@ -391,18 +388,18 @@
     w3_ref[...] = by8[3:4, :8]
 
 
-def final(place, mine, other):
+def final(g, side, mine, other):
     whole = pl.BlockSpec(memory_space=pltpu.VMEM)
     shapes = ((32, 2 * E), (1, 16), (16, E), (1, 8), (1, 8))
     return pl.pallas_call(
         final_kernel,
         out_shape=[jax.ShapeDtypeStruct(shape, jnp.float32) for shape in shapes],
-        in_specs=[pl.BlockSpec(memory_space=pltpu.SMEM), whole, whole],
+        in_specs=[pl.BlockSpec(memory_space=pltpu.SMEM)] * 2 + [whole, whole],
         out_specs=[whole] * 5,
         compiler_params=pltpu.CompilerParams(vmem_limit_bytes=VMEM_LIMIT),
         cost_estimate=pl.CostEstimate(flops=1024, bytes_accessed=100_000, transcendentals=0),
         name="final",
-    )(place, mine, other)
+    )(g, side, mine, other)
 
 
 def shards(
@@ -441,8 +438,8 @@
     part = part.reshape(2, 2, 2, 2, 2, SIDE, E)
     y2 = (g >> 3) & 1
     side = (me[0] ^ (me[0] >> 1)) & 1
-    bits = (((g >> 1) & 1) ^ y2, g & 1, ((g >> 2) & 1) ^ y2, y2, side)
-    for bit, (axis, k) in zip(bits, [("grp", k) for k in GRP_SWAPS] + [("shard", 1)]):
+    bits = ((g >> 1) & 1, g & 1, side, ((g >> 2) & 1) ^ y2, y2)
+    for bit, (axis, k) in zip(bits, STEPS):
         keep = lax.dynamic_index_in_dim(part, bit, 0, False)
         away = lax.dynamic_index_in_dim(part, 1 - bit, 0, False)
         part = keep + swap(away, axis, k)
@@ -457,7 +454,7 @@
         pairs = [(s, s // NX * NX + (s + turn) % NX) for s in range(OWNERS)]
         late.append(lax.ppermute(slab, "shard", pairs))
     table = add_late(me, block_counts, add_main(got), late)
-    grad_w1, grad_b1, grad_w2, grad_b2, grad_w3 = final(jnp.stack([g, side]), total, other)
+    grad_w1, grad_b1, grad_w2, grad_b2, grad_w3 = final(g.reshape(1), side.reshape(1), total, other)
     return (
         table[None],
         grad_w1,

time: 97.1 us -> 94.8 us (0.976)
  the two profiles are of different devices: /device:TPU:20 before, /device:TPU:6 now
where the time goes in v6:
time: 94.8 us; the launch traced here: 93.3 us
  starting transfers between devices  57.6 us (61%)
  waiting for transfers between devices  23.6 us (25%)
  Pallas kernels  10.9 us (11%)
    ppermute x7, starting transfers between devices, swap(): return lax.ppermute(value, axis, [(i, i ^ bits) for i in range(size)])  21.5 us
    ppermute x7, waiting for transfers between devices, swap(): return lax.ppermute(value, axis, [(i, i ^ bits) for i in range(size)])  20.6 us
    all_to_all x1, starting transfers between devices, shards(): got = lax.all_to_all(send, 'shard', split_axis=0, concat_axis=0, tiled=True)  18.4 us
    ppermute x3, starting transfers between devices, shards(): late.append(lax.ppermute(slab, 'shard', pairs))  8.97 us
    all_to_all x1, starting transfers between devices, shards(): lax.all_to_all(copies, 'shard', split_axis=0, concat_axis=0, tiled=True,...  8.72 us
    pallas_call x1, Pallas kernels, dense(): pl.pallas_call(dense_kernel, out_shape=[jax.ShapeDtypeStruct((SLOTS, E),...  3.1 us
    all_to_all x1, waiting for transfers between devices, shards(): lax.all_to_all(copies, 'shard', split_axis=0, concat_axis=0, tiled=True,...  3.02 us
    pallas_call x1, Pallas kernels, pack(): pl.pallas_call(pack_kernel, out_shape=jax.ShapeDtypeStruct((OWNERS, BLOCK...  3 us
  transfers between devices with their start and end apart: 12, of which 7 were waited for; matrix products, arithmetic and copies ran while one was open for 0% of the time, Pallas kernels for 7%

profile of v6, /device:TPU:6, one launch (start us, length us, event | category | flops | bytes accessed | tf_op | source)
XLA Modules:
  0.0 93.3 jit_solution(7034876626607951008)
XLA Ops:
  0.6 3.1 %dense.1 = (f32[1024,128]{1,0:T(8,128)S(1)}, f32[1536,128]{1,0:T(8,128)S(1)}, s32[8,128]{1,0:T(8,128)S(1)}, s32[48,48]{1,0:T(8,128)S(1)}) custom-call(s32[8]{0:T(128)} %lengths_in.1, bf16[8,128]{1,0:T(8,128)(2,1)} %target_in.1, bf16[1024,128]{1,0:T(8,128)(2,1)} %bitcast.38, f32[8,128]{1,0:T(8,128)} %pg_in.1, bf16[512,256]{1,0:T(8,128)(2,1)} %w1_in.1, ...), custom_call_target="tpu_custom_call" | custom-call | flops 1100000000 | bytes 2200000 | tf_op jit(solution)/shard_map/dense/pallas_call | solution.py:126
  3.8 3.5 %collective-permute-start = (f32[2,2,2,2,48,128]{5,4,3,2,1,0:T(8,128)S(1)}, f32[2,2,2,2,48,128]{5,4,3,2,1,0:T(8,128)S(1)}, u32[]{:S(2)}, u32[]{:S(2)}) collective-permute-start(f32[2,2,2,2,48,128]{5,4,3,2,1,0:T(8,128)S(1)} %dynamic-slice_bitcast_fusion), channel_id=1, source_target_pairs={{0,96},{48,144},{96,0},{144,48},{192,288},{240,336},{288,192},{336... | collective-permute-start | bytes 1179656 | tf_op jit(solution)/shard_map/ppermute | solution.py:326
  7.3 3.0 %pack.1 = f32[48,32,128]{2,1,0:T(8,128)} custom-call(s32[1]{0:T(128)} %bitcast.me_ref, s32[1,48]{1,0:T(1,128)} %counts_ref.1, f32[1024,128]{1,0:T(8,128)S(1)} %get-tuple-element.17.drow_ref, s32[8,128]{1,0:T(8,128)S(1)} %get-tuple-element.18.ids_ref, s32[48,48]{1,0:T(8,128)S(1)} %get-tuple-element.19.blocks_ref), custom_call_target="tpu_custom_call" | custom-call | flops 1241513984 | bytes 2000000 | tf_op jit(solution)/shard_map/pack/pallas_call | solution.py:210
  10.3 18.4 %all-to-all-start = ((f32[48,32,128]{2,1,0:T(8,128)}), f32[48,32,128]{2,1,0:T(8,128)S(1)}, u32[]{:S(2)}, u32[]{:S(2)}) async-start(f32[48,32,128]{2,1,0:T(8,128)} %pack.1), calls=%async_computation | async-start | bytes 1572864 | tf_op jit(solution)/shard_map/all_to_all | solution.py:435
  28.7 0.0 collective-permute-done
  28.8 1.9 %collective-permute-start.1 = (f32[2,2,2,48,128]{4,3,2,1,0:T(8,128)S(1)}, f32[2,2,2,48,128]{4,3,2,1,0:T(8,128)S(1)}, u32[]{:S(2)}, u32[]{:S(2)}) collective-permute-start(f32[2,2,2,48,128]{4,3,2,1,0:T(8,128)S(1)} %dynamic-slice_bitcast_fusion.1), channel_id=1, source_target_pairs={{0,48},{48,0},{96,144},{144,96},{192,240},{240,192},{288,336},{336... | collective-permute-start | bytes 589832 | tf_op jit(solution)/shard_map/ppermute | solution.py:326
  30.8 1.4 %collective-permute-done.1 = f32[2,2,2,48,128]{4,3,2,1,0:T(8,128)S(1)} collective-permute-done((f32[2,2,2,48,128]{4,3,2,1,0:T(8,128)S(1)}, f32[2,2,2,48,128]{4,3,2,1,0:T(8,128)S(1)}, u32[]{:S(2)}, u32[]{:S(2)}) %collective-permute-start.1) | collective-permute-done | bytes 196640 | tf_op jit(solution)/shard_map/ppermute | solution.py:326
  32.2 2.8 %collective-permute-start.2 = (f32[2,2,48,128]{3,2,1,0:T(8,128)S(1)}, f32[2,2,48,128]{3,2,1,0:T(8,128)S(1)}, u32[]{:S(2)}, u32[]{:S(2)}) collective-permute-start(f32[2,2,48,128]{3,2,1,0:T(8,128)S(1)} %dynamic-slice_bitcast_fusion.2), channel_id=1, source_target_pairs={{0,1},{1,0},{2,3},{3,2},{4,5},{5,4},{6,7},{7,6},{8,9},{9,8},{10,11... | collective-permute-start | bytes 294920 | tf_op jit(solution)/shard_map/ppermute | solution.py:326
  35.0 5.4 %collective-permute-done.2 = f32[2,2,48,128]{3,2,1,0:T(8,128)S(1)} collective-permute-done((f32[2,2,48,128]{3,2,1,0:T(8,128)S(1)}, f32[2,2,48,128]{3,2,1,0:T(8,128)S(1)}, u32[]{:S(2)}, u32[]{:S(2)}) %collective-permute-start.2) | collective-permute-done | bytes 98336 | tf_op jit(solution)/shard_map/ppermute | solution.py:326
  40.5 4.5 %collective-permute-start.3 = (f32[2,48,128]{2,1,0:T(8,128)S(1)}, f32[2,48,128]{2,1,0:T(8,128)S(1)}, u32[]{:S(2)}, u32[]{:S(2)}) collective-permute-start(f32[2,48,128]{2,1,0:T(8,128)S(1)} %dynamic-slice_bitcast_fusion.3), channel_id=1, source_target_pairs={{0,192},{48,240},{96,288},{144,336},{192,0},{240,48},{288,96},{336... | collective-permute-start | bytes 147464 | tf_op jit(solution)/shard_map/ppermute | solution.py:326
  45.0 2.8 %collective-permute-done.3 = f32[2,48,128]{2,1,0:T(8,128)S(1)} collective-permute-done((f32[2,48,128]{2,1,0:T(8,128)S(1)}, f32[2,48,128]{2,1,0:T(8,128)S(1)}, u32[]{:S(2)}, u32[]{:S(2)}) %collective-permute-start.3) | collective-permute-done | bytes 49184 | tf_op jit(solution)/shard_map/ppermute | solution.py:326
  47.8 5.0 %collective-permute-start.4 = (f32[48,128]{1,0:T(8,128)S(1)}, f32[48,128]{1,0:T(8,128)S(1)}, u32[]{:S(2)}, u32[]{:S(2)}) collective-permute-start(f32[48,128]{1,0:T(8,128)S(1)} %dynamic-slice_bitcast_fusion.4), channel_id=1, source_target_pairs={{0,576},{48,624},{96,672},{144,720},{192,384},{240,432},{288,480},... | collective-permute-start | bytes 73736 | tf_op jit(solution)/shard_map/ppermute | solution.py:326
  52.8 2.9 %collective-permute-done.4 = f32[48,128]{1,0:T(8,128)S(1)} collective-permute-done((f32[48,128]{1,0:T(8,128)S(1)}, f32[48,128]{1,0:T(8,128)S(1)}, u32[]{:S(2)}, u32[]{:S(2)}) %collective-permute-start.4) | collective-permute-done | bytes 24608 | tf_op jit(solution)/shard_map/ppermute | solution.py:326
  55.7 1.9 %collective-permute-start.5 = (f32[48,128]{1,0:T(8,128)S(1)}, f32[48,128]{1,0:T(8,128)S(1)}, u32[]{:S(2)}, u32[]{:S(2)}) collective-permute-start(f32[48,128]{1,0:T(8,128)S(1)} %bitcast_add_fusion.4.keep_ref), channel_id=1, source_target_pairs={{0,3},{1,2},{2,1},{3,0},{4,7},{5,6},{6,5},{7,4},{8,11},{9,10},{10,... | collective-permute-start | bytes 73736 | tf_op jit(solution)/shard_map/ppermute | solution.py:326
  57.6 5.0 %collective-permute-done.5.there_ref = f32[48,128]{1,0:T(8,128)S(1)} collective-permute-done((f32[48,128]{1,0:T(8,128)S(1)}, f32[48,128]{1,0:T(8,128)S(1)}, u32[]{:S(2)}, u32[]{:S(2)}) %collective-permute-start.5) | collective-permute-done | bytes 24608 | tf_op jit(solution)/shard_map/ppermute | solution.py:326
  62.6 0.0 all-to-all-done
  62.6 0.7 join.1
  63.3 8.7 %all-to-all-start.1 = ((f32[12,48,128]{2,1,0:T(8,128)}), f32[12,48,128]{2,1,0:T(8,128)S(1)}, u32[]{:S(2)}, u32[]{:S(2)}) async-start(f32[12,48,128]{2,1,0:T(8,128)} %get-tuple-element.22), calls=%async_computation.1 | async-start | bytes 589824 | tf_op jit(solution)/shard_map/all_to_all | solution.py:447
  72.0 1.9 %collective-permute-start.8 = (f32[384,128]{1,0:T(8,128)S(1)}, f32[384,128]{1,0:T(8,128)S(1)}, u32[]{:S(2)}, u32[]{:S(2)}) collective-permute-start(f32[384,128]{1,0:T(8,128)S(1)} %get-tuple-element.21.own_in), channel_id=1, source_target_pairs={{0,3},{1,0},{2,1},{3,2},{4,7},{5,4},{6,5},{7,6},{8,11},{9,8},{10,9... | collective-permute-start | bytes 589832 | tf_op jit(solution)/shard_map/ppermute | solution.py:455
  74.0 4.1 %collective-permute-start.7 = (f32[384,128]{1,0:T(8,128)S(1)}, f32[384,128]{1,0:T(8,128)S(1)}, u32[]{:S(2)}, u32[]{:S(2)}) collective-permute-start(f32[384,128]{1,0:T(8,128)S(1)} %get-tuple-element.21.own_in), channel_id=1, source_target_pairs={{0,2},{1,3},{2,0},{3,1},{4,6},{5,7},{6,4},{7,5},{8,10},{9,11},{10,... | collective-permute-start | bytes 589832 | tf_op jit(solution)/shard_map/ppermute | solution.py:455
  78.1 3.0 %collective-permute-start.6 = (f32[384,128]{1,0:T(8,128)S(1)}, f32[384,128]{1,0:T(8,128)S(1)}, u32[]{:S(2)}, u32[]{:S(2)}) collective-permute-start(f32[384,128]{1,0:T(8,128)S(1)} %get-tuple-element.21.own_in), channel_id=1, source_target_pairs={{0,1},{1,2},{2,3},{3,0},{4,5},{5,6},{6,7},{7,4},{8,9},{9,10},{10,1... | collective-permute-start | bytes 589832 | tf_op jit(solution)/shard_map/ppermute | solution.py:455
  81.0 2.8 %add_main.1.table_in = f32[2048,128]{1,0:T(8,128)} custom-call(f32[1536,128]{1,0:T(8,128)S(1)} %bitcast.35), custom_call_target="tpu_custom_call" | custom-call | flops 1610612736 | bytes 2500000 | tf_op jit(solution)/shard_map/add_main/pallas_call | solution.py:260
  83.8 0.0 copy-start
  83.8 3.0 %all-to-all-done.1.parts_ref = f32[12,48,128]{2,1,0:T(8,128)S(1)} async-done(((f32[12,48,128]{2,1,0:T(8,128)}), f32[12,48,128]{2,1,0:T(8,128)S(1)}, u32[]{:S(2)}, u32[]{:S(2)}) %all-to-all-start.1) | async-done | bytes 294944 | tf_op jit(solution)/shard_map/all_to_all | solution.py:447
  86.9 1.9 %collective-permute-start.9 = (f32[48,128]{1,0:T(8,128)S(1)}, f32[48,128]{1,0:T(8,128)S(1)}, u32[]{:S(2)}, u32[]{:S(2)}) collective-permute-start(f32[48,128]{1,0:T(8,128)S(1)} %add_parts.1.mine_ref), channel_id=1, source_target_pairs={{0,1},{1,0},{2,3},{3,2},{4,5},{5,4},{6,7},{7,6},{8,9},{9,8},{10,11... | collective-permute-start | bytes 73736 | tf_op jit(solution)/shard_map/ppermute | solution.py:326
  88.8 0.0 collective-permute-done.8.late2_in
  88.8 0.0 collective-permute-done.7.late1_in
  88.8 0.0 collective-permute-done.6.late0_in
  88.8 0.0 copy-done
  88.8 0.6 add_late.1
  89.4 3.1 %collective-permute-done.9.other_ref = f32[48,128]{1,0:T(8,128)S(1)} collective-permute-done((f32[48,128]{1,0:T(8,128)S(1)}, f32[48,128]{1,0:T(8,128)S(1)}, u32[]{:S(2)}, u32[]{:S(2)}) %collective-permute-start.9) | collective-permute-done | bytes 24608 | tf_op jit(solution)/shard_map/ppermute | solution.py:326
  92.6 0.7 final.1
  (11 shorter events, 0.2 us)
Async XLA Ops:
  3.8 25.0 %collective-permute-start = (f32[2,2,2,2,48,128]{5,4,3,2,1,0:T(8,128)S(1)}, f32[2,2,2,2,48,128]{5,4,3,2,1,0:T(8,128)S(1)}, u32[]{:S(2)}, u32[]{:S(2)}) collective-permute-start(f32[2,2,2,2,48,128]{5,4,3,2,1,0:T(8,128)S(1)} %dynamic-slice_bitcast_fusion), channel_id=1, source_target_pairs={{0,96},{48,144},{96,0},{144,48},{192,288},{240,336},{288,192},{336... | collective-permute-start | bytes 1179656 | tf_op jit(solution)/shard_map/ppermute | solution.py:326
  10.3 52.3 %all-to-all-start = ((f32[48,32,128]{2,1,0:T(8,128)}), f32[48,32,128]{2,1,0:T(8,128)S(1)}, u32[]{:S(2)}, u32[]{:S(2)}) async-start(f32[48,32,128]{2,1,0:T(8,128)} %pack.1), calls=%async_computation | async-start | bytes 1572864 | tf_op jit(solution)/shard_map/all_to_all | solution.py:435
  28.8 3.3 %collective-permute-start.1 = (f32[2,2,2,48,128]{4,3,2,1,0:T(8,128)S(1)}, f32[2,2,2,48,128]{4,3,2,1,0:T(8,128)S(1)}, u32[]{:S(2)}, u32[]{:S(2)}) collective-permute-start(f32[2,2,2,48,128]{4,3,2,1,0:T(8,128)S(1)} %dynamic-slice_bitcast_fusion.1), channel_id=1, source_target_pairs={{0,48},{48,0},{96,144},{144,96},{192,240},{240,192},{288,336},{336... | collective-permute-start | bytes 589832 | tf_op jit(solution)/shard_map/ppermute | solution.py:326
  32.2 8.2 %collective-permute-start.2 = (f32[2,2,48,128]{3,2,1,0:T(8,128)S(1)}, f32[2,2,48,128]{3,2,1,0:T(8,128)S(1)}, u32[]{:S(2)}, u32[]{:S(2)}) collective-permute-start(f32[2,2,48,128]{3,2,1,0:T(8,128)S(1)} %dynamic-slice_bitcast_fusion.2), channel_id=1, source_target_pairs={{0,1},{1,0},{2,3},{3,2},{4,5},{5,4},{6,7},{7,6},{8,9},{9,8},{10,11... | collective-permute-start | bytes 294920 | tf_op jit(solution)/shard_map/ppermute | solution.py:326
  40.5 7.3 %collective-permute-start.3 = (f32[2,48,128]{2,1,0:T(8,128)S(1)}, f32[2,48,128]{2,1,0:T(8,128)S(1)}, u32[]{:S(2)}, u32[]{:S(2)}) collective-permute-start(f32[2,48,128]{2,1,0:T(8,128)S(1)} %dynamic-slice_bitcast_fusion.3), channel_id=1, source_target_pairs={{0,192},{48,240},{96,288},{144,336},{192,0},{240,48},{288,96},{336... | collective-permute-start | bytes 147464 | tf_op jit(solution)/shard_map/ppermute | solution.py:326
  47.8 7.8 %collective-permute-start.4 = (f32[48,128]{1,0:T(8,128)S(1)}, f32[48,128]{1,0:T(8,128)S(1)}, u32[]{:S(2)}, u32[]{:S(2)}) collective-permute-start(f32[48,128]{1,0:T(8,128)S(1)} %dynamic-slice_bitcast_fusion.4), channel_id=1, source_target_pairs={{0,576},{48,624},{96,672},{144,720},{192,384},{240,432},{288,480},... | collective-permute-start | bytes 73736 | tf_op jit(solution)/shard_map/ppermute | solution.py:326
  55.7 6.9 %collective-permute-start.5 = (f32[48,128]{1,0:T(8,128)S(1)}, f32[48,128]{1,0:T(8,128)S(1)}, u32[]{:S(2)}, u32[]{:S(2)}) collective-permute-start(f32[48,128]{1,0:T(8,128)S(1)} %bitcast_add_fusion.4.keep_ref), channel_id=1, source_target_pairs={{0,3},{1,2},{2,1},{3,0},{4,7},{5,6},{6,5},{7,4},{8,11},{9,10},{10,... | collective-permute-start | bytes 73736 | tf_op jit(solution)/shard_map/ppermute | solution.py:326
  63.3 23.5 %all-to-all-start.1 = ((f32[12,48,128]{2,1,0:T(8,128)}), f32[12,48,128]{2,1,0:T(8,128)S(1)}, u32[]{:S(2)}, u32[]{:S(2)}) async-start(f32[12,48,128]{2,1,0:T(8,128)} %get-tuple-element.22), calls=%async_computation.1 | async-start | bytes 589824 | tf_op jit(solution)/shard_map/all_to_all | solution.py:447
  72.0 16.8 %collective-permute-start.8 = (f32[384,128]{1,0:T(8,128)S(1)}, f32[384,128]{1,0:T(8,128)S(1)}, u32[]{:S(2)}, u32[]{:S(2)}) collective-permute-start(f32[384,128]{1,0:T(8,128)S(1)} %get-tuple-element.21.own_in), channel_id=1, source_target_pairs={{0,3},{1,0},{2,1},{3,2},{4,7},{5,4},{6,5},{7,6},{8,11},{9,8},{10,9... | collective-permute-start | bytes 589832 | tf_op jit(solution)/shard_map/ppermute | solution.py:455
  74.0 14.8 %collective-permute-start.7 = (f32[384,128]{1,0:T(8,128)S(1)}, f32[384,128]{1,0:T(8,128)S(1)}, u32[]{:S(2)}, u32[]{:S(2)}) collective-permute-start(f32[384,128]{1,0:T(8,128)S(1)} %get-tuple-element.21.own_in), channel_id=1, source_target_pairs={{0,2},{1,3},{2,0},{3,1},{4,6},{5,7},{6,4},{7,5},{8,10},{9,11},{10,... | collective-permute-start | bytes 589832 | tf_op jit(solution)/shard_map/ppermute | solution.py:455
  78.1 10.8 %collective-permute-start.6 = (f32[384,128]{1,0:T(8,128)S(1)}, f32[384,128]{1,0:T(8,128)S(1)}, u32[]{:S(2)}, u32[]{:S(2)}) collective-permute-start(f32[384,128]{1,0:T(8,128)S(1)} %get-tuple-element.21.own_in), channel_id=1, source_target_pairs={{0,1},{1,2},{2,3},{3,0},{4,5},{5,6},{6,7},{7,4},{8,9},{9,10},{10,1... | collective-permute-start | bytes 589832 | tf_op jit(solution)/shard_map/ppermute | solution.py:455
  83.8 5.0 %copy-start = (s32[1,48]{1,0:T(1,128)S(1)}, s32[1,48]{1,0:T(1,128)}, u32[]{:S(2)}) copy-start(s32[1,48]{1,0:T(1,128)} %counts_ref.1) | copy-start | bytes 580
  86.9 5.7 %collective-permute-start.9 = (f32[48,128]{1,0:T(8,128)S(1)}, f32[48,128]{1,0:T(8,128)S(1)}, u32[]{:S(2)}, u32[]{:S(2)}) collective-permute-start(f32[48,128]{1,0:T(8,128)S(1)} %add_parts.1.mine_ref), channel_id=1, source_target_pairs={{0,1},{1,0},{2,3},{3,2},{4,5},{5,4},{6,7},{7,6},{8,9},{9,8},{10,11... | collective-permute-start | bytes 73736 | tf_op jit(solution)/shard_map/ppermute | solution.py:326

commit v7 on v6

--- a/solution.py
+++ b/solution.py
@@ -46,19 +46,19 @@
 
 
 def dense_kernel(
-    lengths_in, target_in, hist_in, pg_in, w1_in, b1_in, w2_in, b2_in, w3_in, ids_in, blocks_in,
+    target_ref, lengths_in, hist_in, pg_in, w1_in, b1_in, w2_in, b2_in, w3_in, ids_in, blocks_in,
     drow_ref, part_ref, ids_ref, blocks_ref,
-    lengths_ref, target_ref, hist_ref, pg_ref, w1_ref, b1_ref, w2_ref, b2_ref, w3_ref,
+    lengths_ref, hist_ref, pg_ref, w1_ref, b1_ref, w2_ref, b2_ref, w3_ref,
     feats, act1s, dz2s, dz1s, sems,
 ):
-    inputs = (hist_in, w1_in, target_in, b1_in, w2_in, b2_in, w3_in, pg_in, lengths_in, ids_in, blocks_in)
-    held = (hist_ref, w1_ref, target_ref, b1_ref, w2_ref, b2_ref, w3_ref, pg_ref, lengths_ref, ids_ref, blocks_ref)
+    inputs = (hist_in, w1_in, b1_in, w2_in, b2_in, w3_in, pg_in, lengths_in, ids_in, blocks_in)
+    held = (hist_ref, w1_ref, b1_ref, w2_ref, b2_ref, w3_ref, pg_ref, lengths_ref, ids_ref, blocks_ref)
     copies = [pltpu.make_async_copy(a, b, sems.at[k]) for k, (a, b) in enumerate(zip(inputs, held))]
     for copy in copies:
         copy.start()
     for copy in copies:
         copy.wait()
-    query = target_ref[...].astype(jnp.float32)
+    query = target_ref[...]
     w1, w2, w3 = w1_ref[...], w2_ref[...], w3_ref[...]
     grad_w3 = jnp.zeros((1, E), jnp.float32)
     grad_b2 = jnp.zeros((1, E), jnp.float32)
@@ -131,23 +131,23 @@
             jax.ShapeDtypeStruct(ids.shape, ids.dtype),
             jax.ShapeDtypeStruct(blocks.shape, blocks.dtype),
         ],
-        in_specs=[pl.BlockSpec(memory_space=pltpu.HBM)] * 11,
+        in_specs=[whole] + [pl.BlockSpec(memory_space=pltpu.HBM)] * 10,
         out_specs=[whole] * 4,
         scratch_shapes=[pltpu.SMEM(lengths.shape, lengths.dtype)]
-        + [pltpu.VMEM(v.shape, v.dtype) for v in (target, hist, pg, w1, b1, w2, b2, w3)]
+        + [pltpu.VMEM(v.shape, v.dtype) for v in (hist, pg, w1, b1, w2, b2, w3)]
         + [
             pltpu.VMEM((SLOTS, 4 * E), jnp.bfloat16),
             pltpu.VMEM((SLOTS, 2 * E), jnp.bfloat16),
             pltpu.VMEM((SLOTS, E), jnp.bfloat16),
             pltpu.VMEM((SLOTS, 2 * E), jnp.bfloat16),
-            pltpu.SemaphoreType.DMA((11,)),
+            pltpu.SemaphoreType.DMA((10,)),
         ],
         compiler_params=pltpu.CompilerParams(vmem_limit_bytes=VMEM_LIMIT),
         cost_estimate=pl.CostEstimate(
             flops=1_100_000_000, bytes_accessed=2_200_000, transcendentals=400_000
         ),
         name="dense",
-    )(*in_hbm(lengths, target, hist, pg, w1, b1, w2, b2, w3, ids, blocks))
+    )(target, *in_hbm(lengths, hist, pg, w1, b1, w2, b2, w3, ids, blocks))
 
 
 def pack_kernel(
@@ -420,7 +420,7 @@
     me = lax.axis_index("shard").reshape(1)
     drow, part, ids, blocks = dense(
         lengths,
-        target,
+        target.astype(jnp.float32),
         history.reshape(SLOTS, E),
         pooled_gradient,
         attn_w1,

time: 94.8 us -> 97.3 us (1.026)
  the two profiles are of different devices: /device:TPU:6 before, /device:TPU:44 now
where the time goes in v7:
time: 97.3 us; the launch traced here: 96.6 us
  starting transfers between devices  59.2 us (61%)
  waiting for transfers between devices  19.7 us (20%)
  Pallas kernels  15.9 us (16%)
    ppermute x7, starting transfers between devices, swap(): return lax.ppermute(value, axis, [(i, i ^ bits) for i in range(size)])  21.3 us
    ppermute x7, waiting for transfers between devices, swap(): return lax.ppermute(value, axis, [(i, i ^ bits) for i in range(size)])  18.6 us
    all_to_all x1, starting transfers between devices, shards(): got = lax.all_to_all(send, 'shard', split_axis=0, concat_axis=0, tiled=True)  18.5 us
    ppermute x3, starting transfers between devices, shards(): late.append(lax.ppermute(slab, 'shard', pairs))  10.7 us
    all_to_all x1, starting transfers between devices, shards(): lax.all_to_all(copies, 'shard', split_axis=0, concat_axis=0, tiled=True,...  8.63 us
    pallas_call x1, Pallas kernels, add_late(): pl.pallas_call(add_late_kernel, out_shape=jax.ShapeDtypeStruct((ROWS_DEV,...  5.62 us
    pallas_call x1, Pallas kernels, dense(): pl.pallas_call(dense_kernel, out_shape=[jax.ShapeDtypeStruct((SLOTS, E),...  3.09 us
    pallas_call x1, Pallas kernels, pack(): pl.pallas_call(pack_kernel, out_shape=jax.ShapeDtypeStruct((OWNERS, BLOCK...  3 us
  transfers between devices with their start and end apart: 12, of which 7 were waited for; matrix products, arithmetic and copies ran while one was open for 0% of the time, Pallas kernels for 12%

profile of v7, /device:TPU:44, one launch (start us, length us, event | category | flops | bytes accessed | tf_op | source)
XLA Modules:
  0.0 96.6 jit_solution(8987094285953241609)
XLA Ops:
  0.6 0.0 copy-start.1
  0.6 0.7 copy-done.1
  1.3 3.1 %dense.1 = (f32[1024,128]{1,0:T(8,128)S(1)}, f32[1536,128]{1,0:T(8,128)S(1)}, s32[8,128]{1,0:T(8,128)S(1)}, s32[48,48]{1,0:T(8,128)S(1)}) custom-call(f32[8,128]{1,0:T(8,128)S(1)} %convert_element_type.3.target_ref, s32[8]{0:T(128)} %lengths_in.1, bf16[1024,128]{1,0:T(8,128)(2,1)} %bitcast.38, f32[8,128]{1,0:T(8,128)} %pg_in.1, bf16[512,256]{1,0:T(8,128)(2,1)} %w1_in.1, ...), custom_call_target="tpu_custom_call" | custom-call | flops 1100000000 | bytes 2200000 | tf_op jit(solution)/shard_map/dense/pallas_call | solution.py:126
  4.5 3.3 %collective-permute-start = (f32[2,2,2,2,48,128]{5,4,3,2,1,0:T(8,128)S(1)}, f32[2,2,2,2,48,128]{5,4,3,2,1,0:T(8,128)S(1)}, u32[]{:S(2)}, u32[]{:S(2)}) collective-permute-start(f32[2,2,2,2,48,128]{5,4,3,2,1,0:T(8,128)S(1)} %dynamic-slice_bitcast_fusion), channel_id=1, source_target_pairs={{0,96},{48,144},{96,0},{144,48},{192,288},{240,336},{288,192},{336... | collective-permute-start | bytes 1179656 | tf_op jit(solution)/shard_map/ppermute | solution.py:326
  7.7 3.0 %pack.1 = f32[48,32,128]{2,1,0:T(8,128)} custom-call(s32[1]{0:T(128)} %bitcast.me_ref, s32[1,48]{1,0:T(1,128)} %counts_ref.1, f32[1024,128]{1,0:T(8,128)S(1)} %get-tuple-element.17.drow_ref, s32[8,128]{1,0:T(8,128)S(1)} %get-tuple-element.18.ids_ref, s32[48,48]{1,0:T(8,128)S(1)} %get-tuple-element.19.blocks_ref), custom_call_target="tpu_custom_call" | custom-call | flops 1241513984 | bytes 2000000 | tf_op jit(solution)/shard_map/pack/pallas_call | solution.py:210
  10.7 18.5 %all-to-all-start = ((f32[48,32,128]{2,1,0:T(8,128)}), f32[48,32,128]{2,1,0:T(8,128)S(1)}, u32[]{:S(2)}, u32[]{:S(2)}) async-start(f32[48,32,128]{2,1,0:T(8,128)} %pack.1), calls=%async_computation | async-start | bytes 1572864 | tf_op jit(solution)/shard_map/all_to_all | solution.py:435
  29.2 0.0 collective-permute-done
  29.3 1.9 %collective-permute-start.1 = (f32[2,2,2,48,128]{4,3,2,1,0:T(8,128)S(1)}, f32[2,2,2,48,128]{4,3,2,1,0:T(8,128)S(1)}, u32[]{:S(2)}, u32[]{:S(2)}) collective-permute-start(f32[2,2,2,48,128]{4,3,2,1,0:T(8,128)S(1)} %dynamic-slice_bitcast_fusion.1), channel_id=1, source_target_pairs={{0,48},{48,0},{96,144},{144,96},{192,240},{240,192},{288,336},{336... | collective-permute-start | bytes 589832 | tf_op jit(solution)/shard_map/ppermute | solution.py:326
  31.3 1.4 %collective-permute-done.1 = f32[2,2,2,48,128]{4,3,2,1,0:T(8,128)S(1)} collective-permute-done((f32[2,2,2,48,128]{4,3,2,1,0:T(8,128)S(1)}, f32[2,2,2,48,128]{4,3,2,1,0:T(8,128)S(1)}, u32[]{:S(2)}, u32[]{:S(2)}) %collective-permute-start.1) | collective-permute-done | bytes 196640 | tf_op jit(solution)/shard_map/ppermute | solution.py:326
  32.7 3.1 %collective-permute-start.2 = (f32[2,2,48,128]{3,2,1,0:T(8,128)S(1)}, f32[2,2,48,128]{3,2,1,0:T(8,128)S(1)}, u32[]{:S(2)}, u32[]{:S(2)}) collective-permute-start(f32[2,2,48,128]{3,2,1,0:T(8,128)S(1)} %dynamic-slice_bitcast_fusion.2), channel_id=1, source_target_pairs={{0,1},{1,0},{2,3},{3,2},{4,5},{5,4},{6,7},{7,6},{8,9},{9,8},{10,11... | collective-permute-start | bytes 294920 | tf_op jit(solution)/shard_map/ppermute | solution.py:326
  35.8 4.3 %collective-permute-done.2 = f32[2,2,48,128]{3,2,1,0:T(8,128)S(1)} collective-permute-done((f32[2,2,48,128]{3,2,1,0:T(8,128)S(1)}, f32[2,2,48,128]{3,2,1,0:T(8,128)S(1)}, u32[]{:S(2)}, u32[]{:S(2)}) %collective-permute-start.2) | collective-permute-done | bytes 98336 | tf_op jit(solution)/shard_map/ppermute | solution.py:326
  40.1 2.7 %collective-permute-start.3 = (f32[2,48,128]{2,1,0:T(8,128)S(1)}, f32[2,48,128]{2,1,0:T(8,128)S(1)}, u32[]{:S(2)}, u32[]{:S(2)}) collective-permute-start(f32[2,48,128]{2,1,0:T(8,128)S(1)} %dynamic-slice_bitcast_fusion.3), channel_id=1, source_target_pairs={{0,192},{48,240},{96,288},{144,336},{192,0},{240,48},{288,96},{336... | collective-permute-start | bytes 147464 | tf_op jit(solution)/shard_map/ppermute | solution.py:326
  42.9 4.2 %collective-permute-done.3 = f32[2,48,128]{2,1,0:T(8,128)S(1)} collective-permute-done((f32[2,48,128]{2,1,0:T(8,128)S(1)}, f32[2,48,128]{2,1,0:T(8,128)S(1)}, u32[]{:S(2)}, u32[]{:S(2)}) %collective-permute-start.3) | collective-permute-done | bytes 49184 | tf_op jit(solution)/shard_map/ppermute | solution.py:326
  47.1 2.2 %collective-permute-start.4 = (f32[48,128]{1,0:T(8,128)S(1)}, f32[48,128]{1,0:T(8,128)S(1)}, u32[]{:S(2)}, u32[]{:S(2)}) collective-permute-start(f32[48,128]{1,0:T(8,128)S(1)} %dynamic-slice_bitcast_fusion.4), channel_id=1, source_target_pairs={{0,576},{48,624},{96,672},{144,720},{192,384},{240,432},{288,480},... | collective-permute-start | bytes 73736 | tf_op jit(solution)/shard_map/ppermute | solution.py:326
  49.3 5.8 %collective-permute-done.4 = f32[48,128]{1,0:T(8,128)S(1)} collective-permute-done((f32[48,128]{1,0:T(8,128)S(1)}, f32[48,128]{1,0:T(8,128)S(1)}, u32[]{:S(2)}, u32[]{:S(2)}) %collective-permute-start.4) | collective-permute-done | bytes 24608 | tf_op jit(solution)/shard_map/ppermute | solution.py:326
  55.2 2.8 %collective-permute-start.5 = (f32[48,128]{1,0:T(8,128)S(1)}, f32[48,128]{1,0:T(8,128)S(1)}, u32[]{:S(2)}, u32[]{:S(2)}) collective-permute-start(f32[48,128]{1,0:T(8,128)S(1)} %bitcast_add_fusion.4.keep_ref), channel_id=1, source_target_pairs={{0,3},{1,2},{2,1},{3,0},{4,7},{5,6},{6,5},{7,4},{8,11},{9,10},{10,... | collective-permute-start | bytes 73736 | tf_op jit(solution)/shard_map/ppermute | solution.py:326
  58.0 2.9 %collective-permute-done.5.there_ref = f32[48,128]{1,0:T(8,128)S(1)} collective-permute-done((f32[48,128]{1,0:T(8,128)S(1)}, f32[48,128]{1,0:T(8,128)S(1)}, u32[]{:S(2)}, u32[]{:S(2)}) %collective-permute-start.5) | collective-permute-done | bytes 24608 | tf_op jit(solution)/shard_map/ppermute | solution.py:326
  60.9 0.4 all-to-all-done
  61.3 0.7 join.1
  62.0 8.6 %all-to-all-start.1 = ((f32[12,48,128]{2,1,0:T(8,128)}), f32[12,48,128]{2,1,0:T(8,128)S(1)}, u32[]{:S(2)}, u32[]{:S(2)}) async-start(f32[12,48,128]{2,1,0:T(8,128)} %get-tuple-element.22), calls=%async_computation.1 | async-start | bytes 589824 | tf_op jit(solution)/shard_map/all_to_all | solution.py:447
  70.7 2.9 %collective-permute-start.8 = (f32[384,128]{1,0:T(8,128)S(1)}, f32[384,128]{1,0:T(8,128)S(1)}, u32[]{:S(2)}, u32[]{:S(2)}) collective-permute-start(f32[384,128]{1,0:T(8,128)S(1)} %get-tuple-element.21.own_in), channel_id=1, source_target_pairs={{0,3},{1,0},{2,1},{3,2},{4,7},{5,4},{6,5},{7,6},{8,11},{9,8},{10,9... | collective-permute-start | bytes 589832 | tf_op jit(solution)/shard_map/ppermute | solution.py:455
  73.6 5.9 %collective-permute-start.7 = (f32[384,128]{1,0:T(8,128)S(1)}, f32[384,128]{1,0:T(8,128)S(1)}, u32[]{:S(2)}, u32[]{:S(2)}) collective-permute-start(f32[384,128]{1,0:T(8,128)S(1)} %get-tuple-element.21.own_in), channel_id=1, source_target_pairs={{0,2},{1,3},{2,0},{3,1},{4,6},{5,7},{6,4},{7,5},{8,10},{9,11},{10,... | collective-permute-start | bytes 589832 | tf_op jit(solution)/shard_map/ppermute | solution.py:455
  79.4 2.0 %collective-permute-start.6 = (f32[384,128]{1,0:T(8,128)S(1)}, f32[384,128]{1,0:T(8,128)S(1)}, u32[]{:S(2)}, u32[]{:S(2)}) collective-permute-start(f32[384,128]{1,0:T(8,128)S(1)} %get-tuple-element.21.own_in), channel_id=1, source_target_pairs={{0,1},{1,2},{2,3},{3,0},{4,5},{5,6},{6,7},{7,4},{8,9},{9,10},{10,1... | collective-permute-start | bytes 589832 | tf_op jit(solution)/shard_map/ppermute | solution.py:455
  81.4 2.8 %add_main.1.table_in = f32[2048,128]{1,0:T(8,128)} custom-call(f32[1536,128]{1,0:T(8,128)S(1)} %bitcast.35), custom_call_target="tpu_custom_call" | custom-call | flops 1610612736 | bytes 2500000 | tf_op jit(solution)/shard_map/add_main/pallas_call | solution.py:260
  84.2 0.7 all-to-all-done.1.parts_ref
  84.9 5.3 %collective-permute-start.9 = (f32[48,128]{1,0:T(8,128)S(1)}, f32[48,128]{1,0:T(8,128)S(1)}, u32[]{:S(2)}, u32[]{:S(2)}) collective-permute-start(f32[48,128]{1,0:T(8,128)S(1)} %add_parts.1.mine_ref), channel_id=1, source_target_pairs={{0,1},{1,0},{2,3},{3,2},{4,5},{5,4},{6,7},{7,6},{8,9},{9,8},{10,11... | collective-permute-start | bytes 73736 | tf_op jit(solution)/shard_map/ppermute | solution.py:326
  90.3 0.0 collective-permute-done.8.late2_in
  90.3 0.0 collective-permute-done.7.late1_in
  90.3 0.0 collective-permute-done.6.late0_in
  90.3 5.6 %add_late.1 = f32[2048,128]{1,0:T(8,128)} custom-call(s32[1]{0:T(128)} %bitcast.me_ref, s32[1,48]{1,0:T(1,128)S(1)} %copy-done, f32[2048,128]{1,0:T(8,128)} %add_main.1.table_in, f32[384,128]{1,0:T(8,128)S(1)} %get-tuple-element.21.own_in, f32[384,128]{1,0:T(8,128)S(1)} %collective-permute-done.6.late0_in, ...), custom_call_target="tpu_custom_call", output_to_operand_aliasing={{}: (2, {})} | custom-call | flops 1610612736 | bytes 2500000 | tf_op jit(solution)/shard_map/add_late/pallas_call | solution.py:301
  95.9 0.0 collective-permute-done.9.other_ref
  95.9 0.7 final.1
  (14 shorter events, 0.2 us)
Async XLA Ops:
  0.6 0.7 copy-start.1
  4.5 24.8 %collective-permute-start = (f32[2,2,2,2,48,128]{5,4,3,2,1,0:T(8,128)S(1)}, f32[2,2,2,2,48,128]{5,4,3,2,1,0:T(8,128)S(1)}, u32[]{:S(2)}, u32[]{:S(2)}) collective-permute-start(f32[2,2,2,2,48,128]{5,4,3,2,1,0:T(8,128)S(1)} %dynamic-slice_bitcast_fusion), channel_id=1, source_target_pairs={{0,96},{48,144},{96,0},{144,48},{192,288},{240,336},{288,192},{336... | collective-permute-start | bytes 1179656 | tf_op jit(solution)/shard_map/ppermute | solution.py:326
  10.7 50.6 %all-to-all-start = ((f32[48,32,128]{2,1,0:T(8,128)}), f32[48,32,128]{2,1,0:T(8,128)S(1)}, u32[]{:S(2)}, u32[]{:S(2)}) async-start(f32[48,32,128]{2,1,0:T(8,128)} %pack.1), calls=%async_computation | async-start | bytes 1572864 | tf_op jit(solution)/shard_map/all_to_all | solution.py:435
  29.3 3.3 %collective-permute-start.1 = (f32[2,2,2,48,128]{4,3,2,1,0:T(8,128)S(1)}, f32[2,2,2,48,128]{4,3,2,1,0:T(8,128)S(1)}, u32[]{:S(2)}, u32[]{:S(2)}) collective-permute-start(f32[2,2,2,48,128]{4,3,2,1,0:T(8,128)S(1)} %dynamic-slice_bitcast_fusion.1), channel_id=1, source_target_pairs={{0,48},{48,0},{96,144},{144,96},{192,240},{240,192},{288,336},{336... | collective-permute-start | bytes 589832 | tf_op jit(solution)/shard_map/ppermute | solution.py:326
  32.7 7.4 %collective-permute-start.2 = (f32[2,2,48,128]{3,2,1,0:T(8,128)S(1)}, f32[2,2,48,128]{3,2,1,0:T(8,128)S(1)}, u32[]{:S(2)}, u32[]{:S(2)}) collective-permute-start(f32[2,2,48,128]{3,2,1,0:T(8,128)S(1)} %dynamic-slice_bitcast_fusion.2), channel_id=1, source_target_pairs={{0,1},{1,0},{2,3},{3,2},{4,5},{5,4},{6,7},{7,6},{8,9},{9,8},{10,11... | collective-permute-start | bytes 294920 | tf_op jit(solution)/shard_map/ppermute | solution.py:326
  40.1 6.9 %collective-permute-start.3 = (f32[2,48,128]{2,1,0:T(8,128)S(1)}, f32[2,48,128]{2,1,0:T(8,128)S(1)}, u32[]{:S(2)}, u32[]{:S(2)}) collective-permute-start(f32[2,48,128]{2,1,0:T(8,128)S(1)} %dynamic-slice_bitcast_fusion.3), channel_id=1, source_target_pairs={{0,192},{48,240},{96,288},{144,336},{192,0},{240,48},{288,96},{336... | collective-permute-start | bytes 147464 | tf_op jit(solution)/shard_map/ppermute | solution.py:326
  47.1 8.1 %collective-permute-start.4 = (f32[48,128]{1,0:T(8,128)S(1)}, f32[48,128]{1,0:T(8,128)S(1)}, u32[]{:S(2)}, u32[]{:S(2)}) collective-permute-start(f32[48,128]{1,0:T(8,128)S(1)} %dynamic-slice_bitcast_fusion.4), channel_id=1, source_target_pairs={{0,576},{48,624},{96,672},{144,720},{192,384},{240,432},{288,480},... | collective-permute-start | bytes 73736 | tf_op jit(solution)/shard_map/ppermute | solution.py:326
  55.2 5.7 %collective-permute-start.5 = (f32[48,128]{1,0:T(8,128)S(1)}, f32[48,128]{1,0:T(8,128)S(1)}, u32[]{:S(2)}, u32[]{:S(2)}) collective-permute-start(f32[48,128]{1,0:T(8,128)S(1)} %bitcast_add_fusion.4.keep_ref), channel_id=1, source_target_pairs={{0,3},{1,2},{2,1},{3,0},{4,7},{5,6},{6,5},{7,4},{8,11},{9,10},{10,... | collective-permute-start | bytes 73736 | tf_op jit(solution)/shard_map/ppermute | solution.py:326
  62.0 22.9 %all-to-all-start.1 = ((f32[12,48,128]{2,1,0:T(8,128)}), f32[12,48,128]{2,1,0:T(8,128)S(1)}, u32[]{:S(2)}, u32[]{:S(2)}) async-start(f32[12,48,128]{2,1,0:T(8,128)} %get-tuple-element.22), calls=%async_computation.1 | async-start | bytes 589824 | tf_op jit(solution)/shard_map/all_to_all | solution.py:447
  70.7 19.6 %collective-permute-start.8 = (f32[384,128]{1,0:T(8,128)S(1)}, f32[384,128]{1,0:T(8,128)S(1)}, u32[]{:S(2)}, u32[]{:S(2)}) collective-permute-start(f32[384,128]{1,0:T(8,128)S(1)} %get-tuple-element.21.own_in), channel_id=1, source_target_pairs={{0,3},{1,0},{2,1},{3,2},{4,7},{5,4},{6,5},{7,6},{8,11},{9,8},{10,9... | collective-permute-start | bytes 589832 | tf_op jit(solution)/shard_map/ppermute | solution.py:455
  73.6 16.7 %collective-permute-start.7 = (f32[384,128]{1,0:T(8,128)S(1)}, f32[384,128]{1,0:T(8,128)S(1)}, u32[]{:S(2)}, u32[]{:S(2)}) collective-permute-start(f32[384,128]{1,0:T(8,128)S(1)} %get-tuple-element.21.own_in), channel_id=1, source_target_pairs={{0,2},{1,3},{2,0},{3,1},{4,6},{5,7},{6,4},{7,5},{8,10},{9,11},{10,... | collective-permute-start | bytes 589832 | tf_op jit(solution)/shard_map/ppermute | solution.py:455
  79.4 10.9 %collective-permute-start.6 = (f32[384,128]{1,0:T(8,128)S(1)}, f32[384,128]{1,0:T(8,128)S(1)}, u32[]{:S(2)}, u32[]{:S(2)}) collective-permute-start(f32[384,128]{1,0:T(8,128)S(1)} %get-tuple-element.21.own_in), channel_id=1, source_target_pairs={{0,1},{1,2},{2,3},{3,0},{4,5},{5,6},{6,7},{7,4},{8,9},{9,10},{10,1... | collective-permute-start | bytes 589832 | tf_op jit(solution)/shard_map/ppermute | solution.py:455
  84.2 6.1 %copy-start = (s32[1,48]{1,0:T(1,128)S(1)}, s32[1,48]{1,0:T(1,128)}, u32[]{:S(2)}) copy-start(s32[1,48]{1,0:T(1,128)} %counts_ref.1) | copy-start | bytes 580
  84.9 11.0 %collective-permute-start.9 = (f32[48,128]{1,0:T(8,128)S(1)}, f32[48,128]{1,0:T(8,128)S(1)}, u32[]{:S(2)}, u32[]{:S(2)}) collective-permute-start(f32[48,128]{1,0:T(8,128)S(1)} %add_parts.1.mine_ref), channel_id=1, source_target_pairs={{0,1},{1,0},{2,3},{3,2},{4,5},{5,4},{6,7},{7,6},{8,9},{9,8},{10,11... | collective-permute-start | bytes 73736 | tf_op jit(solution)/shard_map/ppermute | solution.py:326

commit v8 on v7

--- a/solution.py
+++ b/solution.py
@@ -42,7 +42,7 @@
 
 def place(g, side):
     core, y0, y1, y2 = g & 1, (g >> 1) & 1, (g >> 2) & 1, (g >> 3) & 1
-    return y0 * 16 + core * 8 + side * 4 + (y1 ^ y2) * 2 + y2
+    return side * 16 + core * 8 + y0 * 4 + (y1 ^ y2) * 2 + y2
 
 
 def dense_kernel(
@@ -316,7 +316,7 @@
     )(me, counts, table, *late)
 
 
-STEPS = (("grp", 2), ("grp", 1), ("shard", 1), ("grp", 4), ("grp", 12))
+STEPS = (("shard", 1), ("grp", 1), ("grp", 2), ("grp", 4), ("grp", 12))
 NZ = OWNERS // NX
 Z_GROUPS = [[z * NX + x for z in range(NZ)] for x in range(NX)]
 
@@ -438,7 +438,7 @@
     part = part.reshape(2, 2, 2, 2, 2, SIDE, E)
     y2 = (g >> 3) & 1
     side = (me[0] ^ (me[0] >> 1)) & 1
-    bits = ((g >> 1) & 1, g & 1, side, ((g >> 2) & 1) ^ y2, y2)
+    bits = (side, g & 1, (g >> 1) & 1, ((g >> 2) & 1) ^ y2, y2)
     for bit, (axis, k) in zip(bits, STEPS):
         keep = lax.dynamic_index_in_dim(part, bit, 0, False)
         away = lax.dynamic_index_in_dim(part, 1 - bit, 0, False)

time: 97.3 us -> 93 us (0.956)
  the two profiles are of different devices: /device:TPU:44 before, /device:TPU:6 now
where the time goes in v8:
time: 93 us; the launch traced here: 92.3 us
  starting transfers between devices  59.9 us (64%)
  waiting for transfers between devices  19.7 us (21%)
  Pallas kernels  10.9 us (12%)
    ppermute x7, starting transfers between devices, swap(): return lax.ppermute(value, axis, [(i, i ^ bits) for i in range(size)])  23 us
    all_to_all x1, starting transfers between devices, shards(): got = lax.all_to_all(send, 'shard', split_axis=0, concat_axis=0, tiled=True)  18.8 us
    ppermute x7, waiting for transfers between devices, swap(): return lax.ppermute(value, axis, [(i, i ^ bits) for i in range(size)])  16.7 us
    all_to_all x1, starting transfers between devices, shards(): lax.all_to_all(copies, 'shard', split_axis=0, concat_axis=0, tiled=True,...  9.15 us
    ppermute x3, starting transfers between devices, shards(): late.append(lax.ppermute(slab, 'shard', pairs))  8.97 us
    pallas_call x1, Pallas kernels, dense(): pl.pallas_call(dense_kernel, out_shape=[jax.ShapeDtypeStruct((SLOTS, E),...  3.09 us
    all_to_all x1, waiting for transfers between devices, shards(): lax.all_to_all(copies, 'shard', split_axis=0, concat_axis=0, tiled=True,...  3.02 us
    pallas_call x1, Pallas kernels, pack(): pl.pallas_call(pack_kernel, out_shape=jax.ShapeDtypeStruct((OWNERS, BLOCK...  3 us
  transfers between devices with their start and end apart: 12, of which 7 were waited for; matrix products, arithmetic and copies ran while one was open for 0% of the time, Pallas kernels for 7%

profile of v8, /device:TPU:6, one launch (start us, length us, event | category | flops | bytes accessed | tf_op | source)
XLA Modules:
  0.0 92.3 jit_solution(3310846107502570951)
XLA Ops:
  0.6 0.0 copy-start.1
  0.7 0.7 copy-done.1
  1.3 3.1 %dense.1 = (f32[1024,128]{1,0:T(8,128)S(1)}, f32[1536,128]{1,0:T(8,128)S(1)}, s32[8,128]{1,0:T(8,128)S(1)}, s32[48,48]{1,0:T(8,128)S(1)}) custom-call(f32[8,128]{1,0:T(8,128)S(1)} %convert_element_type.3.target_ref, s32[8]{0:T(128)} %lengths_in.1, bf16[1024,128]{1,0:T(8,128)(2,1)} %bitcast.38, f32[8,128]{1,0:T(8,128)} %pg_in.1, bf16[512,256]{1,0:T(8,128)(2,1)} %w1_in.1, ...), custom_call_target="tpu_custom_call" | custom-call | flops 1100000000 | bytes 2200000 | tf_op jit(solution)/shard_map/dense/pallas_call | solution.py:126
  4.5 2.7 %collective-permute-start = (f32[2,2,2,2,48,128]{5,4,3,2,1,0:T(8,128)S(1)}, f32[2,2,2,2,48,128]{5,4,3,2,1,0:T(8,128)S(1)}, u32[]{:S(2)}, u32[]{:S(2)}) collective-permute-start(f32[2,2,2,2,48,128]{5,4,3,2,1,0:T(8,128)S(1)} %dynamic-slice_bitcast_fusion), channel_id=1, source_target_pairs={{0,1},{1,0},{2,3},{3,2},{4,5},{5,4},{6,7},{7,6},{8,9},{9,8},{10,11... | collective-permute-start | bytes 1179656 | tf_op jit(solution)/shard_map/ppermute | solution.py:326
  7.2 3.0 %pack.1 = f32[48,32,128]{2,1,0:T(8,128)} custom-call(s32[1]{0:T(128)} %bitcast.me_ref, s32[1,48]{1,0:T(1,128)} %counts_ref.1, f32[1024,128]{1,0:T(8,128)S(1)} %get-tuple-element.17.drow_ref, s32[8,128]{1,0:T(8,128)S(1)} %get-tuple-element.18.ids_ref, s32[48,48]{1,0:T(8,128)S(1)} %get-tuple-element.19.blocks_ref), custom_call_target="tpu_custom_call" | custom-call | flops 1241513984 | bytes 2000000 | tf_op jit(solution)/shard_map/pack/pallas_call | solution.py:210
  10.2 18.8 %all-to-all-start = ((f32[48,32,128]{2,1,0:T(8,128)}), f32[48,32,128]{2,1,0:T(8,128)S(1)}, u32[]{:S(2)}, u32[]{:S(2)}) async-start(f32[48,32,128]{2,1,0:T(8,128)} %pack.1), calls=%async_computation | async-start | bytes 1572864 | tf_op jit(solution)/shard_map/all_to_all | solution.py:435
  29.0 0.0 collective-permute-done
  29.1 1.9 %collective-permute-start.1 = (f32[2,2,2,48,128]{4,3,2,1,0:T(8,128)S(1)}, f32[2,2,2,48,128]{4,3,2,1,0:T(8,128)S(1)}, u32[]{:S(2)}, u32[]{:S(2)}) collective-permute-start(f32[2,2,2,48,128]{4,3,2,1,0:T(8,128)S(1)} %dynamic-slice_bitcast_fusion.1), channel_id=1, source_target_pairs={{0,48},{48,0},{96,144},{144,96},{192,240},{240,192},{288,336},{336... | collective-permute-start | bytes 589832 | tf_op jit(solution)/shard_map/ppermute | solution.py:326
  31.1 1.4 %collective-permute-done.1 = f32[2,2,2,48,128]{4,3,2,1,0:T(8,128)S(1)} collective-permute-done((f32[2,2,2,48,128]{4,3,2,1,0:T(8,128)S(1)}, f32[2,2,2,48,128]{4,3,2,1,0:T(8,128)S(1)}, u32[]{:S(2)}, u32[]{:S(2)}) %collective-permute-start.1) | collective-permute-done | bytes 196640 | tf_op jit(solution)/shard_map/ppermute | solution.py:326
  32.5 3.5 %collective-permute-start.2 = (f32[2,2,48,128]{3,2,1,0:T(8,128)S(1)}, f32[2,2,48,128]{3,2,1,0:T(8,128)S(1)}, u32[]{:S(2)}, u32[]{:S(2)}) collective-permute-start(f32[2,2,48,128]{3,2,1,0:T(8,128)S(1)} %dynamic-slice_bitcast_fusion.2), channel_id=1, source_target_pairs={{0,96},{48,144},{96,0},{144,48},{192,288},{240,336},{288,192},{336... | collective-permute-start | bytes 294920 | tf_op jit(solution)/shard_map/ppermute | solution.py:326
  36.0 3.2 %collective-permute-done.2 = f32[2,2,48,128]{3,2,1,0:T(8,128)S(1)} collective-permute-done((f32[2,2,48,128]{3,2,1,0:T(8,128)S(1)}, f32[2,2,48,128]{3,2,1,0:T(8,128)S(1)}, u32[]{:S(2)}, u32[]{:S(2)}) %collective-permute-start.2) | collective-permute-done | bytes 98336 | tf_op jit(solution)/shard_map/ppermute | solution.py:326
  39.3 4.5 %collective-permute-start.3 = (f32[2,48,128]{2,1,0:T(8,128)S(1)}, f32[2,48,128]{2,1,0:T(8,128)S(1)}, u32[]{:S(2)}, u32[]{:S(2)}) collective-permute-start(f32[2,48,128]{2,1,0:T(8,128)S(1)} %dynamic-slice_bitcast_fusion.3), channel_id=1, source_target_pairs={{0,192},{48,240},{96,288},{144,336},{192,0},{240,48},{288,96},{336... | collective-permute-start | bytes 147464 | tf_op jit(solution)/shard_map/ppermute | solution.py:326
  43.8 2.4 %collective-permute-done.3 = f32[2,48,128]{2,1,0:T(8,128)S(1)} collective-permute-done((f32[2,48,128]{2,1,0:T(8,128)S(1)}, f32[2,48,128]{2,1,0:T(8,128)S(1)}, u32[]{:S(2)}, u32[]{:S(2)}) %collective-permute-start.3) | collective-permute-done | bytes 49184 | tf_op jit(solution)/shard_map/ppermute | solution.py:326
  46.2 6.2 %collective-permute-start.4 = (f32[48,128]{1,0:T(8,128)S(1)}, f32[48,128]{1,0:T(8,128)S(1)}, u32[]{:S(2)}, u32[]{:S(2)}) collective-permute-start(f32[48,128]{1,0:T(8,128)S(1)} %dynamic-slice_bitcast_fusion.4), channel_id=1, source_target_pairs={{0,576},{48,624},{96,672},{144,720},{192,384},{240,432},{288,480},... | collective-permute-start | bytes 73736 | tf_op jit(solution)/shard_map/ppermute | solution.py:326
  52.4 1.9 %collective-permute-done.4 = f32[48,128]{1,0:T(8,128)S(1)} collective-permute-done((f32[48,128]{1,0:T(8,128)S(1)}, f32[48,128]{1,0:T(8,128)S(1)}, u32[]{:S(2)}, u32[]{:S(2)}) %collective-permute-start.4) | collective-permute-done | bytes 24608 | tf_op jit(solution)/shard_map/ppermute | solution.py:326
  54.3 2.2 %collective-permute-start.5 = (f32[48,128]{1,0:T(8,128)S(1)}, f32[48,128]{1,0:T(8,128)S(1)}, u32[]{:S(2)}, u32[]{:S(2)}) collective-permute-start(f32[48,128]{1,0:T(8,128)S(1)} %bitcast_add_fusion.4.keep_ref), channel_id=1, source_target_pairs={{0,3},{1,2},{2,1},{3,0},{4,7},{5,6},{6,5},{7,4},{8,11},{9,10},{10,... | collective-permute-start | bytes 73736 | tf_op jit(solution)/shard_map/ppermute | solution.py:326
  56.5 4.7 %collective-permute-done.5.there_ref = f32[48,128]{1,0:T(8,128)S(1)} collective-permute-done((f32[48,128]{1,0:T(8,128)S(1)}, f32[48,128]{1,0:T(8,128)S(1)}, u32[]{:S(2)}, u32[]{:S(2)}) %collective-permute-start.5) | collective-permute-done | bytes 24608 | tf_op jit(solution)/shard_map/ppermute | solution.py:326
  61.2 0.0 all-to-all-done
  61.2 0.7 join.1
  61.9 9.1 %all-to-all-start.1 = ((f32[12,48,128]{2,1,0:T(8,128)}), f32[12,48,128]{2,1,0:T(8,128)S(1)}, u32[]{:S(2)}, u32[]{:S(2)}) async-start(f32[12,48,128]{2,1,0:T(8,128)} %get-tuple-element.22), calls=%async_computation.1 | async-start | bytes 589824 | tf_op jit(solution)/shard_map/all_to_all | solution.py:447
  71.1 1.9 %collective-permute-start.8 = (f32[384,128]{1,0:T(8,128)S(1)}, f32[384,128]{1,0:T(8,128)S(1)}, u32[]{:S(2)}, u32[]{:S(2)}) collective-permute-start(f32[384,128]{1,0:T(8,128)S(1)} %get-tuple-element.21.own_in), channel_id=1, source_target_pairs={{0,3},{1,0},{2,1},{3,2},{4,7},{5,4},{6,5},{7,6},{8,11},{9,8},{10,9... | collective-permute-start | bytes 589832 | tf_op jit(solution)/shard_map/ppermute | solution.py:455
  73.0 3.9 %collective-permute-start.7 = (f32[384,128]{1,0:T(8,128)S(1)}, f32[384,128]{1,0:T(8,128)S(1)}, u32[]{:S(2)}, u32[]{:S(2)}) collective-permute-start(f32[384,128]{1,0:T(8,128)S(1)} %get-tuple-element.21.own_in), channel_id=1, source_target_pairs={{0,2},{1,3},{2,0},{3,1},{4,6},{5,7},{6,4},{7,5},{8,10},{9,11},{10,... | collective-permute-start | bytes 589832 | tf_op jit(solution)/shard_map/ppermute | solution.py:455
  76.9 3.2 %collective-permute-start.6 = (f32[384,128]{1,0:T(8,128)S(1)}, f32[384,128]{1,0:T(8,128)S(1)}, u32[]{:S(2)}, u32[]{:S(2)}) collective-permute-start(f32[384,128]{1,0:T(8,128)S(1)} %get-tuple-element.21.own_in), channel_id=1, source_target_pairs={{0,1},{1,2},{2,3},{3,0},{4,5},{5,6},{6,7},{7,4},{8,9},{9,10},{10,1... | collective-permute-start | bytes 589832 | tf_op jit(solution)/shard_map/ppermute | solution.py:455
  80.1 2.8 %add_main.1.table_in = f32[2048,128]{1,0:T(8,128)} custom-call(f32[1536,128]{1,0:T(8,128)S(1)} %bitcast.35), custom_call_target="tpu_custom_call" | custom-call | flops 1610612736 | bytes 2500000 | tf_op jit(solution)/shard_map/add_main/pallas_call | solution.py:260
  82.9 3.0 %all-to-all-done.1.parts_ref = f32[12,48,128]{2,1,0:T(8,128)S(1)} async-done(((f32[12,48,128]{2,1,0:T(8,128)}), f32[12,48,128]{2,1,0:T(8,128)S(1)}, u32[]{:S(2)}, u32[]{:S(2)}) %all-to-all-start.1) | async-done | bytes 294944 | tf_op jit(solution)/shard_map/all_to_all | solution.py:447
  85.9 1.9 %collective-permute-start.9 = (f32[48,128]{1,0:T(8,128)S(1)}, f32[48,128]{1,0:T(8,128)S(1)}, u32[]{:S(2)}, u32[]{:S(2)}) collective-permute-start(f32[48,128]{1,0:T(8,128)S(1)} %add_parts.1.mine_ref), channel_id=1, source_target_pairs={{0,1},{1,0},{2,3},{3,2},{4,5},{5,4},{6,7},{7,6},{8,9},{9,8},{10,11... | collective-permute-start | bytes 73736 | tf_op jit(solution)/shard_map/ppermute | solution.py:326
  87.9 0.0 collective-permute-done.8.late2_in
  87.9 0.0 collective-permute-done.7.late1_in
  87.9 0.0 collective-permute-done.6.late0_in
  87.9 0.6 add_late.1
  88.5 3.1 %collective-permute-done.9.other_ref = f32[48,128]{1,0:T(8,128)S(1)} collective-permute-done((f32[48,128]{1,0:T(8,128)S(1)}, f32[48,128]{1,0:T(8,128)S(1)}, u32[]{:S(2)}, u32[]{:S(2)}) %collective-permute-start.9) | collective-permute-done | bytes 24608 | tf_op jit(solution)/shard_map/ppermute | solution.py:326
  91.6 0.7 final.1
  (14 shorter events, 0.2 us)
Async XLA Ops:
  0.6 0.7 copy-start.1
  4.5 24.6 %collective-permute-start = (f32[2,2,2,2,48,128]{5,4,3,2,1,0:T(8,128)S(1)}, f32[2,2,2,2,48,128]{5,4,3,2,1,0:T(8,128)S(1)}, u32[]{:S(2)}, u32[]{:S(2)}) collective-permute-start(f32[2,2,2,2,48,128]{5,4,3,2,1,0:T(8,128)S(1)} %dynamic-slice_bitcast_fusion), channel_id=1, source_target_pairs={{0,1},{1,0},{2,3},{3,2},{4,5},{5,4},{6,7},{7,6},{8,9},{9,8},{10,11... | collective-permute-start | bytes 1179656 | tf_op jit(solution)/shard_map/ppermute | solution.py:326
  10.2 51.0 %all-to-all-start = ((f32[48,32,128]{2,1,0:T(8,128)}), f32[48,32,128]{2,1,0:T(8,128)S(1)}, u32[]{:S(2)}, u32[]{:S(2)}) async-start(f32[48,32,128]{2,1,0:T(8,128)} %pack.1), calls=%async_computation | async-start | bytes 1572864 | tf_op jit(solution)/shard_map/all_to_all | solution.py:435
  29.1 3.3 %collective-permute-start.1 = (f32[2,2,2,48,128]{4,3,2,1,0:T(8,128)S(1)}, f32[2,2,2,48,128]{4,3,2,1,0:T(8,128)S(1)}, u32[]{:S(2)}, u32[]{:S(2)}) collective-permute-start(f32[2,2,2,48,128]{4,3,2,1,0:T(8,128)S(1)} %dynamic-slice_bitcast_fusion.1), channel_id=1, source_target_pairs={{0,48},{48,0},{96,144},{144,96},{192,240},{240,192},{288,336},{336... | collective-permute-start | bytes 589832 | tf_op jit(solution)/shard_map/ppermute | solution.py:326
  32.5 6.7 %collective-permute-start.2 = (f32[2,2,48,128]{3,2,1,0:T(8,128)S(1)}, f32[2,2,48,128]{3,2,1,0:T(8,128)S(1)}, u32[]{:S(2)}, u32[]{:S(2)}) collective-permute-start(f32[2,2,48,128]{3,2,1,0:T(8,128)S(1)} %dynamic-slice_bitcast_fusion.2), channel_id=1, source_target_pairs={{0,96},{48,144},{96,0},{144,48},{192,288},{240,336},{288,192},{336... | collective-permute-start | bytes 294920 | tf_op jit(solution)/shard_map/ppermute | solution.py:326
  39.3 6.9 %collective-permute-start.3 = (f32[2,48,128]{2,1,0:T(8,128)S(1)}, f32[2,48,128]{2,1,0:T(8,128)S(1)}, u32[]{:S(2)}, u32[]{:S(2)}) collective-permute-start(f32[2,48,128]{2,1,0:T(8,128)S(1)} %dynamic-slice_bitcast_fusion.3), channel_id=1, source_target_pairs={{0,192},{48,240},{96,288},{144,336},{192,0},{240,48},{288,96},{336... | collective-permute-start | bytes 147464 | tf_op jit(solution)/shard_map/ppermute | solution.py:326
  46.2 8.1 %collective-permute-start.4 = (f32[48,128]{1,0:T(8,128)S(1)}, f32[48,128]{1,0:T(8,128)S(1)}, u32[]{:S(2)}, u32[]{:S(2)}) collective-permute-start(f32[48,128]{1,0:T(8,128)S(1)} %dynamic-slice_bitcast_fusion.4), channel_id=1, source_target_pairs={{0,576},{48,624},{96,672},{144,720},{192,384},{240,432},{288,480},... | collective-permute-start | bytes 73736 | tf_op jit(solution)/shard_map/ppermute | solution.py:326
  54.3 6.9 %collective-permute-start.5 = (f32[48,128]{1,0:T(8,128)S(1)}, f32[48,128]{1,0:T(8,128)S(1)}, u32[]{:S(2)}, u32[]{:S(2)}) collective-permute-start(f32[48,128]{1,0:T(8,128)S(1)} %bitcast_add_fusion.4.keep_ref), channel_id=1, source_target_pairs={{0,3},{1,2},{2,1},{3,0},{4,7},{5,6},{6,5},{7,4},{8,11},{9,10},{10,... | collective-permute-start | bytes 73736 | tf_op jit(solution)/shard_map/ppermute | solution.py:326
  61.9 24.0 %all-to-all-start.1 = ((f32[12,48,128]{2,1,0:T(8,128)}), f32[12,48,128]{2,1,0:T(8,128)S(1)}, u32[]{:S(2)}, u32[]{:S(2)}) async-start(f32[12,48,128]{2,1,0:T(8,128)} %get-tuple-element.22), calls=%async_computation.1 | async-start | bytes 589824 | tf_op jit(solution)/shard_map/all_to_all | solution.py:447
  71.1 16.8 %collective-permute-start.8 = (f32[384,128]{1,0:T(8,128)S(1)}, f32[384,128]{1,0:T(8,128)S(1)}, u32[]{:S(2)}, u32[]{:S(2)}) collective-permute-start(f32[384,128]{1,0:T(8,128)S(1)} %get-tuple-element.21.own_in), channel_id=1, source_target_pairs={{0,3},{1,0},{2,1},{3,2},{4,7},{5,4},{6,5},{7,6},{8,11},{9,8},{10,9... | collective-permute-start | bytes 589832 | tf_op jit(solution)/shard_map/ppermute | solution.py:455
  73.0 14.8 %collective-permute-start.7 = (f32[384,128]{1,0:T(8,128)S(1)}, f32[384,128]{1,0:T(8,128)S(1)}, u32[]{:S(2)}, u32[]{:S(2)}) collective-permute-start(f32[384,128]{1,0:T(8,128)S(1)} %get-tuple-element.21.own_in), channel_id=1, source_target_pairs={{0,2},{1,3},{2,0},{3,1},{4,6},{5,7},{6,4},{7,5},{8,10},{9,11},{10,... | collective-permute-start | bytes 589832 | tf_op jit(solution)/shard_map/ppermute | solution.py:455
  76.9 10.9 %collective-permute-start.6 = (f32[384,128]{1,0:T(8,128)S(1)}, f32[384,128]{1,0:T(8,128)S(1)}, u32[]{:S(2)}, u32[]{:S(2)}) collective-permute-start(f32[384,128]{1,0:T(8,128)S(1)} %get-tuple-element.21.own_in), channel_id=1, source_target_pairs={{0,1},{1,2},{2,3},{3,0},{4,5},{5,6},{6,7},{7,4},{8,9},{9,10},{10,1... | collective-permute-start | bytes 589832 | tf_op jit(solution)/shard_map/ppermute | solution.py:455
  82.9 5.0 %copy-start = (s32[1,48]{1,0:T(1,128)S(1)}, s32[1,48]{1,0:T(1,128)}, u32[]{:S(2)}) copy-start(s32[1,48]{1,0:T(1,128)} %counts_ref.1) | copy-start | bytes 580
  85.9 5.7 %collective-permute-start.9 = (f32[48,128]{1,0:T(8,128)S(1)}, f32[48,128]{1,0:T(8,128)S(1)}, u32[]{:S(2)}, u32[]{:S(2)}) collective-permute-start(f32[48,128]{1,0:T(8,128)S(1)} %add_parts.1.mine_ref), channel_id=1, source_target_pairs={{0,1},{1,0},{2,3},{3,2},{4,5},{5,4},{6,7},{7,6},{8,9},{9,8},{10,11... | collective-permute-start | bytes 73736 | tf_op jit(solution)/shard_map/ppermute | solution.py:326
